TPU v7x, 32 devices: a whole 2x2x4 slice. The times are simulated.
32 devices in a mesh: dp: 4 (over y, x), graph: 8 (over z, core).
Axes of the slice: x: 2, y: 2, z: 4, core: 2. Of those that a mesh axis runs over, the one named last changes fastest.
Arguments:
- node_feats: bfloat16 [4, 256, 49, 128], P('dp', 'graph'), may hold values from -6 to 6
- cotangent: bfloat16 [4, 256, 49, 128], P('dp', 'graph'), may hold values from -10 to 10
- sources: int32 [4, 2048], P('dp', 'graph'), may hold values from 0 to 255, as said below
- targets: int32 [4, 2048], P('dp', 'graph'), may hold values from 0 to 255, as said below
- bins: int32 [4, 2048], P('dp', 'graph'), may hold values from 0 to 63
- live_mask: int32 [4, 2048], P('dp', 'graph'), may hold values from 0 to 1, as said below
- radial: bfloat16 [4, 2048, 512], P('dp', 'graph'), may hold values from 0 to 1
- edge_bias: bfloat16 [4, 2048, 8], P('dp', 'graph'), may hold values from -4 to 256
- w_value: bfloat16 [128, 128], replicated, may hold values from -0.5 to 0.5
- w_query: bfloat16 [128, 128], replicated, may hold values from -0.5 to 0.5
- w_out: bfloat16 [128, 128], replicated, may hold values from -0.5 to 0.5
- w_radial: bfloat16 [512, 128], replicated, may hold values from -0.25 to 0.25
- w_mix: bfloat16 [5, 128, 128], replicated, may hold values from -0.5 to 0.5
- rotations: bfloat16 [64, 49, 49], replicated, may hold values from -1 to 3, as said below
Outputs:
- updated: bfloat16 [4, 256, 49, 128], P('dp', 'graph')
- grad_nodes: bfloat16 [4, 256, 49, 128], P('dp', 'graph')
- grad_value: float32 [128, 128], replicated
- grad_query: float32 [128, 128], replicated
- grad_out: float32 [128, 128], replicated
- grad_radial: float32 [512, 128], replicated
- grad_mix: float32 [5, 128, 128], replicated
Inputs may be any that keep to these rules, and one draw needn't show every extreme that they name: `sources`: every slot of graph index j's block of 256 slots names a source node owned by j, one of nodes j * 32 to j * 32 + 31. `targets`: in each device's block of 256 slots, slots j * 32 to j * 32 + 31 hold edges into nodes j * 32 to j * 32 + 31, owned by graph index j. `live_mask`: in each group of 32 slots the live slots come first; in every batch some owner receives 32 live edges from every device's block. `rotations`: entry (i, j) of a rotation is zero unless i and j lie in the same degree block l*l to l*l + 2l.
All inputs are finite; a program needn't handle non-finite values.
Results may differ from a plain program's by a relative error of at most 0.012.
Values may be sent and summed in bfloat16 or wider, within the bound.
No kernel may reach another device: no remote copies, remote signals or barrier semaphores. Data moves between devices by JAX's collectives and lax.ppermute only.
A program may use at most 128 MiB of HBM per device.

v0:
```python
import functools

import jax
import jax.numpy as jnp
import numpy as np
from jax import lax
from jax.experimental import pallas as pl
from jax.experimental.pallas import tpu as pltpu
from jax.sharding import PartitionSpec as P

H = 8
VH = 16
LMAX = 6
MMAX = 2
K = (LMAX + 1) ** 2
BF = jnp.bfloat16
F32 = jnp.float32
CHUNK = 16
LANES = 128


def frame_layout():
    index, degree_of = [], []
    for order in range(MMAX + 1):
        for sign in (1, -1) if order else (1,):
            for degree in range(order, LMAX + 1):
                index.append(degree * degree + degree + sign * order)
                degree_of.append(degree)
    return index, degree_of


ROWS, DEGREE = frame_layout()
R = len(ROWS)
OF_DEGREE = [[r for r in range(R) if DEGREE[r] == degree] for degree in range(LMAX + 1)]
PAIRS = []
_offset = LMAX + 1
for _order in range(1, MMAX + 1):
    _length = LMAX + 1 - _order
    for _i in range(_length):
        PAIRS.append((_order, _offset + _i, _offset + _length + _i))
    _offset += 2 * _length


def dot(a, b, ca=1, cb=0, exact=False):
    return lax.dot_general(
        a,
        b,
        (((ca,), (cb,)), ((), ())),
        precision=lax.Precision.HIGHEST if exact else None,
        preferred_element_type=F32,
    )


def flip(a):
    return jnp.transpose(a.astype(F32)).astype(a.dtype)


def hits(row, count, dtype):
    lines = lax.broadcasted_iota(jnp.int32, (count, row.shape[1]), 0)
    return jnp.where(lines == row.astype(jnp.int32), 1.0, 0.0).astype(dtype)


def head_sum(a):
    return jnp.sum(a.reshape(H, VH, a.shape[1]), axis=1)


def spread(a):
    return jnp.broadcast_to(a[:, None, :], (H, VH, a.shape[1])).reshape(H * VH, a.shape[1])


def turn(table, source, degrees, emit):
    channels, edges = source.shape[1], source.shape[2]

    def step(i, carry):
        rows = pl.ds(pl.multiple_of(i * CHUNK, CHUNK), CHUNK)
        for start in range(0, edges, LANES):
            lanes = pl.ds(start, LANES)
            for degree in degrees:
                block = range(degree * degree, (degree + 1) ** 2)
                parts = [source[k, rows, lanes].astype(F32) for k in block]
                for r in OF_DEGREE[degree]:
                    total = None
                    for k, part in zip(block, parts):
                        term = table[r, k : k + 1, start : start + LANES] * part
                        total = term if total is None else total + term
                    emit(r, rows, lanes, total)
        return carry

    lax.fori_loop(0, channels // CHUNK, step, 0)


def turn_back(table, source, degrees, out):
    channels, edges = source.shape[1], source.shape[2]

    def step(i, carry):
        rows = pl.ds(pl.multiple_of(i * CHUNK, CHUNK), CHUNK)
        for start in range(0, edges, LANES):
            lanes = pl.ds(start, LANES)
            for degree in degrees:
                parts = [source[r, rows, lanes].astype(F32) for r in OF_DEGREE[degree]]
                for k in range(degree * degree, (degree + 1) ** 2):
                    total = None
                    for r, part in zip(OF_DEGREE[degree], parts):
                        term = table[r, k : k + 1, start : start + LANES] * part
                        total = term if total is None else total + term
                    out[k, rows, lanes] = total.astype(out.dtype)
        return carry

    lax.fori_loop(0, channels // CHUNK, step, 0)


def each_k(body, first=0):
    def step(i, carry):
        for j in range(LMAX + 1):
            body(i * (LMAX + 1) + j)
        return carry

    lax.fori_loop(0, LMAX + 1, step, 0)


def mix_block(w_mix, order, back):
    even, odd = w_mix[2 * order - 1], w_mix[2 * order]
    if back:
        return jnp.concatenate(
            [
                jnp.concatenate([even, odd], axis=1),
                jnp.concatenate([-odd, even], axis=1),
            ],
            axis=0,
        )
    even, odd = flip(even), flip(odd)
    return jnp.concatenate(
        [
            jnp.concatenate([even, -odd], axis=1),
            jnp.concatenate([odd, even], axis=1),
        ],
        axis=0,
    )


def forward_kernel(chips, core, *refs):
    (pack_own, pack_sib, radial_own, radial_sib, feats_own, feats_sib) = refs[:6]
    firsts = refs[6 : 6 + chips]
    (w_value, w_query, w_radial, w_mix, rot) = refs[6 + chips : 11 + chips]
    (table, scaled, mixed, gating, pack, radial, weight, stats, query) = refs[11 + chips : 20 + chips]
    (incoming,) = refs[20 + chips :]
    slots = pack_own.shape[1]
    cap = slots // (2 * chips)
    half = slots // 2
    nodes = feats_own.shape[1]
    targets = chips * nodes
    bins = rot.shape[2]

    edge = lax.broadcasted_iota(jnp.int32, (2 * slots, slots), 1)
    place = lax.broadcasted_iota(jnp.int32, (2 * slots, slots), 0)
    within = edge % half
    origin = (edge // half) * slots + (2 * (within // cap) + core[0]) * cap + within % cap
    pick = jnp.where(place == origin, 1.0, 0.0).astype(BF)
    packs = jnp.concatenate([pack_own[...], pack_sib[...]], axis=1).astype(BF)
    rows = dot(packs, pick)
    pack[...] = rows
    radial[...] = dot(
        pick, jnp.concatenate([radial_own[...], radial_sib[...]], axis=0), 0, 0
    ).astype(BF)
    gating[...] = jax.nn.sigmoid(dot(flip(w_radial[...]), radial[...], 1, 1))

    bin_hit = hits(rows[2:3], bins, BF)
    for r, row in enumerate(ROWS):
        table[r, 0:K, :] = dot(rot[row], bin_hit)
    source_hit = hits(rows[0:1], 2 * nodes, BF)
    value_t = flip(w_value[...])

    def gather(k):
        here = jnp.concatenate([feats_own[k], feats_sib[k]], axis=0)
        values = dot(value_t, here, 1, 1).astype(BF)
        incoming[k] = dot(values, source_hit).astype(BF)

    each_k(gather)

    def emit(r, rows_, lanes, total):
        scaled[r, rows_, lanes] = (total * gating[rows_, lanes]).astype(BF)

    turn(table, incoming, range(LMAX + 1), emit)

    zero_t = flip(w_mix[0])
    for r in range(LMAX + 1):
        mixed[r] = dot(zero_t, scaled[r]).astype(BF)
    blocks = [None] + [mix_block(w_mix, order, False) for order in range(1, MMAX + 1)]
    for order, plus, minus in PAIRS:
        both = jnp.concatenate([scaled[plus], scaled[minus]], axis=0)
        out = dot(blocks[order], both).astype(BF)
        mixed[plus] = out[: H * VH]
        mixed[minus] = out[H * VH :]

    target_hit = hits(rows[1:2], targets, BF)
    first = jnp.concatenate([f[...] for f in firsts], axis=0)
    queries = dot(flip(w_query[...]), first, 1, 1).astype(BF)
    query[...] = dot(queries, target_hit)
    scores = head_sum(mixed[0].astype(F32) * query[...]) * (1.0 / VH**0.5) + rows[8:16]
    live = rows[3:4] > 0.5
    columns = jnp.transpose(rows)
    score_columns = jnp.transpose(scores)
    line = lax.broadcasted_iota(jnp.int32, (slots, targets), 1)
    chosen = (line == columns[:, 1:2].astype(jnp.int32)) & (columns[:, 3:4] > 0.5)
    top = jnp.concatenate(
        [
            jnp.max(jnp.where(chosen, score_columns[:, h : h + 1], 0.0), axis=0, keepdims=True)
            for h in range(H)
        ],
        axis=0,
    )
    top = jnp.maximum(top, 0.0)
    target_hit32 = target_hit.astype(F32)
    top_edge = dot(top, target_hit32, exact=True)
    weights = jnp.where(live, jnp.exp(jnp.where(live, scores - top_edge, 0.0)), 0.0)
    weight[...] = weights
    stats[0:H] = top
    stats[H : 2 * H] = dot(weights, target_hit32, 1, 1, exact=True)


def attend_kernel(chips, *refs):
    stats = refs[:chips]
    weight, pack, table, mixed = refs[chips : chips + 4]
    share = refs[chips + 4]
    parts = refs[chips + 5 : 2 * chips + 5]
    scaled_rows, back = refs[2 * chips + 5 :]
    targets = stats[0].shape[1]
    nodes = targets // chips
    target_hit = hits(pack[1:2], targets, BF)
    tops, sums = [], []
    for p in range(chips):
        pieces = [stats[p][:, (q ^ p) * nodes : ((q ^ p) + 1) * nodes] for q in range(chips)]
        whole = jnp.concatenate(pieces, axis=1)
        tops.append(whole[0:H])
        sums.append(whole[H : 2 * H])
    top = functools.reduce(jnp.maximum, tops)
    bottom = jnp.exp(-top)
    for own_top, own_sum in zip(tops, sums):
        bottom = bottom + own_sum * jnp.exp(own_top - top)
    factor = jnp.exp(tops[0] - top) / bottom
    shares = weight[...] * dot(factor, target_hit.astype(F32), exact=True)
    share[...] = shares
    wide = spread(shares)
    for r in range(R):
        scaled_rows[r] = (mixed[r].astype(F32) * wide).astype(BF)
    turn_back(table, scaled_rows, range(LMAX + 1), back)

    def collect(k):
        out = dot(target_hit, back[k], 1, 1).astype(BF)
        for p in range(chips):
            parts[p][k] = out[p * nodes : (p + 1) * nodes]

    each_k(collect)


def pull_kernel(chips, *refs):
    cots = refs[:chips]
    w_out, pack, table, mixed, share = refs[chips : chips + 5]
    pulled, pulled0, dalpha, dots = refs[chips + 5 : chips + 9]
    incoming, total_ref = refs[chips + 9 :]
    nodes = cots[0].shape[1]
    targets = chips * nodes
    target_hit = hits(pack[1:2], targets, BF)
    out_w = w_out[...]

    def gather(k):
        here = jnp.concatenate([c[k] for c in cots], axis=0)
        back = dot(out_w, here, 1, 1).astype(BF)
        incoming[k] = dot(back, target_hit).astype(BF)

    each_k(gather)
    total_ref[...] = jnp.zeros_like(total_ref)
    shares = share[...]
    wide_ref = pulled0
    wide_ref[...] = spread(shares)

    def emit(r, rows, lanes, total):
        total_ref[rows, lanes] += total * mixed[r, rows, lanes].astype(F32)
        pulled[r, rows, lanes] = (total * wide_ref[rows, lanes]).astype(BF)

    turn(table, incoming, range(LMAX + 1), emit)
    sums = head_sum(total_ref[...])
    dalpha[...] = sums
    dots[...] = dot(shares * sums, target_hit.astype(F32), 1, 1, exact=True)
    pulled0[...] = table[0, 0:1, :] * incoming[0].astype(F32) * wide_ref[...]


def back_kernel(chips, *refs):
    parts = refs[:chips]
    cots = refs[chips : 2 * chips]
    (feats_own, feats_sib, pulled, scaled, gating, table, pack, w_mix) = refs[2 * chips : 2 * chips + 8]
    (gate_sum, dv_own, dv_sib, g_mix, g_value, g_out) = refs[2 * chips + 8 : 2 * chips + 14]
    turned, spread_back = refs[2 * chips + 14 :]
    nodes = feats_own.shape[1]
    wide = H * VH
    gate = gating[...]
    zero = w_mix[0]
    gates = jnp.zeros_like(gate)
    grad = jnp.zeros((wide, wide), F32)
    for r in range(1, LMAX + 1):
        here = scaled[r]
        down = pulled[r]
        grad = grad + dot(here, down, 1, 1)
        out = dot(zero, down)
        gates = gates + out * here.astype(F32)
        turned[r] = (out * gate).astype(BF)
    g_mix[0] = grad
    for order in range(1, MMAX + 1):
        block = mix_block(w_mix, order, True)
        grad = jnp.zeros((2 * wide, 2 * wide), F32)
        for own, plus, minus in PAIRS:
            if own != order:
                continue
            down = jnp.concatenate([pulled[plus], pulled[minus]], axis=0)
            here = jnp.concatenate([scaled[plus], scaled[minus]], axis=0)
            grad = grad + dot(here, down, 1, 1)
            out = dot(block, down)
            prod = out * here.astype(F32)
            gates = gates + prod[:wide] + prod[wide:]
            turned[plus] = (out[:wide] * gate).astype(BF)
            turned[minus] = (out[wide:] * gate).astype(BF)
        g_mix[2 * order - 1] = grad[:wide, :wide] + grad[wide:, wide:]
        g_mix[2 * order] = grad[:wide, wide:] - grad[wide:, :wide]
    gate_sum[...] = gates
    turn_back(table, turned, range(1, LMAX + 1), spread_back)
    spread_back[0] = jnp.zeros_like(spread_back[0])
    source_hit = hits(pack[0:1], 2 * nodes, BF)

    def collect(k):
        out = dot(source_hit, spread_back[k], 1, 1).astype(BF)
        dv_own[k] = out[:nodes]
        dv_sib[k] = out[nodes:]

    each_k(collect)
    g_value[...] = jnp.zeros_like(g_value)
    g_out[...] = jnp.zeros_like(g_out)

    def weigh(i, carry):
        some = pl.ds(i * (LMAX + 1), LMAX + 1)

        def flat(ref):
            return ref[some].reshape((LMAX + 1) * nodes, wide)

        g_value[...] += dot(flat(feats_own), flat(dv_own), 0, 0) + dot(
            flat(feats_sib), flat(dv_sib), 0, 0
        )
        total = dot(flat(parts[0]), flat(cots[0]), 0, 0)
        for p in range(1, chips):
            total = total + dot(flat(parts[p]), flat(cots[p]), 0, 0)
        g_out[...] += total
        return carry

    lax.fori_loop(0, LMAX + 1, weigh, 0)


def tail_kernel(chips, *refs):
    dots = refs[:chips]
    firsts = refs[chips : 2 * chips]
    (
        feat0_sib,
        dalpha,
        share,
        pulled0,
        query,
        mixed0,
        scaled0,
        gating,
        table0,
        gate_sum,
        radial,
        pack,
        w_zero,
        g_mix,
        g_value,
        g_out,
    ) = refs[2 * chips : 2 * chips + 16]
    grads, dv_own, dv_sib, dquery = refs[2 * chips + 16 :]
    targets = dots[0].shape[1]
    nodes = targets // chips
    wide = H * VH
    target_hit = hits(pack[1:2], targets, F32)
    total = dots[0][...]
    for p in range(1, chips):
        pieces = [dots[p][:, (q ^ p) * nodes : ((q ^ p) + 1) * nodes] for q in range(chips)]
        total = total + jnp.concatenate(pieces, axis=1)
    dscore = share[...] * (dalpha[...] - dot(total, target_hit, exact=True))
    dlogit = spread(dscore) * (1.0 / VH**0.5)
    down = (pulled0[...] + dlogit * query[...]).astype(BF)
    here = scaled0[...]
    gate = gating[...]
    out = dot(w_zero[...], down)
    dgate = ((gate_sum[...] + out * here.astype(F32)) * (1.0 - gate)).astype(BF)
    back = (table0[0:1, :] * (out * gate).astype(BF).astype(F32)).astype(BF)
    source_hit = hits(pack[0:1], 2 * nodes, BF)
    dv = dot(source_hit, back, 1, 1).astype(BF)
    dv_own[...] = dv[:nodes]
    dv_sib[...] = dv[nodes:]
    dq = dot(target_hit, dlogit * mixed0[...].astype(F32), 1, 1, exact=True)
    dquery[...] = dq
    first = jnp.concatenate([f[...] for f in firsts], axis=0)
    node0 = jnp.concatenate([firsts[0][...], feat0_sib[...]], axis=0)
    grads[0:wide] = g_value[...] + dot(node0, dv, 0, 0)
    grads[wide : 2 * wide] = dot(first, dq.astype(BF), 0, 0)
    grads[2 * wide : 3 * wide] = g_out[...]
    grads[3 * wide : 4 * wide] = g_mix[0] + dot(here, down, 1, 1)
    for i in range(1, 2 * MMAX + 1):
        grads[(3 + i) * wide : (4 + i) * wide] = g_mix[i]
    at = (4 + 2 * MMAX) * wide
    grads[at:] = jnp.transpose(dot(dgate, radial[...]))


def nodes_kernel(chips, *refs):
    dqs = refs[:chips]
    dv_own, dv_sib, dv0_own, dv0_sib, cot, w_value, w_query, out = refs[chips:]
    value_w = w_value[...]

    def one(k):
        dv = (dv_own[k].astype(F32) + dv_sib[k].astype(F32)).astype(BF)
        out[k] = (cot[k].astype(F32) + dot(dv, value_w, 1, 1)).astype(BF)

    each_k(one)
    dv = (dv0_own[...].astype(F32) + dv0_sib[...].astype(F32)).astype(BF)
    dq = functools.reduce(jnp.add, [d[...] for d in dqs]).astype(BF)
    out[0] = (cot[0].astype(F32) + dot(dv, value_w, 1, 1) + dot(dq, w_query[...], 1, 1)).astype(BF)


def update_kernel(chips, *refs):
    parts = refs[:chips]
    feats, w_out, out = refs[chips:]
    out_w = w_out[...]

    def one(k):
        total = parts[0][k].astype(F32)
        for p in range(1, chips):
            total = total + parts[p][k].astype(F32)
        out[k] = (feats[k].astype(F32) + dot(total.astype(BF), out_w)).astype(BF)

    each_k(one)


def call(kernel, args, outs, scratch=(), smem=0, flops=0, limit=24):
    whole = pl.BlockSpec(memory_space=pltpu.VMEM)
    moved = sum(a.size * a.dtype.itemsize for a in args)
    moved += sum(int(np.prod(s)) * jnp.dtype(d).itemsize for s, d in outs)
    return pl.pallas_call(
        kernel,
        out_shape=[jax.ShapeDtypeStruct(s, d) for s, d in outs],
        in_specs=[pl.BlockSpec(memory_space=pltpu.SMEM)] * smem + [whole] * (len(args) - smem),
        out_specs=[whole] * len(outs),
        scratch_shapes=[pltpu.VMEM(s, d) for s, d in scratch],
        compiler_params=pltpu.CompilerParams(vmem_limit_bytes=limit << 20),
        cost_estimate=pl.CostEstimate(flops=flops, bytes_accessed=moved, transcendentals=0),
    )(*args)


def shards(
    node_feats,
    cotangent,
    sources,
    targets,
    bins,
    live_mask,
    radial,
    edge_bias,
    w_value,
    w_query,
    w_out,
    w_radial,
    w_mix,
    rotations,
):
    feats = jnp.transpose(node_feats[0], (1, 0, 2))
    cot = jnp.transpose(cotangent[0], (1, 0, 2))
    rot = jnp.transpose(rotations, (1, 2, 0))
    nodes = feats.shape[1]
    wide = feats.shape[2]
    slots = sources.shape[1]
    ranks = lax.axis_size("graph")
    planes = lax.axis_size("dp")
    chips = ranks // 2
    rank = lax.axis_index("graph")
    plane = lax.axis_index("dp")
    core, chip = rank % 2, rank // 2
    spot = chips * nodes

    def other_core(a):
        return lax.ppermute(a, "graph", [(i, i ^ 1) for i in range(ranks)])

    def along(a, step):
        return lax.ppermute(a, "graph", [(i, i ^ (2 * step)) for i in range(ranks)])

    def beside(a, step):
        return lax.ppermute(a, "dp", [(i, i ^ step) for i in range(planes)])

    def gathered(a):
        return [a] + [along(a, step) for step in range(1, chips)]

    ids = jnp.stack(
        [
            sources[0] - rank * nodes,
            ((targets[0] // (2 * nodes)) ^ chip) * nodes + targets[0] % nodes,
            bins[0],
            live_mask[0],
            *([jnp.zeros_like(bins[0])] * 4),
        ]
    )
    pack_own = jnp.concatenate([ids.astype(F32), jnp.transpose(edge_bias[0]).astype(F32)])
    bump = jnp.where(lax.broadcasted_iota(jnp.int32, pack_own.shape, 0) == 0, float(nodes), 0.0)
    pack_sib = other_core(pack_own + bump)
    radial_sib = other_core(radial[0])
    feats_sib = other_core(feats)
    firsts = gathered(feats[0])
    cots = gathered(cot)

    edge_f32 = ((wide, slots), F32)
    table, scaled, mixed, gating, pack, radial_here, weight, stats, query = call(
        functools.partial(lambda core_ref, *refs: forward_kernel(chips, core_ref, *refs)),
        [
            core.reshape(1),
            pack_own,
            pack_sib,
            radial[0],
            radial_sib,
            feats,
            feats_sib,
            *firsts,
            w_value,
            w_query,
            w_radial,
            w_mix,
            rot,
        ],
        [
            ((R, 56, slots), F32),
            ((R, wide, slots), BF),
            ((R, wide, slots), BF),
            edge_f32,
            ((16, slots), F32),
            ((slots, radial.shape[2]), BF),
            ((H, slots), F32),
            ((2 * H, spot), F32),
            edge_f32,
        ],
        [((K, wide, slots), BF)],
        smem=1,
        flops=4_000_000_000,
    )
    share, *parts = call(
        functools.partial(attend_kernel, chips),
        [*gathered(stats), weight, pack, table, mixed],
        [((H, slots), F32), *([((K, nodes, wide), BF)] * chips)],
        [((R, wide, slots), BF), ((K, wide, slots), BF)],
        flops=2_000_000_000,
    )
    arrived = [parts[0]] + [along(parts[step], step) for step in range(1, chips)]
    pulled, pulled0, dalpha, dots = call(
        functools.partial(pull_kernel, chips),
        [*cots, w_out, pack, table, mixed, share],
        [((R, wide, slots), BF), edge_f32, ((H, slots), F32), ((H, spot), F32)],
        [((K, wide, slots), BF), edge_f32],
        flops=2_000_000_000,
    )
    all_dots = gathered(dots)
    gate_sum, dv_own, dv_sib, g_mix, g_value, g_out = call(
        functools.partial(back_kernel, chips),
        [*parts, *cots, feats, feats_sib, pulled, scaled, gating, table, pack, w_mix],
        [
            edge_f32,
            ((K, nodes, wide), BF),
            ((K, nodes, wide), BF),
            (w_mix.shape, F32),
            ((wide, wide), F32),
            ((wide, wide), F32),
        ],
        [((R, wide, slots), BF), ((K, wide, slots), BF)],
        flops=4_000_000_000,
        limit=32,
    )
    dv_got = other_core(dv_sib)
    total_rows = (4 + 2 * MMAX) * wide + radial.shape[2]
    grads, dv0_own, dv0_sib, dquery = call(
        functools.partial(tail_kernel, chips),
        [
            *all_dots,
            *firsts,
            feats_sib[0],
            dalpha,
            share,
            pulled0,
            query,
            mixed[0],
            scaled[0],
            gating,
            table[0, 0:8],
            gate_sum,
            radial_here,
            pack,
            w_mix[0],
            g_mix,
            g_value,
            g_out,
        ],
        [
            ((total_rows, wide), F32),
            ((nodes, wide), BF),
            ((nodes, wide), BF),
            ((spot, wide), F32),
        ],
        flops=300_000_000,
    )

    halves = grads.reshape(2, total_rows // 2, wide)
    half = lax.dynamic_index_in_dim(halves, core, 0, False)
    half = half + other_core(
        lax.dynamic_index_in_dim(halves, 1 - core, 0, False).astype(BF)
    ).astype(F32)
    cut = half.reshape(planes, -1, wide)
    cut_b = cut.astype(BF)
    piece = lax.dynamic_index_in_dim(cut, plane, 0, False)
    for step in range(1, planes):
        piece = piece + beside(
            lax.dynamic_index_in_dim(cut_b, plane ^ step, 0, False), step
        ).astype(F32)
    sent = piece.astype(BF)
    for step in range(1, chips):
        piece = piece + along(sent, step).astype(F32)
    piece = piece.astype(BF)
    whole = jnp.zeros(cut.shape, BF)
    whole = lax.dynamic_update_index_in_dim(whole, piece, plane, 0)
    for step in range(1, planes):
        whole = lax.dynamic_update_index_in_dim(whole, beside(piece, step), plane ^ step, 0)
    mine = whole.reshape(-1, wide)
    theirs = other_core(mine)
    summed = jnp.where(
        core == 0, jnp.concatenate([mine, theirs]), jnp.concatenate([theirs, mine])
    ).astype(F32)

    dv0_got = other_core(dv0_sib)
    dq_blocks = dquery.reshape(chips, nodes, wide)
    dqs = [dq_blocks[0]] + [along(dq_blocks[step], step) for step in range(1, chips)]
    (grad_nodes,) = call(
        functools.partial(nodes_kernel, chips),
        [*dqs, dv_own, dv_got, dv0_own, dv0_got, cot, w_value, w_query],
        [((K, nodes, wide), BF)],
        flops=100_000_000,
    )
    (updated,) = call(
        functools.partial(update_kernel, chips),
        [*arrived, feats, w_out],
        [((K, nodes, wide), BF)],
        flops=100_000_000,
    )
    return (
        jnp.transpose(updated, (1, 0, 2))[None],
        jnp.transpose(grad_nodes, (1, 0, 2))[None],
        summed[0:wide],
        summed[wide : 2 * wide],
        summed[2 * wide : 3 * wide],
        summed[(4 + 2 * MMAX) * wide :],
        summed[3 * wide : (4 + 2 * MMAX) * wide].reshape(w_mix.shape),
    )


def solution(mesh):
    edge = P("dp", "graph")
    return jax.shard_map(
        shards,
        mesh=mesh,
        in_specs=(edge, edge, edge, edge, edge, edge, edge, edge, P(), P(), P(), P(), P(), P()),
        out_specs=(edge, edge, P(), P(), P(), P(), P()),
        check_vma=False,
    )
```

profile of v0, /device:TPU:0, one launch (start us, length us, event | category | flops | bytes accessed | tf_op | source)
XLA Modules:
  0.0 151.5 jit_solution(13228585346400638361)
XLA Ops:
  1.3 5.0 %collective-permute-start.5 = (bf16[32,128]{1,0:T(8,128)(2,1)S(1)}, bf16[32,128]{1,0:T(8,128)(2,1)S(1)}, u32[]{:S(2)}, u32[]{:S(2)}) collective-permute-start(bf16[32,128]{1,0:T(8,128)(2,1)S(1)} %slice_bitcast_fusion.4.refs_6_.refs_4_), channel_id=1, source_target_pairs={{0,6},{1,7},{2,4},{3,5},{4,2},{5,3},{6,0},{7,1},{8,14},{9,15},{10,... | collective-permute-start | bytes 24584 | tf_op jit(solution)/shard_map/ppermute | solution.py:490
  10.9 3.3 %collective-permute-start.14 = (bf16[49,32,128]{2,1,0:T(8,128)(2,1)}, bf16[49,32,128]{2,1,0:T(8,128)(2,1)S(1)}, u32[]{:S(2)}, u32[]{:S(2)}) collective-permute-start(bf16[49,32,128]{2,1,0:T(8,128)(2,1)} %bitcast.72), channel_id=1, source_target_pairs={{0,6},{1,7},{2,4},{3,5},{4,2},{5,3},{6,0},{7,1},{8,14},{9,15},{10,... | collective-permute-start | bytes 1204232 | tf_op jit(solution)/shard_map/ppermute | solution.py:490
  21.7 9.8 %shard_map.189 = (f32[29,56,256]{2,1,0:T(8,128)S(1)}, bf16[29,128,256]{2,1,0:T(8,128)(2,1)S(1)}, bf16[29,128,256]{2,1,0:T(8,128)(2,1)S(1)}, f32[128,256]{1,0:T(8...) custom-call(s32[1]{0:T(128)} %bitcast.core_ref, ...), custom_call_target="tpu_custom_call" | custom-call | flops 4000000000 | bytes 8081540 | tf_op jit(solution)/shard_map/pallas_call | solution.py:445
  31.6 3.3 %collective-permute-start.8 = (f32[16,128]{1,0:T(8,128)S(1)}, f32[16,128]{1,0:T(8,128)S(1)}, u32[]{:S(2)}, u32[]{:S(2)}) collective-permute-start(f32[16,128]{1,0:T(8,128)S(1)} %get-tuple-element.35.refs_0_), channel_id=1, source_target_pairs={{0,6},{1,7},{2,4},{3,5},{4,2},{5,3},{6,0},{7,1},{8,14},{9,15},{10,... | collective-permute-start | bytes 24584 | tf_op jit(solution)/shard_map/ppermute | solution.py:490
  34.9 7.2 %collective-permute-done.8.refs_3_ = f32[16,128]{1,0:T(8,128)S(1)} collective-permute-done((f32[16,128]{1,0:T(8,128)S(1)}, f32[16,128]{1,0:T(8,128)S(1)}, u32[]{:S(2)}, u32[]{:S(2)}) %collective-permute-start.8) | collective-permute-done | bytes 8224 | tf_op jit(solution)/shard_map/ppermute | solution.py:490
  42.1 8.2 %collective-permute-start.6 = (f32[16,128]{1,0:T(8,128)S(1)}, f32[16,128]{1,0:T(8,128)S(1)}, u32[]{:S(2)}, u32[]{:S(2)}) collective-permute-start(f32[16,128]{1,0:T(8,128)S(1)} %get-tuple-element.35.refs_0_), channel_id=1, source_target_pairs={{0,2},{1,3},{2,0},{3,1},{4,6},{5,7},{6,4},{7,5},{8,10},{9,11},{10,... | collective-permute-start | bytes 24584 | tf_op jit(solution)/shard_map/ppermute | solution.py:490
  51.9 4.7 %shard_map.190 = (f32[8,256]{1,0:T(8,128)S(1)}, bf16[49,32,128]{2,1,0:T(8,128)(2,1)S(1)}, bf16[49,32,128]{2,1,0:T(8,128)(2,1)S(1)}, bf16[49,32,128]{2,1,0:T(8,128)(2,1)S(1)}, bf16[49,32,128]{2,1,0:T(8,128)(2,1)S(1)}) custom-call(f32[16,128]{1,0:T(8,128)S(1)} %get-tuple-element.35.refs_0_, f32[16,128]{1,0:T(8,128)S(1)} %collective-permute-done.6.refs_1_, ...), custom_call_target="tpu_custom_call" | custom-call | flops 2000000000 | bytes 5234688 | tf_op jit(solution)/shard_map/pallas_call | solution.py:445
  56.7 11.5 %shard_map.192 = (bf16[29,128,256]{2,1,0:T(8,128)(2,1)S(1)}, f32[128,256]{1,0:T(8,128)S(1)}, f32[8,256]{1,0:T(8,128)S(1)}, f32[8,128]{1,0:T(8,128)S(1)}) custom-call(bf16[49,32,128]{2,1,0:T(8,128)(2,1)S(1)} %bitcast.75, bf16[49,32,128]{2,1,0:T(8,128)(2,1)S(1)} %collective-permute-done.12.refs_1_.refs_5_, ...), custom_call_target="tpu_custom_call" | custom-call | flops 2000000000 | bytes 7270400 | tf_op jit(solution)/shard_map/pallas_call | solution.py:445
  68.2 2.4 %collective-permute-start.17 = (f32[8,128]{1,0:T(8,128)S(1)}, f32[8,128]{1,0:T(8,128)S(1)}, u32[]{:S(2)}, u32[]{:S(2)}) collective-permute-start(f32[8,128]{1,0:T(8,128)S(1)} %get-tuple-element.45.refs_0_), channel_id=1, source_target_pairs={{0,6},{1,7},{2,4},{3,5},{4,2},{5,3},{6,0},{7,1},{8,14},{9,15},{10,... | collective-permute-start | bytes 12296 | tf_op jit(solution)/shard_map/ppermute | solution.py:490
  72.6 7.7 %shard_map.193 = (f32[128,256]{1,0:T(8,128)S(1)}, bf16[49,32,128]{2,1,0:T(8,128)(2,1)S(1)}, bf16[49,32,128]{2,1,0:T(8,128)(2,1)S(1)}, f32[5,128,128]{2,1,0:T(8,1...) custom-call(bf16[49,32,128]{2,1,0:T(8,128)(2,1)S(1)} %get-tuple-element.40.refs_0_, ...), custom_call_target="tpu_custom_call" | custom-call | flops 4000000000 | bytes 11182080 | tf_op jit(solution)/shard_map/pallas_call | solution.py:445
  82.2 1.6 %collective-permute-done.23 = bf16[768,128]{1,0:T(8,128)(2,1)S(1)} collective-permute-done((bf16[768,128]{1,0:T(8,128)(2,1)}, bf16[768,128]{1,0:T(8,128)(2,1)S(1)}, u32[]{:S(2)}, u32[]{:S(2)}) %collective-permute-start.23) | collective-permute-done | bytes 196640 | tf_op jit(solution)/shard_map/ppermute | solution.py:487
  88.9 2.4 %collective-permute-done.26 = bf16[192,128]{1,0:T(8,128)(2,1)S(1)} collective-permute-done((bf16[192,128]{1,0:T(8,128)(2,1)S(1)}, bf16[192,128]{1,0:T(8,128)(2,1)S(1)}, u32[]{:S(2)}, u32[]{:S(2)}) %collective-permute-start.26) | collective-permute-done | bytes 49184 | tf_op jit(solution)/shard_map/ppermute | solution.py:493
  92.8 2.4 %collective-permute-start.29 = (bf16[192,128]{1,0:T(8,128)(2,1)S(1)}, bf16[192,128]{1,0:T(8,128)(2,1)S(1)}, u32[]{:S(2)}, u32[]{:S(2)}) collective-permute-start(bf16[192,128]{1,0:T(8,128)(2,1)S(1)} %fusion.4), channel_id=1, source_target_pairs={{0,6},{1,7},{2,4},{3,5},{4,2},{5,3},{6,0},{7,1},{8,14},{9,15},{10,... | collective-permute-start | bytes 147464 | tf_op jit(solution)/shard_map/ppermute | solution.py:490
  95.5 1.8 %collective-permute-start.27 = (bf16[192,128]{1,0:T(8,128)(2,1)S(1)}, bf16[192,128]{1,0:T(8,128)(2,1)S(1)}, u32[]{:S(2)}, u32[]{:S(2)}) collective-permute-start(bf16[192,128]{1,0:T(8,128)(2,1)S(1)} %fusion.4), channel_id=1, source_target_pairs={{0,2},{1,3},{2,0},{3,1},{4,6},{5,7},{6,4},{7,5},{8,10},{9,11},{10,... | collective-permute-start | bytes 147464 | tf_op jit(solution)/shard_map/ppermute | solution.py:490
  98.8 1.8 %collective-permute-done.28 = bf16[192,128]{1,0:T(8,128)(2,1)S(1)} collective-permute-done((bf16[192,128]{1,0:T(8,128)(2,1)S(1)}, bf16[192,128]{1,0:T(8,128)(2,1)S(1)}, u32[]{:S(2)}, u32[]{:S(2)}) %collective-permute-start.28) | collective-permute-done | bytes 49184 | tf_op jit(solution)/shard_map/ppermute | solution.py:490
  105.1 1.6 %collective-permute-start.10 = (bf16[49,32,128]{2,1,0:T(8,128)(2,1)}, bf16[49,32,128]{2,1,0:T(8,128)(2,1)S(1)}, u32[]{:S(2)}, u32[]{:S(2)}) collective-permute-start(bf16[49,32,128]{2,1,0:T(8,128)(2,1)} %copy-done.11), channel_id=1, source_target_pairs={{0,4},{1,5},{2,6},{3,7},{4,0},{5,1},{6,2},{7,3},{8,12},{9,13},{10,... | collective-permute-start | bytes 1204232 | tf_op jit(solution)/shard_map/ppermute | solution.py:490
  106.7 1.8 %collective-permute-start.11 = (bf16[49,32,128]{2,1,0:T(8,128)(2,1)S(1)}, bf16[49,32,128]{2,1,0:T(8,128)(2,1)S(1)}, u32[]{:S(2)}, u32[]{:S(2)}) collective-permute-start(bf16[49,32,128]{2,1,0:T(8,128)(2,1)S(1)} %get-tuple-element.43.refs_3_), channel_id=1, source_target_pairs={{0,6},{1,7},{2,4},{3,5},{4,2},{5,3},{6,0},{7,1},{8,14},{9,15},{10,... | collective-permute-start | bytes 1204232 | tf_op jit(solution)/shard_map/ppermute | solution.py:490
  109.7 3.0 %collective-permute-done.31 = bf16[192,128]{1,0:T(8,128)(2,1)S(1)} collective-permute-done((bf16[192,128]{1,0:T(8,128)(2,1)S(1)}, bf16[192,128]{1,0:T(8,128)(2,1)S(1)}, u32[]{:S(2)}, u32[]{:S(2)}) %collective-permute-start.31) | collective-permute-done | bytes 49184 | tf_op jit(solution)/shard_map/ppermute | solution.py:493
  114.3 3.4 %collective-permute-done.32 = bf16[192,128]{1,0:T(8,128)(2,1)S(1)} collective-permute-done((bf16[192,128]{1,0:T(8,128)(2,1)S(1)}, bf16[192,128]{1,0:T(8,128)(2,1)S(1)}, u32[]{:S(2)}, u32[]{:S(2)}) %collective-permute-start.32) | collective-permute-done | bytes 49184 | tf_op jit(solution)/shard_map/ppermute | solution.py:493
  119.0 2.6 %collective-permute-done.9.refs_1_ = bf16[49,32,128]{2,1,0:T(8,128)(2,1)S(1)} collective-permute-done((bf16[49,32,128]{2,1,0:T(8,128)(2,1)}, bf16[49,32,128]{2,1,0:T(8,128)(2,1)S(1)}, u32[]{:S(2)}, u32[]{:S(2)}) %collective-permute-start.9) | collective-permute-done | bytes 401440 | tf_op jit(solution)/shard_map/ppermute | solution.py:490
  122.7 13.5 %collective-permute-done.10.refs_2_ = bf16[49,32,128]{2,1,0:T(8,128)(2,1)S(1)} collective-permute-done((bf16[49,32,128]{2,1,0:T(8,128)(2,1)}, bf16[49,32,128]{2,1,0:T(8,128)(2,1)S(1)}, u32[]{:S(2)}, u32[]{:S(2)}) %collective-permute-start.10) | collective-permute-done | bytes 401440 | tf_op jit(solution)/shard_map/ppermute | solution.py:490
  136.1 6.1 %collective-permute-start.18 = (f32[32,128]{1,0:T(8,128)S(1)}, f32[32,128]{1,0:T(8,128)S(1)}, u32[]{:S(2)}, u32[]{:S(2)}) collective-permute-start(f32[32,128]{1,0:T(8,128)S(1)} %get-tuple-element.73), channel_id=1, source_target_pairs={{0,2},{1,3},{2,0},{3,1},{4,6},{5,7},{6,4},{7,5},{8,10},{9,11},{10,... | collective-permute-start | bytes 49160 | tf_op jit(solution)/shard_map/ppermute | solution.py:490
  142.3 2.1 %shard_map.191 = bf16[49,32,128]{2,1,0:T(8,128)(2,1)} custom-call(bf16[49,32,128]{2,1,0:T(8,128)(2,1)S(1)} %get-tuple-element.40.refs_0_, bf16[49,32,128]{2,1,0:T(8,128)(2,1)S(1)} %collective-permute-done.9.refs_1_, bf16[49,32,128]{2,1,0:T(8,128)(2,1)S(1)} %collective-permute-done.10.refs_2_, bf16[49,32,128]{2,1,0:T(8,128)(2,1)S(1)} %collective-permute-done.11.refs_3_, ...), custom_call_target="tpu_custom_call" | custom-call | flops 100000000 | bytes 2441216 | tf_op jit(solution)/shard_map/pallas_call | solution.py:445
  144.4 3.6 %shard_map.195 = bf16[49,32,128]{2,1,0:T(8,128)(2,1)} custom-call(f32[32,128]{1,0:T(8,128)S(1)} %get-tuple-element.74.refs_0_, f32[32,128]{1,0:T(8,128)S(1)} %collective-permute-done.18.refs_1_, f32[32,128]{1,0:T(8,128)S(1)} %collective-permute-done.19.refs_2_, f32[32,128]{1,0:T(8,128)S(1)} %collective-permute-done.20.refs_3_, ...), custom_call_target="tpu_custom_call" | custom-call | flops 100000000 | bytes 1753088 | tf_op jit(solution)/shard_map/pallas_call | solution.py:445
  (113 shorter events, 39.6 us)
Async XLA Ops:
  1.3 8.3 %collective-permute-start.5 = (bf16[32,128]{1,0:T(8,128)(2,1)S(1)}, bf16[32,128]{1,0:T(8,128)(2,1)S(1)}, u32[]{:S(2)}, u32[]{:S(2)}) collective-permute-start(bf16[32,128]{1,0:T(8,128)(2,1)S(1)} %slice_bitcast_fusion.4.refs_6_.refs_4_), channel_id=1, source_target_pairs={{0,6},{1,7},{2,4},{3,5},{4,2},{5,3},{6,0},{7,1},{8,14},{9,15},{10,... | collective-permute-start | bytes 24584 | tf_op jit(solution)/shard_map/ppermute | solution.py:490
  6.4 7.9 %collective-permute-start.3 = (bf16[32,128]{1,0:T(8,128)(2,1)S(1)}, bf16[32,128]{1,0:T(8,128)(2,1)S(1)}, u32[]{:S(2)}, u32[]{:S(2)}) collective-permute-start(bf16[32,128]{1,0:T(8,128)(2,1)S(1)} %slice_bitcast_fusion.4.refs_6_.refs_4_), channel_id=1, source_target_pairs={{0,2},{1,3},{2,0},{3,1},{4,6},{5,7},{6,4},{7,5},{8,10},{9,11},{10,... | collective-permute-start | bytes 24584 | tf_op jit(solution)/shard_map/ppermute | solution.py:490
  6.9 8.4 %collective-permute-start.2 = (bf16[49,32,128]{2,1,0:T(8,128)(2,1)}, bf16[49,32,128]{2,1,0:T(8,128)(2,1)S(1)}, u32[]{:S(2)}, u32[]{:S(2)}) collective-permute-start(bf16[49,32,128]{2,1,0:T(8,128)(2,1)} %bitcast.68), channel_id=1, source_target_pairs={{0,1},{1,0},{2,3},{3,2},{4,5},{5,4},{6,7},{7,6},{8,9},{9,8},{10,11... | collective-permute-start | bytes 1204232 | tf_op jit(solution)/shard_map/ppermute | solution.py:487
  7.0 8.4 %collective-permute-start.1 = (bf16[256,512]{1,0:T(8,128)(2,1)}, bf16[256,512]{1,0:T(8,128)(2,1)S(1)}, u32[]{:S(2)}, u32[]{:S(2)}) collective-permute-start(bf16[256,512]{1,0:T(8,128)(2,1)} %bitcast.79), channel_id=1, source_target_pairs={{0,1},{1,0},{2,3},{3,2},{4,5},{5,4},{6,7},{7,6},{8,9},{9,8},{10,11... | collective-permute-start | bytes 786440 | tf_op jit(solution)/shard_map/ppermute | solution.py:487
  10.9 45.7 %collective-permute-start.14 = (bf16[49,32,128]{2,1,0:T(8,128)(2,1)}, bf16[49,32,128]{2,1,0:T(8,128)(2,1)S(1)}, u32[]{:S(2)}, u32[]{:S(2)}) collective-permute-start(bf16[49,32,128]{2,1,0:T(8,128)(2,1)} %bitcast.72), channel_id=1, source_target_pairs={{0,6},{1,7},{2,4},{3,5},{4,2},{5,3},{6,0},{7,1},{8,14},{9,15},{10,... | collective-permute-start | bytes 1204232 | tf_op jit(solution)/shard_map/ppermute | solution.py:490
  14.3 42.3 %collective-permute-start.13 = (bf16[49,32,128]{2,1,0:T(8,128)(2,1)}, bf16[49,32,128]{2,1,0:T(8,128)(2,1)S(1)}, u32[]{:S(2)}, u32[]{:S(2)}) collective-permute-start(bf16[49,32,128]{2,1,0:T(8,128)(2,1)} %bitcast.73), channel_id=1, source_target_pairs={{0,4},{1,5},{2,6},{3,7},{4,0},{5,1},{6,2},{7,3},{8,12},{9,13},{10,... | collective-permute-start | bytes 1204232 | tf_op jit(solution)/shard_map/ppermute | solution.py:490
  14.3 42.3 %collective-permute-start.12 = (bf16[49,32,128]{2,1,0:T(8,128)(2,1)}, bf16[49,32,128]{2,1,0:T(8,128)(2,1)S(1)}, u32[]{:S(2)}, u32[]{:S(2)}) collective-permute-start(bf16[49,32,128]{2,1,0:T(8,128)(2,1)} %bitcast.74), channel_id=1, source_target_pairs={{0,2},{1,3},{2,0},{3,1},{4,6},{5,7},{6,4},{7,5},{8,10},{9,11},{10,... | collective-permute-start | bytes 1204232 | tf_op jit(solution)/shard_map/ppermute | solution.py:490
  31.6 10.5 %collective-permute-start.8 = (f32[16,128]{1,0:T(8,128)S(1)}, f32[16,128]{1,0:T(8,128)S(1)}, u32[]{:S(2)}, u32[]{:S(2)}) collective-permute-start(f32[16,128]{1,0:T(8,128)S(1)} %get-tuple-element.35.refs_0_), channel_id=1, source_target_pairs={{0,6},{1,7},{2,4},{3,5},{4,2},{5,3},{6,0},{7,1},{8,14},{9,15},{10,... | collective-permute-start | bytes 24584 | tf_op jit(solution)/shard_map/ppermute | solution.py:490
  34.9 15.4 %collective-permute-start.7 = (f32[16,128]{1,0:T(8,128)S(1)}, f32[16,128]{1,0:T(8,128)S(1)}, u32[]{:S(2)}, u32[]{:S(2)}) collective-permute-start(f32[16,128]{1,0:T(8,128)S(1)} %get-tuple-element.35.refs_0_), channel_id=1, source_target_pairs={{0,4},{1,5},{2,6},{3,7},{4,0},{5,1},{6,2},{7,3},{8,12},{9,13},{10,... | collective-permute-start | bytes 24584 | tf_op jit(solution)/shard_map/ppermute | solution.py:490
  42.1 9.8 %collective-permute-start.6 = (f32[16,128]{1,0:T(8,128)S(1)}, f32[16,128]{1,0:T(8,128)S(1)}, u32[]{:S(2)}, u32[]{:S(2)}) collective-permute-start(f32[16,128]{1,0:T(8,128)S(1)} %get-tuple-element.35.refs_0_), channel_id=1, source_target_pairs={{0,2},{1,3},{2,0},{3,1},{4,6},{5,7},{6,4},{7,5},{8,10},{9,11},{10,... | collective-permute-start | bytes 24584 | tf_op jit(solution)/shard_map/ppermute | solution.py:490
  68.2 12.1 %collective-permute-start.17 = (f32[8,128]{1,0:T(8,128)S(1)}, f32[8,128]{1,0:T(8,128)S(1)}, u32[]{:S(2)}, u32[]{:S(2)}) collective-permute-start(f32[8,128]{1,0:T(8,128)S(1)} %get-tuple-element.45.refs_0_), channel_id=1, source_target_pairs={{0,6},{1,7},{2,4},{3,5},{4,2},{5,3},{6,0},{7,1},{8,14},{9,15},{10,... | collective-permute-start | bytes 12296 | tf_op jit(solution)/shard_map/ppermute | solution.py:490
  70.6 9.7 %collective-permute-start.16 = (f32[8,128]{1,0:T(8,128)S(1)}, f32[8,128]{1,0:T(8,128)S(1)}, u32[]{:S(2)}, u32[]{:S(2)}) collective-permute-start(f32[8,128]{1,0:T(8,128)S(1)} %get-tuple-element.45.refs_0_), channel_id=1, source_target_pairs={{0,4},{1,5},{2,6},{3,7},{4,0},{5,1},{6,2},{7,3},{8,12},{9,13},{10,... | collective-permute-start | bytes 12296 | tf_op jit(solution)/shard_map/ppermute | solution.py:490
  71.7 8.6 %collective-permute-start.15 = (f32[8,128]{1,0:T(8,128)S(1)}, f32[8,128]{1,0:T(8,128)S(1)}, u32[]{:S(2)}, u32[]{:S(2)}) collective-permute-start(f32[8,128]{1,0:T(8,128)S(1)} %get-tuple-element.45.refs_0_), channel_id=1, source_target_pairs={{0,2},{1,3},{2,0},{3,1},{4,6},{5,7},{6,4},{7,5},{8,10},{9,11},{10,... | collective-permute-start | bytes 12296 | tf_op jit(solution)/shard_map/ppermute | solution.py:490
  92.8 6.0 %collective-permute-start.29 = (bf16[192,128]{1,0:T(8,128)(2,1)S(1)}, bf16[192,128]{1,0:T(8,128)(2,1)S(1)}, u32[]{:S(2)}, u32[]{:S(2)}) collective-permute-start(bf16[192,128]{1,0:T(8,128)(2,1)S(1)} %fusion.4), channel_id=1, source_target_pairs={{0,6},{1,7},{2,4},{3,5},{4,2},{5,3},{6,0},{7,1},{8,14},{9,15},{10,... | collective-permute-start | bytes 147464 | tf_op jit(solution)/shard_map/ppermute | solution.py:490
  95.2 5.4 %collective-permute-start.28 = (bf16[192,128]{1,0:T(8,128)(2,1)S(1)}, bf16[192,128]{1,0:T(8,128)(2,1)S(1)}, u32[]{:S(2)}, u32[]{:S(2)}) collective-permute-start(bf16[192,128]{1,0:T(8,128)(2,1)S(1)} %fusion.4), channel_id=1, source_target_pairs={{0,4},{1,5},{2,6},{3,7},{4,0},{5,1},{6,2},{7,3},{8,12},{9,13},{10,... | collective-permute-start | bytes 147464 | tf_op jit(solution)/shard_map/ppermute | solution.py:490
  102.8 5.7 %collective-permute-start.30 = (bf16[192,128]{1,0:T(8,128)(2,1)S(1)}, bf16[192,128]{1,0:T(8,128)(2,1)S(1)}, u32[]{:S(2)}, u32[]{:S(2)}) collective-permute-start(bf16[192,128]{1,0:T(8,128)(2,1)S(1)} %get-tuple-element.64), channel_id=1, source_target_pairs={{0,8},{8,0},{16,24},{24,16},{1,9},{9,1},{17,25},{25,17},{2,10},{10... | collective-permute-start | bytes 147464 | tf_op jit(solution)/shard_map/ppermute | solution.py:493
  104.1 17.5 %collective-permute-start.9 = (bf16[49,32,128]{2,1,0:T(8,128)(2,1)}, bf16[49,32,128]{2,1,0:T(8,128)(2,1)S(1)}, u32[]{:S(2)}, u32[]{:S(2)}) collective-permute-start(bf16[49,32,128]{2,1,0:T(8,128)(2,1)} %copy-done.13), channel_id=1, source_target_pairs={{0,2},{1,3},{2,0},{3,1},{4,6},{5,7},{6,4},{7,5},{8,10},{9,11},{10,... | collective-permute-start | bytes 1204232 | tf_op jit(solution)/shard_map/ppermute | solution.py:490
  105.1 31.1 %collective-permute-start.10 = (bf16[49,32,128]{2,1,0:T(8,128)(2,1)}, bf16[49,32,128]{2,1,0:T(8,128)(2,1)S(1)}, u32[]{:S(2)}, u32[]{:S(2)}) collective-permute-start(bf16[49,32,128]{2,1,0:T(8,128)(2,1)} %copy-done.11), channel_id=1, source_target_pairs={{0,4},{1,5},{2,6},{3,7},{4,0},{5,1},{6,2},{7,3},{8,12},{9,13},{10,... | collective-permute-start | bytes 1204232 | tf_op jit(solution)/shard_map/ppermute | solution.py:490
  106.7 29.4 %collective-permute-start.11 = (bf16[49,32,128]{2,1,0:T(8,128)(2,1)S(1)}, bf16[49,32,128]{2,1,0:T(8,128)(2,1)S(1)}, u32[]{:S(2)}, u32[]{:S(2)}) collective-permute-start(bf16[49,32,128]{2,1,0:T(8,128)(2,1)S(1)} %get-tuple-element.43.refs_3_), channel_id=1, source_target_pairs={{0,6},{1,7},{2,4},{3,5},{4,2},{5,3},{6,0},{7,1},{8,14},{9,15},{10,... | collective-permute-start | bytes 1204232 | tf_op jit(solution)/shard_map/ppermute | solution.py:490
  108.5 35.9 %collective-permute-start.21 = (bf16[49,32,128]{2,1,0:T(8,128)(2,1)}, bf16[49,32,128]{2,1,0:T(8,128)(2,1)}, u32[]{:S(2)}, u32[]{:S(2)}) collective-permute-start(bf16[49,32,128]{2,1,0:T(8,128)(2,1)} %copy-done.12), channel_id=1, source_target_pairs={{0,1},{1,0},{2,3},{3,2},{4,5},{5,4},{6,7},{7,6},{8,9},{9,8},{10,11... | collective-permute-start | bytes 1204232 | tf_op jit(solution)/shard_map/ppermute | solution.py:487
  118.8 29.2 %collective-permute-start.33 = (bf16[768,128]{1,0:T(8,128)(2,1)}, bf16[768,128]{1,0:T(8,128)(2,1)}, u32[]{:S(2)}, u32[]{:S(2)}) collective-permute-start(bf16[768,128]{1,0:T(8,128)(2,1)} %bitcast.33), channel_id=1, source_target_pairs={{0,1},{1,0},{2,3},{3,2},{4,5},{5,4},{6,7},{7,6},{8,9},{9,8},{10,11... | collective-permute-start | bytes 589832 | tf_op jit(solution)/shard_map/ppermute | solution.py:487
  121.6 22.7 %collective-permute-start.20 = (f32[32,128]{1,0:T(8,128)S(1)}, f32[32,128]{1,0:T(8,128)S(1)}, u32[]{:S(2)}, u32[]{:S(2)}) collective-permute-start(f32[32,128]{1,0:T(8,128)S(1)} %get-tuple-element.71), channel_id=1, source_target_pairs={{0,6},{1,7},{2,4},{3,5},{4,2},{5,3},{6,0},{7,1},{8,14},{9,15},{10,... | collective-permute-start | bytes 49160 | tf_op jit(solution)/shard_map/ppermute | solution.py:490
  136.1 8.2 %collective-permute-start.19 = (f32[32,128]{1,0:T(8,128)S(1)}, f32[32,128]{1,0:T(8,128)S(1)}, u32[]{:S(2)}, u32[]{:S(2)}) collective-permute-start(f32[32,128]{1,0:T(8,128)S(1)} %get-tuple-element.72), channel_id=1, source_target_pairs={{0,4},{1,5},{2,6},{3,7},{4,0},{5,1},{6,2},{7,3},{8,12},{9,13},{10,... | collective-permute-start | bytes 49160 | tf_op jit(solution)/shard_map/ppermute | solution.py:490
  136.1 8.2 %collective-permute-start.18 = (f32[32,128]{1,0:T(8,128)S(1)}, f32[32,128]{1,0:T(8,128)S(1)}, u32[]{:S(2)}, u32[]{:S(2)}) collective-permute-start(f32[32,128]{1,0:T(8,128)S(1)} %get-tuple-element.73), channel_id=1, source_target_pairs={{0,2},{1,3},{2,0},{3,1},{4,6},{5,7},{6,4},{7,5},{8,10},{9,11},{10,... | collective-permute-start | bytes 49160 | tf_op jit(solution)/shard_map/ppermute | solution.py:490
  (27 other events, 233.7 us)
where the time goes:
time: 152 us
  starting transfers between devices  49 us (32%)
  waiting for transfers between devices  40.8 us (27%)
  Pallas kernels  40.6 us (27%)
  local copies, waits for them, and re-layouts  14.8 us (10%)
  other arithmetic  5.32 us (4%)
    ppermute x21, starting transfers between devices, along(): return lax.ppermute(a, 'graph', [(i, i ^ 2 * step) for i in range(ranks)])  41.9 us
    pallas_call x7, Pallas kernels, call(): pl.pallas_call(kernel, out_shape=[jax.ShapeDtypeStruct(s, d) for s, d in...  40.6 us
    ppermute x21, waiting for transfers between devices, along(): return lax.ppermute(a, 'graph', [(i, i ^ 2 * step) for i in range(ranks)])  28.7 us
    ppermute x6, waiting for transfers between devices, beside(): return lax.ppermute(a, 'dp', [(i, i ^ step) for i in range(planes)])  9.92 us
    unnamed x34, local copies, waits for them, and re-layouts  7.19 us
    ppermute x6, starting transfers between devices, beside(): return lax.ppermute(a, 'dp', [(i, i ^ step) for i in range(planes)])  6.43 us
  transfers between devices with their start and end apart: 34, of which 14 were waited for; matrix products, arithmetic and copies ran while one was open for 3% of the time, Pallas kernels for 18%

commit v1 on v0

v1 whole, which is shorter than its diff:
```python
import functools

import jax
import jax.numpy as jnp
import numpy as np
from jax import lax
from jax.experimental import pallas as pl
from jax.experimental.pallas import tpu as pltpu
from jax.sharding import PartitionSpec as P

H = 8
VH = 16
LMAX = 6
MMAX = 2
K = (LMAX + 1) ** 2
BF = jnp.bfloat16
F32 = jnp.float32
CHUNK = 16
LANES = 128


def frame_layout():
    index, degree_of = [], []
    for order in range(MMAX + 1):
        for sign in (1, -1) if order else (1,):
            for degree in range(order, LMAX + 1):
                index.append(degree * degree + degree + sign * order)
                degree_of.append(degree)
    return index, degree_of


ROWS, DEGREE = frame_layout()
R = len(ROWS)
OF_DEGREE = [[r for r in range(R) if DEGREE[r] == degree] for degree in range(LMAX + 1)]
PAIRS = []
_offset = LMAX + 1
for _order in range(1, MMAX + 1):
    _length = LMAX + 1 - _order
    for _i in range(_length):
        PAIRS.append((_order, _offset + _i, _offset + _length + _i))
    _offset += 2 * _length


def dot(a, b, ca=1, cb=0, exact=False):
    return lax.dot_general(
        a,
        b,
        (((ca,), (cb,)), ((), ())),
        precision=lax.Precision.HIGHEST if exact else None,
        preferred_element_type=F32,
    )


def flip(a):
    return jnp.transpose(a.astype(F32)).astype(a.dtype)


def hits(row, count, dtype):
    lines = lax.broadcasted_iota(jnp.int32, (count, row.shape[1]), 0)
    return jnp.where(lines == row.astype(jnp.int32), 1.0, 0.0).astype(dtype)


def head_sum(a):
    return jnp.sum(a.reshape(H, VH, a.shape[1]), axis=1)


def spread(a):
    return jnp.broadcast_to(a[:, None, :], (H, VH, a.shape[1])).reshape(H * VH, a.shape[1])


def turn(table, source, base, degrees, emit, finish=None):
    channels, edges = source.shape[1], source.shape[2]

    def step(i, carry):
        rows = pl.ds(pl.multiple_of(i * CHUNK, CHUNK), CHUNK)
        for start in range(0, edges, LANES):
            lanes = pl.ds(start, LANES)
            carried = None
            for degree in degrees:
                block = range(degree * degree, (degree + 1) ** 2)
                parts = [source[k, rows, lanes].astype(F32) for k in block]
                for r in OF_DEGREE[degree]:
                    total = None
                    for k, part in zip(block, parts):
                        at = base + start
                        term = table[r, k : k + 1, at : at + LANES] * part
                        total = term if total is None else total + term
                    carried = emit(r, rows, lanes, total, carried)
            if finish is not None:
                finish(rows, lanes, carried)
        return carry

    lax.fori_loop(0, channels // CHUNK, step, 0)


def turn_back(table, source, degrees, out):
    channels, edges = source.shape[1], source.shape[2]

    def step(i, carry):
        rows = pl.ds(pl.multiple_of(i * CHUNK, CHUNK), CHUNK)
        for start in range(0, edges, LANES):
            lanes = pl.ds(start, LANES)
            for degree in degrees:
                parts = [source[r, rows, lanes].astype(F32) for r in OF_DEGREE[degree]]
                for k in range(degree * degree, (degree + 1) ** 2):
                    total = None
                    for r, part in zip(OF_DEGREE[degree], parts):
                        term = table[r, k : k + 1, start : start + LANES] * part
                        total = term if total is None else total + term
                    out[k, rows, lanes] = total.astype(out.dtype)
        return carry

    lax.fori_loop(0, channels // CHUNK, step, 0)


def by_sevens(body):
    def step(i, carry):
        body(i * (LMAX + 1))
        return carry

    lax.fori_loop(0, LMAX + 1, step, 0)


def each_k(body):
    by_sevens(lambda k: [body(k + j) for j in range(LMAX + 1)] and None)


def rows_of(pieces):
    return jnp.concatenate(pieces, axis=0)


def whole_order(own, chips, p, span):
    return [own[:, (q ^ p) * span : ((q ^ p) + 1) * span] for q in range(chips)]


def mix_block(w_mix, order, back):
    even, odd = w_mix[2 * order - 1], w_mix[2 * order]
    if back:
        return jnp.concatenate(
            [
                jnp.concatenate([even, odd], axis=1),
                jnp.concatenate([-odd, even], axis=1),
            ],
            axis=0,
        )
    even, odd = flip(even), flip(odd)
    return jnp.concatenate(
        [
            jnp.concatenate([even, -odd], axis=1),
            jnp.concatenate([odd, even], axis=1),
        ],
        axis=0,
    )


def forward_kernel(chips, where, *refs):
    far = refs[:7]
    pack_own, pack_sib, radial_sib, feats_sib = refs[7:11]
    firsts = refs[11 : 11 + chips]
    refs = refs[11 + chips :]
    table, scaled, mixed, gating, pack, radial, weight, stats, query = refs[:9]
    parts = refs[9 : 9 + chips]
    incoming, scaled_rows, back = refs[9 + chips : 12 + chips]
    near = refs[12 + chips : 19 + chips]
    sems = refs[19 + chips]
    copies = [pltpu.make_async_copy(a, b, sems.at[i]) for i, (a, b) in enumerate(zip(far, near))]
    for c in copies:
        c.start()
    radial_own, w_radial, rot, feats_own, w_value, w_mix, w_query = near
    core, chip = where[0], where[1]
    slots = pack_own.shape[1]
    cap = slots // (2 * chips)
    nodes = feats_sib.shape[1]
    targets = chips * nodes
    bins = rot.shape[2]

    edge = lax.broadcasted_iota(jnp.int32, (2 * slots, slots), 1)
    place = lax.broadcasted_iota(jnp.int32, (2 * slots, slots), 0)
    side = (edge // cap) % 2
    origin = side * slots + (2 * ((edge // (2 * cap)) ^ chip) + core) * cap + edge % cap
    pick = jnp.where(place == origin, 1.0, 0.0).astype(BF)
    node_shift = jnp.where(
        (lax.broadcasted_iota(jnp.int32, (16, slots), 0) == 0), float(nodes), 0.0
    )
    packs = jnp.concatenate([pack_own[...], pack_sib[...] + node_shift], axis=1).astype(BF)
    rows = dot(packs, pick)
    lines = rows[4:5] * float(nodes) + rows[1:2]
    pack[...] = rows
    pack[1:2, :] = lines
    bin_hit = hits(rows[2:3], bins, BF)
    source_hit = hits(rows[0:1], 2 * nodes, BF)
    target_hit = hits(lines, targets, BF)
    for c in copies[:2]:
        c.wait()
    radial[...] = dot(pick, rows_of([radial_own[...], radial_sib[...]]), 0, 0).astype(BF)
    gating[...] = jax.nn.sigmoid(dot(flip(w_radial[...]), radial[...], 1, 1))
    copies[2].wait()
    for r, row in enumerate(ROWS):
        table[r, 0:K, :] = dot(rot[row], bin_hit)
    for c in copies[3:]:
        c.wait()
    value_t = flip(w_value[...])

    def gather(k):
        values = [
            dot(value_t, rows_of([feats_own[k + j], feats_sib[k + j]]), 1, 1).astype(BF)
            for j in range(LMAX + 1)
        ]
        got = dot(rows_of(values), source_hit).astype(BF)
        for j in range(LMAX + 1):
            incoming[k + j] = got[j * H * VH : (j + 1) * H * VH]

    by_sevens(gather)

    def emit(r, rows_, lanes, total, carried):
        gate = gating[rows_, lanes] if carried is None else carried
        scaled[r, rows_, lanes] = (total * gate).astype(BF)
        return gate

    turn(table, incoming, 0, range(LMAX + 1), emit)

    zero_t = flip(w_mix[0])
    for r in range(LMAX + 1):
        mixed[r] = dot(zero_t, scaled[r]).astype(BF)
    blocks = [None] + [mix_block(w_mix, order, False) for order in range(1, MMAX + 1)]
    for order, plus, minus in PAIRS:
        out = dot(blocks[order], rows_of([scaled[plus], scaled[minus]])).astype(BF)
        mixed[plus] = out[: H * VH]
        mixed[minus] = out[H * VH :]

    first = rows_of([f[...] for f in firsts])
    queries = dot(flip(w_query[...]), first, 1, 1).astype(BF)
    query[...] = dot(queries, target_hit)
    scores = head_sum(mixed[0].astype(F32) * query[...]) * (1.0 / VH**0.5) + rows[8:16]
    live = rows[3:4] > 0.5
    columns = jnp.transpose(pack[...])
    score_columns = jnp.transpose(scores)
    line = lax.broadcasted_iota(jnp.int32, (slots, targets), 1)
    chosen = (line == columns[:, 1:2].astype(jnp.int32)) & (columns[:, 3:4] > 0.5)
    top = jnp.concatenate(
        [
            jnp.max(jnp.where(chosen, score_columns[:, h : h + 1], 0.0), axis=0, keepdims=True)
            for h in range(H)
        ],
        axis=0,
    )
    top = jnp.maximum(top, 0.0)
    target_hit32 = target_hit.astype(F32)
    top_edge = dot(top, target_hit32, exact=True)
    weights = jnp.where(live, jnp.exp(jnp.where(live, scores - top_edge, 0.0)), 0.0)
    weight[...] = weights
    stats[0:H] = top
    stats[H : 2 * H] = dot(weights, target_hit32, 1, 1, exact=True)

    wide = spread(weights)
    for r in range(R):
        scaled_rows[r] = (mixed[r].astype(F32) * wide).astype(BF)
    turn_back(table, scaled_rows, range(LMAX + 1), back)

    def collect(k):
        out = dot(target_hit, back[k], 1, 1)
        for p in range(chips):
            parts[p][k] = out[p * nodes : (p + 1) * nodes].astype(parts[p].dtype)

    each_k(collect)


def pull_kernel(chips, second, *refs):
    some = chips // 2
    stats = refs[:chips]
    cots = refs[chips : chips + some]
    refs = refs[chips + some :]
    if second:
        before, refs = refs[0], refs[1:]
    else:
        raw, refs = refs[:chips], refs[chips:]
    w_out, pack, weight, table, mixed = refs[:5]
    pulled, pulled0, dalpha, share, dots = refs[5:10]
    parts, refs = ((), refs[10:]) if second else (refs[10 : 10 + chips], refs[10 + chips :])
    incoming, total_ref, wide_ref = refs
    nodes = cots[0].shape[1]
    edges = pulled.shape[2]
    base = edges if second else 0
    span = some * nodes
    lines = pack[1:2, base : base + edges] - (span if second else 0)
    target_hit = hits(lines, span, BF)
    target_hit32 = target_hit.astype(F32)
    out_w = w_out[...]

    def gather(k):
        backs = [
            dot(out_w, rows_of([c[k + j] for c in cots]), 1, 1).astype(BF) for j in range(LMAX + 1)
        ]
        got = dot(rows_of(backs), target_hit).astype(BF)
        for j in range(LMAX + 1):
            incoming[k + j] = got[j * H * VH : (j + 1) * H * VH]

    by_sevens(gather)

    wholes = [
        jnp.concatenate(whole_order(stats[p], chips, p, nodes), axis=1) for p in range(chips)
    ]
    top = functools.reduce(jnp.maximum, [w[0:H] for w in wholes])
    bottom = jnp.exp(-top)
    for w in wholes:
        bottom = bottom + w[H : 2 * H] * jnp.exp(w[0:H] - top)
    factor = jnp.exp(wholes[0][0:H] - top) / bottom
    mine = factor[:, (span if second else 0) : (2 * span if second else span)]
    shares = weight[:, base : base + edges] * dot(mine, target_hit32, exact=True)
    share[...] = shares
    wide_ref[...] = spread(shares)

    def emit(r, rows, lanes, total, carried):
        if carried is None:
            carried = (wide_ref[rows, lanes], None)
        wide, sums = carried
        far = pl.ds(base + lanes.start, lanes.size)
        term = total * mixed[r, rows, far].astype(F32)
        pulled[r, rows, lanes] = (total * wide).astype(BF)
        return (wide, term if sums is None else sums + term)

    def finish(rows, lanes, carried):
        total_ref[rows, lanes] = carried[1]

    turn(table, incoming, base, range(LMAX + 1), emit, finish)
    sums = head_sum(total_ref[...])
    dalpha[...] = sums
    here = dot(shares * sums, target_hit32, 1, 1, exact=True)
    if second:
        dots[...] = jnp.concatenate([before[...], here], axis=1)
    else:
        dots[...] = here
    pulled0[...] = table[0, 0:1, base : base + edges] * incoming[0].astype(F32) * wide_ref[...]
    if not second:
        scale = jnp.transpose(spread(factor))

        def normalize(k):
            for p in range(chips):
                parts[p][k] = (raw[p][k] * scale[p * nodes : (p + 1) * nodes]).astype(BF)

        each_k(normalize)


def back_kernel(chips, *refs):
    parts = refs[:chips]
    cots = refs[chips : 2 * chips]
    (feats_own, feats_sib, pulled_a, pulled_b, scaled, gating, table, pack, w_mix) = refs[
        2 * chips : 2 * chips + 9
    ]
    (gate_sum, dv_own, dv_sib, g_mix, g_value, g_out) = refs[2 * chips + 9 : 2 * chips + 15]
    turned, spread_back = refs[2 * chips + 15 :]
    nodes = feats_own.shape[1]
    wide = H * VH
    gate = gating[...]
    zero = w_mix[0]
    gates = jnp.zeros_like(gate)
    grad = jnp.zeros((wide, wide), F32)

    def pulled(r):
        return jnp.concatenate([pulled_a[r], pulled_b[r]], axis=1)

    for r in range(1, LMAX + 1):
        here = scaled[r]
        down = pulled(r)
        grad = grad + dot(here, down, 1, 1)
        out = dot(zero, down)
        gates = gates + out * here.astype(F32)
        turned[r] = (out * gate).astype(BF)
    g_mix[0] = grad
    for order in range(1, MMAX + 1):
        block = mix_block(w_mix, order, True)
        grad = jnp.zeros((2 * wide, 2 * wide), F32)
        for own, plus, minus in PAIRS:
            if own != order:
                continue
            down = rows_of([pulled(plus), pulled(minus)])
            here = rows_of([scaled[plus], scaled[minus]])
            grad = grad + dot(here, down, 1, 1)
            out = dot(block, down)
            prod = out * here.astype(F32)
            gates = gates + prod[:wide] + prod[wide:]
            turned[plus] = (out[:wide] * gate).astype(BF)
            turned[minus] = (out[wide:] * gate).astype(BF)
        g_mix[2 * order - 1] = grad[:wide, :wide] + grad[wide:, wide:]
        g_mix[2 * order] = grad[:wide, wide:] - grad[wide:, :wide]
    gate_sum[...] = gates
    turn_back(table, turned, range(1, LMAX + 1), spread_back)
    spread_back[0] = jnp.zeros_like(spread_back[0])
    source_hit = hits(pack[0:1], 2 * nodes, BF)

    def collect(k):
        out = dot(source_hit, spread_back[k], 1, 1).astype(BF)
        dv_own[k] = out[:nodes]
        dv_sib[k] = out[nodes:]

    each_k(collect)
    g_value[...] = jnp.zeros_like(g_value)
    g_out[...] = jnp.zeros_like(g_out)

    def weigh(k):
        some = pl.ds(k, LMAX + 1)

        def flat(ref):
            return ref[some].reshape((LMAX + 1) * nodes, wide)

        g_value[...] += dot(flat(feats_own), flat(dv_own), 0, 0) + dot(
            flat(feats_sib), flat(dv_sib), 0, 0
        )
        total = dot(flat(parts[0]), flat(cots[0]), 0, 0)
        for p in range(1, chips):
            total = total + dot(flat(parts[p]), flat(cots[p]), 0, 0)
        g_out[...] += total

    by_sevens(weigh)


def tail_kernel(chips, where, *refs):
    dots = refs[:chips]
    firsts = refs[chips : 2 * chips]
    refs = refs[2 * chips :]
    feat0_sib = refs[0]
    dalphas, shares, pulled0s = refs[1:3], refs[3:5], refs[5:7]
    query, mixed, scaled, gating, table, gate_sum, radial, pack, w_zero = refs[7:16]
    g_mix, g_value, g_out = refs[16:19]
    keep, send, dv_own = refs[19:22]
    dqs = refs[22 : 22 + chips]
    (grads,) = refs[22 + chips :]
    nodes = feat0_sib.shape[0]
    targets = chips * nodes
    wide = H * VH
    target_hit = hits(pack[1:2], targets, F32)

    def both(pair):
        return jnp.concatenate([pair[0][...], pair[1][...]], axis=1)

    total = dots[0][...]
    for p in range(1, chips):
        total = total + jnp.concatenate(whole_order(dots[p], chips, p, nodes), axis=1)
    dscore = both(shares) * (both(dalphas) - dot(total, target_hit, exact=True))
    dlogit = spread(dscore) * (1.0 / VH**0.5)
    down = (both(pulled0s) + dlogit * query[...]).astype(BF)
    here = scaled[0]
    gate = gating[...]
    out = dot(w_zero[...], down)
    dgate = ((gate_sum[...] + out * here.astype(F32)) * (1.0 - gate)).astype(BF)
    back = (table[0, 0:1, :] * (out * gate).astype(BF).astype(F32)).astype(BF)
    source_hit = hits(pack[0:1], 2 * nodes, BF)
    dv = dot(source_hit, back, 1, 1).astype(BF)
    dv_own[...] = dv[:nodes]
    dq = dot(target_hit, dlogit * mixed[0].astype(F32), 1, 1, exact=True)
    for p in range(chips):
        some = dq[p * nodes : (p + 1) * nodes]
        dqs[p][:nodes] = some.astype(BF)
        dqs[p][nodes:] = (some - some.astype(BF).astype(F32)).astype(BF)
    first = rows_of([f[...] for f in firsts])
    node0 = rows_of([firsts[0][...], feat0_sib[...]])
    pieces = [g_value[...] + dot(node0, dv, 0, 0), dot(first, dq.astype(BF), 0, 0), g_out[...]]
    pieces += [g_mix[0] + dot(here, down, 1, 1)]
    pieces += [g_mix[i] for i in range(1, 2 * MMAX + 1)]
    turned = dot(dgate, radial[...])
    for i in range(radial.shape[1] // wide):
        pieces.append(jnp.transpose(turned[:, i * wide : (i + 1) * wide]))
    half = grads.shape[1]
    for i, piece in enumerate(pieces):
        at = i * wide
        grads[at // half, at % half : at % half + wide] = piece
    keep[...] = grads[where[0]]
    send[: keep.shape[0]] = grads[1 - where[0]].astype(BF)
    send[keep.shape[0] :] = dv[nodes:]


def split_kernel(planes, where, keep, got, own, dv0, *outs):
    *sends, total = outs
    rows = keep.shape[0]
    total[...] = (keep[...] + got[:rows].astype(F32)).reshape(total.shape)
    dv0[...] = got[rows:]
    own[...] = total[where[1]]
    for step in range(1, planes):
        sends[step - 1][...] = total[where[1] ^ step].astype(BF)


def address_kernel(planes, own, *refs):
    got, refs = refs[: planes - 1], refs[planes - 1 :]
    dqs, outs = refs[: len(refs) // 2], refs[len(refs) // 2 :]
    total = functools.reduce(jnp.add, [own[...]] + [g[...].astype(F32) for g in got]).astype(BF)
    for dq, out in zip(dqs, outs):
        out[: own.shape[0]] = total
        out[own.shape[0] :] = dq[...]


def settle_kernel(*refs):
    *terms, piece, dquery = refs
    rows, nodes = piece.shape[0], dquery.shape[0]

    def total(values):
        while len(values) > 1:
            values = [a + b for a, b in zip(values[0::2], values[1::2])]
        return values[0].astype(BF)

    piece[...] = total([t[:rows].astype(F32) for t in terms])
    dquery[...] = total(
        [t[rows : rows + nodes].astype(F32) + t[rows + nodes :].astype(F32) for t in terms]
    )


def join_kernel(planes, where, *refs):
    mine, theirs = refs[:planes], refs[planes : 2 * planes]
    g_value, g_query, g_out, g_radial, g_mix, total = refs[2 * planes :]
    for step in range(planes):
        total[where[0] * planes + (where[1] ^ step)] = mine[step][...].astype(F32)
        total[(1 - where[0]) * planes + (where[1] ^ step)] = theirs[step][...].astype(F32)
    wide = H * VH
    flat = total[...].reshape(total.shape[0] * total.shape[1], wide)
    pieces = [flat[i * wide : (i + 1) * wide] for i in range(flat.shape[0] // wide)]
    g_value[...], g_query[...], g_out[...] = pieces[:3]
    for i in range(2 * MMAX + 1):
        g_mix[i] = pieces[3 + i]
    at = 4 + 2 * MMAX
    for i in range(g_radial.shape[0] // wide):
        g_radial[i * wide : (i + 1) * wide] = pieces[at + i]


def nodes_kernel(dquery, dv_own, dv_sib, dv0_own, dv0_sib, cot, w_value, w_query, out):
    value_w = w_value[...]

    def one(k):
        dv = (dv_own[k].astype(F32) + dv_sib[k].astype(F32)).astype(BF)
        out[k] = (cot[k].astype(F32) + dot(dv, value_w, 1, 1)).astype(BF)

    each_k(one)
    dv = (dv0_own[...].astype(F32) + dv0_sib[...].astype(F32)).astype(BF)
    query_part = dot(dquery[...], w_query[...], 1, 1)
    out[0] = (cot[0].astype(F32) + dot(dv, value_w, 1, 1) + query_part).astype(BF)


def add_kernel(*refs):
    *terms, out = refs

    def one(k):
        out[k] = functools.reduce(jnp.add, [t[k].astype(F32) for t in terms]).astype(BF)

    each_k(one)


def update_kernel(*refs):
    *parts, feats, w_out, out = refs
    out_w = w_out[...]

    def one(k):
        total = functools.reduce(jnp.add, [t[k].astype(F32) for t in parts])
        out[k] = (feats[k].astype(F32) + dot(total.astype(BF), out_w)).astype(BF)

    each_k(one)


def call(name, us, kernel, args, outs, scratch=(), smem=0, far=0, limit=24):
    whole = pl.BlockSpec(memory_space=pltpu.VMEM)
    specs = [pl.BlockSpec(memory_space=pltpu.SMEM)] * smem
    specs += [pl.BlockSpec(memory_space=pltpu.HBM)] * far
    specs += [whole] * (len(args) - smem - far)
    buffers = [pltpu.VMEM(s, d) for s, d in scratch]
    if far:
        buffers += [pltpu.VMEM(a.shape, a.dtype) for a in args[smem : smem + far]]
        buffers += [pltpu.SemaphoreType.DMA((far,))]
    return pl.pallas_call(
        kernel,
        out_shape=[jax.ShapeDtypeStruct(s, d) for s, d in outs],
        in_specs=specs,
        out_specs=[whole] * len(outs),
        scratch_shapes=buffers,
        compiler_params=pltpu.CompilerParams(vmem_limit_bytes=limit << 20),
        cost_estimate=pl.CostEstimate(
            flops=int(us * 1.15e9), bytes_accessed=1000, transcendentals=0
        ),
        name=name,
    )(*args)


def shards(
    node_feats,
    cotangent,
    sources,
    targets,
    bins,
    live_mask,
    radial,
    edge_bias,
    w_value,
    w_query,
    w_out,
    w_radial,
    w_mix,
    rotations,
):
    feats = jnp.transpose(node_feats[0], (1, 0, 2))
    cot = jnp.transpose(cotangent[0], (1, 0, 2))
    rot = jnp.transpose(rotations, (1, 2, 0))
    bias = jnp.transpose(edge_bias[0])
    nodes = feats.shape[1]
    wide = feats.shape[2]
    slots = sources.shape[1]
    ranks = lax.axis_size("graph")
    planes = lax.axis_size("dp")
    chips = ranks // 2
    some = chips // 2
    rank = lax.axis_index("graph")
    plane = lax.axis_index("dp")
    core, chip = rank % 2, rank // 2
    spot = chips * nodes
    where = jnp.stack([core, chip, plane]).astype(jnp.int32)
    where_sum = jnp.stack([core, plane]).astype(jnp.int32)

    def other_core(a):
        return lax.ppermute(a, "graph", [(i, i ^ 1) for i in range(ranks)])

    def along(a, step):
        return lax.ppermute(a, "graph", [(i, i ^ (2 * step)) for i in range(ranks)])

    def beside(a, step):
        return lax.ppermute(a, "dp", [(i, i ^ step) for i in range(planes)])

    def direct(a):
        return [a] + [along(a, step) for step in range(1, chips)]

    def doubled(a):
        have = {0: a}
        step = chips // 2
        while step:
            for p in list(have):
                have[p ^ step] = along(have[p], step)
            step //= 2
        return [have[p] for p in range(chips)]

    owner = targets // nodes
    line = lax.broadcasted_iota(jnp.int32, (16, slots), 0)
    ids = jnp.where(line == 0, sources - rank * nodes, 0)
    ids = jnp.where(line == 1, targets - owner * nodes, ids)
    ids = jnp.where(line == 2, bins, ids)
    ids = jnp.where(line == 3, live_mask, ids)
    ids = jnp.where(line == 4, (owner // 2) ^ chip, ids)
    pack_own = ids.astype(F32) + jnp.pad(bias.astype(F32), ((8, 0), (0, 0)))
    cots = doubled(cot)
    pack_sib = other_core(pack_own)
    radial_sib = other_core(radial[0])
    feats_sib = other_core(feats)
    firsts = direct(feats[0])

    edge_f32 = ((wide, slots), F32)
    half_f32 = ((wide, slots // 2), F32)
    block = ((K, nodes, wide), BF)
    table, scaled, mixed, gating, pack, radial_here, weight, stats, query, *raw = call(
        "forward",
        15,
        functools.partial(forward_kernel, chips),
        [
            where,
            radial[0],
            w_radial,
            rot,
            feats,
            w_value,
            w_mix,
            w_query,
            pack_own,
            pack_sib,
            radial_sib,
            feats_sib,
            *firsts,
        ],
        [
            ((R, 56, slots), F32),
            ((R, wide, slots), BF),
            ((R, wide, slots), BF),
            edge_f32,
            ((16, slots), F32),
            ((slots, radial.shape[2]), BF),
            ((H, slots), F32),
            ((2 * H, spot), F32),
            edge_f32,
            *([((K, nodes, wide), F32)] * chips),
        ],
        [((K, wide, slots), BF), ((R, wide, slots), BF), ((K, wide, slots), BF)],
        smem=1,
        far=7,
        limit=32,
    )
    all_stats = direct(stats)

    def pull(second, extra):
        mine = slice(some, chips) if second else slice(0, some)
        return call(
        "pull",
        4.5,
            functools.partial(pull_kernel, chips, second),
            [*all_stats, *cots[mine], *extra, w_out, pack, weight, table, mixed],
            [
                ((R, wide, slots // 2), BF),
                half_f32,
                ((H, slots // 2), F32),
                ((H, slots // 2), F32),
                ((H, spot if second else spot // 2), F32),
                *([] if second else [block] * chips),
            ],
            [((K, wide, slots // 2), BF), half_f32, half_f32],
        )

    pulled_a, pulled0_a, dalpha_a, share_a, dots_a, *parts = pull(False, raw)

    parts, cots[-1] = lax.optimization_barrier((parts, cots[-1]))
    pending = {p: [parts[p]] for p in range(chips)}
    near = {p: along(parts[p], 1) for p in range(chips) if p & 1}
    pulled_b, pulled0_b, dalpha_b, share_b, dots = pull(True, [dots_a])
    all_dots = direct(dots)
    for p, got in near.items():
        del pending[p]
        pending[p ^ 1].append(got)
    summed = {}
    for p in pending:
        if p:
            (summed[p],) = call("add", 1, add_kernel, pending[p], [block])
    summed, pulled_b = lax.optimization_barrier((summed, pulled_b))
    step = 2
    while step < chips:
        for p in [p for p in summed if p & step]:
            got = along(summed.pop(p), step)
            if p ^ step:
                (summed[p ^ step],) = call("add", 1, add_kernel, [summed[p ^ step], got], [block])
            else:
                pending[0].append(got)
        step *= 2
    gate_sum, dv_own, dv_sib, g_mix, g_value, g_out = call(
        "back",
        7.5,
        functools.partial(back_kernel, chips),
        [*parts, *cots, feats, feats_sib, pulled_a, pulled_b, scaled, gating, table, pack, w_mix],
        [edge_f32, block, block, (w_mix.shape, F32), ((wide, wide), F32), ((wide, wide), F32)],
        [((R, wide, slots), BF), ((K, wide, slots), BF)],
        limit=32,
    )
    dv_got = other_core(dv_sib)

    total_rows = (4 + 2 * MMAX) * wide + radial.shape[2]
    cut = total_rows // (2 * planes)
    small = ((nodes, wide), BF)
    keep, send, dv0_own, *dqs = call(
        "tail",
        1.8,
        functools.partial(tail_kernel, chips),
        [
            where_sum,
            *all_dots,
            *firsts,
            feats_sib[0],
            dalpha_a,
            dalpha_b,
            share_a,
            share_b,
            pulled0_a,
            pulled0_b,
            query,
            mixed,
            scaled,
            gating,
            table,
            gate_sum,
            radial_here,
            pack,
            w_mix[0],
            g_mix,
            g_value,
            g_out,
        ],
        [
            ((total_rows // 2, wide), F32),
            ((total_rows // 2 + nodes, wide), BF),
            small,
            *([((2 * nodes, wide), BF)] * chips),
        ],
        [((2, total_rows // 2, wide), F32)],
        smem=1,
    )

    got = other_core(send)
    own, dv0_got, *sends = call(
        "split",
        0.6,
        functools.partial(split_kernel, planes),
        [where_sum, keep, got],
        [((cut, wide), F32), small, *([((cut, wide), BF)] * (planes - 1))],
        [((planes, cut, wide), F32)],
        smem=1,
    )
    got = [beside(sends[step - 1], step) for step in range(1, planes)]
    got, pending[0][1] = lax.optimization_barrier((got, pending[0][1]))
    letters = call(
        "address",
        0.6,
        functools.partial(address_kernel, planes),
        [own, *got, *dqs],
        [((cut + 2 * nodes, wide), BF)] * chips,
    )
    terms = [letters[0]] + [along(letters[step], step) for step in range(1, chips)]
    terms, pending[0] = lax.optimization_barrier((terms, pending[0]))
    piece, dquery = call("settle", 0.6, settle_kernel, terms, [((cut, wide), BF), small])
    (updated,) = call("update", 2, update_kernel, [*pending[0], feats, w_out], [block])
    mine = [piece] + [beside(piece, step) for step in range(1, planes)]
    theirs = [other_core(a) for a in mine]
    grads = call(
        "join",
        1.5,
        functools.partial(join_kernel, planes),
        [where_sum, *mine, *theirs],
        [
            ((wide, wide), F32),
            ((wide, wide), F32),
            ((wide, wide), F32),
            ((radial.shape[2], wide), F32),
            (w_mix.shape, F32),
        ],
        [((2 * planes, cut, wide), F32)],
        smem=1,
    )

    (grad_nodes,) = call(
        "nodes",
        2.6,
        nodes_kernel,
        [dquery, dv_own, dv_got, dv0_own, dv0_got, cot, w_value, w_query],
        [block],
    )
    return (
        jnp.transpose(updated, (1, 0, 2))[None],
        jnp.transpose(grad_nodes, (1, 0, 2))[None],
        *grads,
    )


def solution(mesh):
    edge = P("dp", "graph")
    return jax.shard_map(
        shards,
        mesh=mesh,
        in_specs=(edge, edge, edge, edge, edge, edge, edge, edge, P(), P(), P(), P(), P(), P()),
        out_specs=(edge, edge, P(), P(), P(), P(), P()),
        check_vma=False,
    )
```

time: 152 us -> 110 us (0.72)
  waiting for transfers between devices: 40.8 us -> 23.4 us
  starting transfers between devices: 49 us -> 33.7 us
  local copies, waits for them, and re-layouts: 14.8 us -> 7.87 us
  other arithmetic: 5.32 us -> 3.02 us
    ppermute x21 -> x18, starting transfers between devices: 41.9 us -> 25.3 us  [along(): return lax.ppermute(a, 'graph', [(i, i ^ 2 * step) for i in range(ranks)])]
    ppermute x21 -> x18, waiting for transfers between devices: 28.7 us -> 17.3 us  [along(): return lax.ppermute(a, 'graph', [(i, i ^ 2 * step) for i in range(ranks)])]
    ppermute x6, waiting for transfers between devices: 9.92 us -> 5.77 us  [beside(): return lax.ppermute(a, 'dp', [(i, i ^ step) for i in range(planes)])]
    convert_element_type x5 -> x0, other arithmetic: 2.94 us -> none  [the longest x1 1.3 us: shards(): summed = jnp.where(core == 0, jnp.concatenate([mine, theirs]), jnp.concat...]
    slice x4 -> x0, local copies, waits for them, and re-layouts: 2.15 us -> none  [the longest x1 0.75 us: shards(): summed[3 * wide:(4 + 2 * MMAX) * wide].reshape(w_mix.shape)]
    ppermute x7 -> x9, waiting for transfers between devices: 2.21 us -> 0.33 us  [other_core(): return lax.ppermute(a, 'graph', [(i, i ^ 1) for i in range(ranks)])]
    dynamic_update_slice x3 -> x0, local copies, waits for them, and re-layouts: 1.87 us -> none  [shards(): lax.dynamic_update_index_in_dim(whole, beside(piece, step), plane ^ step, 0)]
    dynamic_update_slice x1 -> x0, other arithmetic: 1.56 us -> none  [shards(): whole = lax.dynamic_update_index_in_dim(whole, piece, plane, 0)]
  transfers between devices with their start and end apart: 34 -> 33, of which waited for: 14 -> 11; matrix products, arithmetic and copies ran while one was open for 3% -> 3% of each run, Pallas kernels for 18% -> 35%
where the time goes in v1:
time: 110 us; the launch traced here: 109 us
  Pallas kernels  40.2 us (37%)
  starting transfers between devices  33.7 us (31%)
  waiting for transfers between devices  23.4 us (21%)
  local copies, waits for them, and re-layouts  7.87 us (7%)
  other arithmetic  3.02 us (3%)
    pallas_call x12, Pallas kernels, call(): pl.pallas_call(kernel, out_shape=[jax.ShapeDtypeStruct(s, d) for s, d in...  40.2 us
    ppermute x18, starting transfers between devices, along(): return lax.ppermute(a, 'graph', [(i, i ^ 2 * step) for i in range(ranks)])  25.3 us
    ppermute x18, waiting for transfers between devices, along(): return lax.ppermute(a, 'graph', [(i, i ^ 2 * step) for i in range(ranks)])  17.3 us
    ppermute x6, starting transfers between devices, beside(): return lax.ppermute(a, 'dp', [(i, i ^ step) for i in range(planes)])  7.11 us
    unnamed x26, local copies, waits for them, and re-layouts  6.41 us
    ppermute x6, waiting for transfers between devices, beside(): return lax.ppermute(a, 'dp', [(i, i ^ step) for i in range(planes)])  5.77 us
  transfers between devices with their start and end apart: 33, of which 11 were waited for; matrix products, arithmetic and copies ran while one was open for 3% of the time, Pallas kernels for 35%

profile of v1, /device:TPU:0, one launch (start us, length us, event | category | flops | bytes accessed | tf_op | source)
XLA Modules:
  0.0 109.1 jit_solution(13475388844458848337)
XLA Ops:
  1.3 3.0 %collective-permute-start.3 = (bf16[32,128]{1,0:T(8,128)(2,1)S(1)}, bf16[32,128]{1,0:T(8,128)(2,1)S(1)}, u32[]{:S(2)}, u32[]{:S(2)}) collective-permute-start(bf16[32,128]{1,0:T(8,128)(2,1)S(1)} %slice_bitcast_fusion.2.refs_11_.refs_4_), channel_id=1, source_target_pairs={{0,2},{1,3},{2,0},{3,1},{4,6},{5,7},{6,4},{7,5},{8,10},{9,11},{10,... | collective-permute-start | bytes 24584 | tf_op jit(solution)/shard_map/ppermute | solution.py:617
  4.4 2.6 %collective-permute-start.4 = (bf16[32,128]{1,0:T(8,128)(2,1)S(1)}, bf16[32,128]{1,0:T(8,128)(2,1)S(1)}, u32[]{:S(2)}, u32[]{:S(2)}) collective-permute-start(bf16[32,128]{1,0:T(8,128)(2,1)S(1)} %slice_bitcast_fusion.2.refs_11_.refs_4_), channel_id=1, source_target_pairs={{0,4},{1,5},{2,6},{3,7},{4,0},{5,1},{6,2},{7,3},{8,12},{9,13},{10,... | collective-permute-start | bytes 24584 | tf_op jit(solution)/shard_map/ppermute | solution.py:617
  12.4 3.3 %collective-permute-start.9 = (bf16[49,32,128]{2,1,0:T(8,128)(2,1)}, bf16[49,32,128]{2,1,0:T(8,128)(2,1)S(1)}, u32[]{:S(2)}, u32[]{:S(2)}) collective-permute-start(bf16[49,32,128]{2,1,0:T(8,128)(2,1)} %bitcast.38), channel_id=1, source_target_pairs={{0,4},{1,5},{2,6},{3,7},{4,0},{5,1},{6,2},{7,3},{8,12},{9,13},{10,... | collective-permute-start | bytes 1204232 | tf_op jit(solution)/shard_map/ppermute | solution.py:617
  22.1 14.9 %forward.1 = (f32[29,56,256]{2,1,0:T(8,128)S(1)}, bf16[29,128,256]{2,1,0:T(8,128)(2,1)S(1)}, bf16[29,128,256]{2,1,0:T(8,128)(2,1)S(1)}, f32[128,256]{1,0:T(8,128...) custom-call(s32[3]{0:T(128)S(1)} %pad_add_fusion.1.where, ...), custom_call_target="tpu_custom_call" | custom-call | flops 17250000896 | bytes 1000 | tf_op jit(solution)/shard_map/forward/pallas_call | solution.py:565
  38.2 3.3 %collective-permute-start.8 = (f32[16,128]{1,0:T(8,128)S(1)}, f32[16,128]{1,0:T(8,128)S(1)}, u32[]{:S(2)}, u32[]{:S(2)}) collective-permute-start(f32[16,128]{1,0:T(8,128)S(1)} %get-tuple-element.81.refs_0_), channel_id=1, source_target_pairs={{0,6},{1,7},{2,4},{3,5},{4,2},{5,3},{6,0},{7,1},{8,14},{9,15},{10,... | collective-permute-start | bytes 24584 | tf_op jit(solution)/shard_map/ppermute | solution.py:617
  41.8 2.0 %collective-permute-done.8.refs_3_ = f32[16,128]{1,0:T(8,128)S(1)} collective-permute-done((f32[16,128]{1,0:T(8,128)S(1)}, f32[16,128]{1,0:T(8,128)S(1)}, u32[]{:S(2)}, u32[]{:S(2)}) %collective-permute-start.8) | collective-permute-done | bytes 8224 | tf_op jit(solution)/shard_map/ppermute | solution.py:617
  43.8 4.5 %pull.2 = (bf16[29,128,128]{2,1,0:T(8,128)(2,1)S(1)}, f32[128,128]{1,0:T(8,128)S(1)}, f32[8,128]{1,0:T(8,128)S(1)}, f32[8,128]{1,0:T(8,128)S(1)}, f32[8,64]{1,0:...) custom-call(f32[16,128]{1,0:T(8,128)S(1)} %get-tuple-element.81.refs, ...), custom_call_target="tpu_custom_call" | custom-call | flops 5175000064 | bytes 1000 | tf_op jit(solution)/shard_map/pull/pallas_call | solution.py:565
  48.3 3.6 %collective-permute-done.11.refs_5_.refs_7_ = bf16[49,32,128]{2,1,0:T(8,128)(2,1)S(1)} collective-permute-done((bf16[49,32,128]{2,1,0:T(8,128)(2,1)S(1)}, bf16[49,32,128]{2,1,0:T(8,128)(2,1)S(1)}, u32[]{:S(2)}, u32[]{:S(2)}) %collective-permute-start.11) | collective-permute-done | bytes 401440 | tf_op jit(solution)/shard_map/ppermute | solution.py:617
  52.2 4.4 %pull.3 = (bf16[29,128,128]{2,1,0:T(8,128)(2,1)S(1)}, f32[128,128]{1,0:T(8,128)S(1)}, f32[8,128]{1,0:T(8,128)S(1)}, f32[8,128]{1,0:T(8,128)S(1)}, f32[8,128]{1,0:T(8,128)S(1)}) custom-call(f32[16,128]{1,0:T(8,128)S(1)} %get-tuple-element.81.refs_0_, f32[16,128]{1,0:T(8,128)S(1)} %collective-permute-done.6.refs_1_, ...), custom_call_target="tpu_custom_call" | custom-call | flops 5175000064 | bytes 1000 | tf_op jit(solution)/shard_map/pull/pallas_call | solution.py:565
  56.6 1.7 %collective-permute-start.12 = (f32[8,128]{1,0:T(8,128)S(1)}, f32[8,128]{1,0:T(8,128)S(1)}, u32[]{:S(2)}, u32[]{:S(2)}) collective-permute-start(f32[8,128]{1,0:T(8,128)S(1)} %get-tuple-element.96.refs_0_), channel_id=1, source_target_pairs={{0,2},{1,3},{2,0},{3,1},{4,6},{5,7},{6,4},{7,5},{8,10},{9,11},{10,... | collective-permute-start | bytes 12296 | tf_op jit(solution)/shard_map/ppermute | solution.py:617
  58.4 2.7 %collective-permute-start.14 = (f32[8,128]{1,0:T(8,128)S(1)}, f32[8,128]{1,0:T(8,128)S(1)}, u32[]{:S(2)}, u32[]{:S(2)}) collective-permute-start(f32[8,128]{1,0:T(8,128)S(1)} %get-tuple-element.96.refs_0_), channel_id=1, source_target_pairs={{0,6},{1,7},{2,4},{3,5},{4,2},{5,3},{6,0},{7,1},{8,14},{9,15},{10,... | collective-permute-start | bytes 12296 | tf_op jit(solution)/shard_map/ppermute | solution.py:617
  62.0 7.6 %back.1 = (f32[128,256]{1,0:T(8,128)S(1)}, bf16[49,32,128]{2,1,0:T(8,128)(2,1)S(1)}, bf16[49,32,128]{2,1,0:T(8,128)(2,1)S(1)}, f32[5,128,128]{2,1,0:T(8,128)S(1)...) custom-call(bf16[49,32,128]{2,1,0:T(8,128)(2,1)S(1)} %get-tuple-element.137.refs_0_, ...), custom_call_target="tpu_custom_call" | custom-call | flops 8625000448 | bytes 1000 | tf_op jit(solution)/shard_map/back/pallas_call | solution.py:565
  69.7 1.8 %tail.1 = (f32[768,128]{1,0:T(8,128)S(1)}, bf16[800,128]{1,0:T(8,128)(2,1)S(1)}, bf16[32,128]{1,0:T(8,128)(2,1)S(1)}, bf16[64,128]{1,0:T(8,128)(2,1)S(1)}, bf16[...) custom-call(s32[2]{0:T(128)S(1)} %pad_add_fusion.where, ...), custom_call_target="tpu_custom_call" | custom-call | flops 2070000000 | bytes 1000 | tf_op jit(solution)/shard_map/tail/pallas_call | solution.py:565
  73.6 1.6 %collective-permute-start.17 = (bf16[192,128]{1,0:T(8,128)(2,1)S(1)}, bf16[192,128]{1,0:T(8,128)(2,1)S(1)}, u32[]{:S(2)}, u32[]{:S(2)}) collective-permute-start(bf16[192,128]{1,0:T(8,128)(2,1)S(1)} %get-tuple-element.121), channel_id=1, source_target_pairs={{0,8},{8,0},{16,24},{24,16},{1,9},{9,1},{17,25},{25,17},{2,10},{10... | collective-permute-start | bytes 147464 | tf_op jit(solution)/shard_map/ppermute | solution.py:620
  75.1 1.5 %collective-permute-start.18 = (bf16[192,128]{1,0:T(8,128)(2,1)S(1)}, bf16[192,128]{1,0:T(8,128)(2,1)S(1)}, u32[]{:S(2)}, u32[]{:S(2)}) collective-permute-start(bf16[192,128]{1,0:T(8,128)(2,1)S(1)} %get-tuple-element.122), channel_id=1, source_target_pairs={{0,16},{8,24},{16,0},{24,8},{1,17},{9,25},{17,1},{25,9},{2,18},{10... | collective-permute-start | bytes 147464 | tf_op jit(solution)/shard_map/ppermute | solution.py:620
  77.7 1.5 %collective-permute-done.18.refs_1_ = bf16[192,128]{1,0:T(8,128)(2,1)S(1)} collective-permute-done((bf16[192,128]{1,0:T(8,128)(2,1)S(1)}, bf16[192,128]{1,0:T(8,128)(2,1)S(1)}, u32[]{:S(2)}, u32[]{:S(2)}) %collective-permute-start.18) | collective-permute-done | bytes 49184 | tf_op jit(solution)/shard_map/ppermute | solution.py:620
  79.2 2.4 %collective-permute-done.19.refs_2_ = bf16[192,128]{1,0:T(8,128)(2,1)S(1)} collective-permute-done((bf16[192,128]{1,0:T(8,128)(2,1)S(1)}, bf16[192,128]{1,0:T(8,128)(2,1)S(1)}, u32[]{:S(2)}, u32[]{:S(2)}) %collective-permute-start.19) | collective-permute-done | bytes 49184 | tf_op jit(solution)/shard_map/ppermute | solution.py:620
  83.0 1.7 %collective-permute-start.22 = (bf16[256,128]{1,0:T(8,128)(2,1)S(1)}, bf16[256,128]{1,0:T(8,128)(2,1)S(1)}, u32[]{:S(2)}, u32[]{:S(2)}) collective-permute-start(bf16[256,128]{1,0:T(8,128)(2,1)S(1)} %get-tuple-element.133), channel_id=1, source_target_pairs={{0,4},{1,5},{2,6},{3,7},{4,0},{5,1},{6,2},{7,3},{8,12},{9,13},{10,... | collective-permute-start | bytes 196616 | tf_op jit(solution)/shard_map/ppermute | solution.py:617
  86.3 11.1 %collective-permute-done.22.refs_2_ = bf16[256,128]{1,0:T(8,128)(2,1)S(1)} collective-permute-done((bf16[256,128]{1,0:T(8,128)(2,1)S(1)}, bf16[256,128]{1,0:T(8,128)(2,1)S(1)}, u32[]{:S(2)}, u32[]{:S(2)}) %collective-permute-start.22) | collective-permute-done | bytes 65568 | tf_op jit(solution)/shard_map/ppermute | solution.py:617
  97.5 1.6 %collective-permute-start.26 = (bf16[192,128]{1,0:T(8,128)(2,1)S(1)}, bf16[192,128]{1,0:T(8,128)(2,1)S(1)}, u32[]{:S(2)}, u32[]{:S(2)}) collective-permute-start(bf16[192,128]{1,0:T(8,128)(2,1)S(1)} %get-tuple-element.149.refs_0_), channel_id=1, source_target_pairs={{0,8},{8,0},{16,24},{24,16},{1,9},{9,1},{17,25},{25,17},{2,10},{10... | collective-permute-start | bytes 147464 | tf_op jit(solution)/shard_map/ppermute | solution.py:620
  99.0 1.5 %collective-permute-start.27 = (bf16[192,128]{1,0:T(8,128)(2,1)S(1)}, bf16[192,128]{1,0:T(8,128)(2,1)S(1)}, u32[]{:S(2)}, u32[]{:S(2)}) collective-permute-start(bf16[192,128]{1,0:T(8,128)(2,1)S(1)} %get-tuple-element.149.refs_0_), channel_id=1, source_target_pairs={{0,16},{8,24},{16,0},{24,8},{1,17},{9,25},{17,1},{25,9},{2,18},{10... | collective-permute-start | bytes 147464 | tf_op jit(solution)/shard_map/ppermute | solution.py:620
  101.0 2.6 %nodes.1 = bf16[49,32,128]{2,1,0:T(8,128)(2,1)} custom-call(bf16[32,128]{1,0:T(8,128)(2,1)S(1)} %get-tuple-element.144.dquery, bf16[49,32,128]{2,1,0:T(8,128)(2,1)S(1)} %get-tuple-element.145.dv_own, bf16[49,32,128]{2,1,0:T(8,128)(2,1)S(1)} %collective-permute-done.25.dv_sib, bf16[32,128]{1,0:T(8,128)(2,1)S(1)} %get-tuple-element.147.dv0_own, ...), custom_call_target="tpu_custom_call" | custom-call | flops 2990000128 | bytes 1000 | tf_op jit(solution)/shard_map/nodes/pallas_call | solution.py:565
  105.5 2.1 %update.1 = bf16[49,32,128]{2,1,0:T(8,128)(2,1)} custom-call(bf16[49,32,128]{2,1,0:T(8,128)(2,1)S(1)} %get-tuple-element.137.refs_0_, bf16[49,32,128]{2,1,0:T(8,128)(2,1)S(1)} %collective-permute-done.20.refs_1_, bf16[49,32,128]{2,1,0:T(8,128)(2,1)S(1)} %collective-permute-done.24.refs_2_, bf16[49,32,128]{2,1,0:T(8,128)(2,1)S(1)} %bitcast.35, ...), custom_call_target="tpu_custom_call" | custom-call | flops 2300000000 | bytes 1000 | tf_op jit(solution)/shard_map/update/pallas_call | solution.py:565
  107.6 1.5 %join.1 = (f32[128,128]{1,0:T(8,128)}, f32[128,128]{1,0:T(8,128)}, f32[128,128]{1,0:T(8,128)}, f32[512,128]{1,0:T(8,128)}, f32[5,128,128]{2,1,0:T(8,128)}) custom-call(s32[2]{0:T(128)S(1)} %pad_add_fusion.where, bf16[192,128]{1,0:T(8,128)(2,1)S(1)} %get-tuple-element.149.refs_0_, bf16[192,128]{1,0:T(8,128)(2,1)S(1)} %collective-permute-done.26.refs_1_, ...), custom_call_target="tpu_custom_call" | custom-call | flops 1724999936 | bytes 1000 | tf_op jit(solution)/shard_map/join/pallas_call | solution.py:565
  (92 shorter events, 23.6 us)
Async XLA Ops:
  1.3 9.9 %collective-permute-start.3 = (bf16[32,128]{1,0:T(8,128)(2,1)S(1)}, bf16[32,128]{1,0:T(8,128)(2,1)S(1)}, u32[]{:S(2)}, u32[]{:S(2)}) collective-permute-start(bf16[32,128]{1,0:T(8,128)(2,1)S(1)} %slice_bitcast_fusion.2.refs_11_.refs_4_), channel_id=1, source_target_pairs={{0,2},{1,3},{2,0},{3,1},{4,6},{5,7},{6,4},{7,5},{8,10},{9,11},{10,... | collective-permute-start | bytes 24584 | tf_op jit(solution)/shard_map/ppermute | solution.py:617
  4.4 7.0 %collective-permute-start.4 = (bf16[32,128]{1,0:T(8,128)(2,1)S(1)}, bf16[32,128]{1,0:T(8,128)(2,1)S(1)}, u32[]{:S(2)}, u32[]{:S(2)}) collective-permute-start(bf16[32,128]{1,0:T(8,128)(2,1)S(1)} %slice_bitcast_fusion.2.refs_11_.refs_4_), channel_id=1, source_target_pairs={{0,4},{1,5},{2,6},{3,7},{4,0},{5,1},{6,2},{7,3},{8,12},{9,13},{10,... | collective-permute-start | bytes 24584 | tf_op jit(solution)/shard_map/ppermute | solution.py:617
  6.9 5.4 %collective-permute-start.5 = (bf16[32,128]{1,0:T(8,128)(2,1)S(1)}, bf16[32,128]{1,0:T(8,128)(2,1)S(1)}, u32[]{:S(2)}, u32[]{:S(2)}) collective-permute-start(bf16[32,128]{1,0:T(8,128)(2,1)S(1)} %slice_bitcast_fusion.2.refs_11_.refs_4_), channel_id=1, source_target_pairs={{0,6},{1,7},{2,4},{3,5},{4,2},{5,3},{6,0},{7,1},{8,14},{9,15},{10,... | collective-permute-start | bytes 24584 | tf_op jit(solution)/shard_map/ppermute | solution.py:617
  6.9 8.8 %collective-permute-start.2 = (bf16[49,32,128]{2,1,0:T(8,128)(2,1)}, bf16[49,32,128]{2,1,0:T(8,128)(2,1)S(1)}, u32[]{:S(2)}, u32[]{:S(2)}) collective-permute-start(bf16[49,32,128]{2,1,0:T(8,128)(2,1)} %bitcast.32), channel_id=1, source_target_pairs={{0,1},{1,0},{2,3},{3,2},{4,5},{5,4},{6,7},{7,6},{8,9},{9,8},{10,11... | collective-permute-start | bytes 1204232 | tf_op jit(solution)/shard_map/ppermute | solution.py:614
  7.0 8.8 %collective-permute-start.1 = (bf16[256,512]{1,0:T(8,128)(2,1)}, bf16[256,512]{1,0:T(8,128)(2,1)S(1)}, u32[]{:S(2)}, u32[]{:S(2)}) collective-permute-start(bf16[256,512]{1,0:T(8,128)(2,1)} %bitcast.42), channel_id=1, source_target_pairs={{0,1},{1,0},{2,3},{3,2},{4,5},{5,4},{6,7},{7,6},{8,9},{9,8},{10,11... | collective-permute-start | bytes 786440 | tf_op jit(solution)/shard_map/ppermute | solution.py:614
  11.3 30.2 %collective-permute-start.10 = (bf16[49,32,128]{2,1,0:T(8,128)(2,1)}, bf16[49,32,128]{2,1,0:T(8,128)(2,1)S(1)}, u32[]{:S(2)}, u32[]{:S(2)}) collective-permute-start(bf16[49,32,128]{2,1,0:T(8,128)(2,1)} %bitcast.37), channel_id=1, source_target_pairs={{0,2},{1,3},{2,0},{3,1},{4,6},{5,7},{6,4},{7,5},{8,10},{9,11},{10,... | collective-permute-start | bytes 1204232 | tf_op jit(solution)/shard_map/ppermute | solution.py:617
  12.4 29.1 %collective-permute-start.9 = (bf16[49,32,128]{2,1,0:T(8,128)(2,1)}, bf16[49,32,128]{2,1,0:T(8,128)(2,1)S(1)}, u32[]{:S(2)}, u32[]{:S(2)}) collective-permute-start(bf16[49,32,128]{2,1,0:T(8,128)(2,1)} %bitcast.38), channel_id=1, source_target_pairs={{0,4},{1,5},{2,6},{3,7},{4,0},{5,1},{6,2},{7,3},{8,12},{9,13},{10,... | collective-permute-start | bytes 1204232 | tf_op jit(solution)/shard_map/ppermute | solution.py:617
  38.2 5.6 %collective-permute-start.8 = (f32[16,128]{1,0:T(8,128)S(1)}, f32[16,128]{1,0:T(8,128)S(1)}, u32[]{:S(2)}, u32[]{:S(2)}) collective-permute-start(f32[16,128]{1,0:T(8,128)S(1)} %get-tuple-element.81.refs_0_), channel_id=1, source_target_pairs={{0,6},{1,7},{2,4},{3,5},{4,2},{5,3},{6,0},{7,1},{8,14},{9,15},{10,... | collective-permute-start | bytes 24584 | tf_op jit(solution)/shard_map/ppermute | solution.py:617
  41.5 10.4 %collective-permute-start.11 = (bf16[49,32,128]{2,1,0:T(8,128)(2,1)S(1)}, bf16[49,32,128]{2,1,0:T(8,128)(2,1)S(1)}, u32[]{:S(2)}, u32[]{:S(2)}) collective-permute-start(bf16[49,32,128]{2,1,0:T(8,128)(2,1)S(1)} %collective-permute-done.9.refs_4_.refs_6_), channel_id=1, source_target_pairs={{0,2},{1,3},{2,0},{3,1},{4,6},{5,7},{6,4},{7,5},{8,10},{9,11},{10,... | collective-permute-start | bytes 1204232 | tf_op jit(solution)/shard_map/ppermute | solution.py:617
  51.9 10.0 %collective-permute-start.15 = (bf16[49,32,128]{2,1,0:T(8,128)(2,1)S(1)}, bf16[49,32,128]{2,1,0:T(8,128)(2,1)S(1)}, u32[]{:S(2)}, u32[]{:S(2)}) collective-permute-start(bf16[49,32,128]{2,1,0:T(8,128)(2,1)S(1)} %get-tuple-element.109.refs_3_), channel_id=1, source_target_pairs={{0,2},{1,3},{2,0},{3,1},{4,6},{5,7},{6,4},{7,5},{8,10},{9,11},{10,... | collective-permute-start | bytes 1204232 | tf_op jit(solution)/shard_map/ppermute | solution.py:617
  56.6 13.0 %collective-permute-start.12 = (f32[8,128]{1,0:T(8,128)S(1)}, f32[8,128]{1,0:T(8,128)S(1)}, u32[]{:S(2)}, u32[]{:S(2)}) collective-permute-start(f32[8,128]{1,0:T(8,128)S(1)} %get-tuple-element.96.refs_0_), channel_id=1, source_target_pairs={{0,2},{1,3},{2,0},{3,1},{4,6},{5,7},{6,4},{7,5},{8,10},{9,11},{10,... | collective-permute-start | bytes 12296 | tf_op jit(solution)/shard_map/ppermute | solution.py:617
  58.4 11.3 %collective-permute-start.13 = (f32[8,128]{1,0:T(8,128)S(1)}, f32[8,128]{1,0:T(8,128)S(1)}, u32[]{:S(2)}, u32[]{:S(2)}) collective-permute-start(f32[8,128]{1,0:T(8,128)S(1)} %get-tuple-element.96.refs_0_), channel_id=1, source_target_pairs={{0,4},{1,5},{2,6},{3,7},{4,0},{5,1},{6,2},{7,3},{8,12},{9,13},{10,... | collective-permute-start | bytes 12296 | tf_op jit(solution)/shard_map/ppermute | solution.py:617
  58.4 11.3 %collective-permute-start.14 = (f32[8,128]{1,0:T(8,128)S(1)}, f32[8,128]{1,0:T(8,128)S(1)}, u32[]{:S(2)}, u32[]{:S(2)}) collective-permute-start(f32[8,128]{1,0:T(8,128)S(1)} %get-tuple-element.96.refs_0_), channel_id=1, source_target_pairs={{0,6},{1,7},{2,4},{3,5},{4,2},{5,3},{6,0},{7,1},{8,14},{9,15},{10,... | collective-permute-start | bytes 12296 | tf_op jit(solution)/shard_map/ppermute | solution.py:617
  61.1 15.6 %collective-permute-start.20 = (bf16[49,32,128]{2,1,0:T(8,128)(2,1)S(1)}, bf16[49,32,128]{2,1,0:T(8,128)(2,1)S(1)}, u32[]{:S(2)}, u32[]{:S(2)}) collective-permute-start(bf16[49,32,128]{2,1,0:T(8,128)(2,1)S(1)} %get-tuple-element.107.refs_1_), channel_id=1, source_target_pairs={{0,2},{1,3},{2,0},{3,1},{4,6},{5,7},{6,4},{7,5},{8,10},{9,11},{10,... | collective-permute-start | bytes 1204232 | tf_op jit(solution)/shard_map/ppermute | solution.py:617
  71.5 25.9 %collective-permute-start.24 = (bf16[49,32,128]{2,1,0:T(8,128)(2,1)S(1)}, bf16[49,32,128]{2,1,0:T(8,128)(2,1)S(1)}, u32[]{:S(2)}, u32[]{:S(2)}) collective-permute-start(bf16[49,32,128]{2,1,0:T(8,128)(2,1)S(1)} %add.22), channel_id=1, source_target_pairs={{0,4},{1,5},{2,6},{3,7},{4,0},{5,1},{6,2},{7,3},{8,12},{9,13},{10,... | collective-permute-start | bytes 1204232 | tf_op jit(solution)/shard_map/ppermute | solution.py:617
  72.5 28.5 %collective-permute-start.25 = (bf16[49,32,128]{2,1,0:T(8,128)(2,1)S(1)}, bf16[49,32,128]{2,1,0:T(8,128)(2,1)S(1)}, u32[]{:S(2)}, u32[]{:S(2)}) collective-permute-start(bf16[49,32,128]{2,1,0:T(8,128)(2,1)S(1)} %get-tuple-element.146), channel_id=1, source_target_pairs={{0,1},{1,0},{2,3},{3,2},{4,5},{5,4},{6,7},{7,6},{8,9},{9,8},{10,11... | collective-permute-start | bytes 1204232 | tf_op jit(solution)/shard_map/ppermute | solution.py:614
  76.7 5.0 %collective-permute-start.19 = (bf16[192,128]{1,0:T(8,128)(2,1)S(1)}, bf16[192,128]{1,0:T(8,128)(2,1)S(1)}, u32[]{:S(2)}, u32[]{:S(2)}) collective-permute-start(bf16[192,128]{1,0:T(8,128)(2,1)S(1)} %get-tuple-element.123), channel_id=1, source_target_pairs={{0,24},{8,16},{16,8},{24,0},{1,25},{9,17},{17,9},{25,1},{2,26},{10... | collective-permute-start | bytes 147464 | tf_op jit(solution)/shard_map/ppermute | solution.py:620
  81.7 4.6 %collective-permute-start.21 = (bf16[256,128]{1,0:T(8,128)(2,1)S(1)}, bf16[256,128]{1,0:T(8,128)(2,1)S(1)}, u32[]{:S(2)}, u32[]{:S(2)}) collective-permute-start(bf16[256,128]{1,0:T(8,128)(2,1)S(1)} %get-tuple-element.132), channel_id=1, source_target_pairs={{0,2},{1,3},{2,0},{3,1},{4,6},{5,7},{6,4},{7,5},{8,10},{9,11},{10,... | collective-permute-start | bytes 196616 | tf_op jit(solution)/shard_map/ppermute | solution.py:617
  83.0 14.4 %collective-permute-start.22 = (bf16[256,128]{1,0:T(8,128)(2,1)S(1)}, bf16[256,128]{1,0:T(8,128)(2,1)S(1)}, u32[]{:S(2)}, u32[]{:S(2)}) collective-permute-start(bf16[256,128]{1,0:T(8,128)(2,1)S(1)} %get-tuple-element.133), channel_id=1, source_target_pairs={{0,4},{1,5},{2,6},{3,7},{4,0},{5,1},{6,2},{7,3},{8,12},{9,13},{10,... | collective-permute-start | bytes 196616 | tf_op jit(solution)/shard_map/ppermute | solution.py:617
  84.8 12.6 %collective-permute-start.23 = (bf16[256,128]{1,0:T(8,128)(2,1)S(1)}, bf16[256,128]{1,0:T(8,128)(2,1)S(1)}, u32[]{:S(2)}, u32[]{:S(2)}) collective-permute-start(bf16[256,128]{1,0:T(8,128)(2,1)S(1)} %get-tuple-element.134), channel_id=1, source_target_pairs={{0,6},{1,7},{2,4},{3,5},{4,2},{5,3},{6,0},{7,1},{8,14},{9,15},{10,... | collective-permute-start | bytes 196616 | tf_op jit(solution)/shard_map/ppermute | solution.py:617
  97.5 6.2 %collective-permute-start.26 = (bf16[192,128]{1,0:T(8,128)(2,1)S(1)}, bf16[192,128]{1,0:T(8,128)(2,1)S(1)}, u32[]{:S(2)}, u32[]{:S(2)}) collective-permute-start(bf16[192,128]{1,0:T(8,128)(2,1)S(1)} %get-tuple-element.149.refs_0_), channel_id=1, source_target_pairs={{0,8},{8,0},{16,24},{24,16},{1,9},{9,1},{17,25},{25,17},{2,10},{10... | collective-permute-start | bytes 147464 | tf_op jit(solution)/shard_map/ppermute | solution.py:620
  99.0 5.2 %collective-permute-start.27 = (bf16[192,128]{1,0:T(8,128)(2,1)S(1)}, bf16[192,128]{1,0:T(8,128)(2,1)S(1)}, u32[]{:S(2)}, u32[]{:S(2)}) collective-permute-start(bf16[192,128]{1,0:T(8,128)(2,1)S(1)} %get-tuple-element.149.refs_0_), channel_id=1, source_target_pairs={{0,16},{8,24},{16,0},{24,8},{1,17},{9,25},{17,1},{25,9},{2,18},{10... | collective-permute-start | bytes 147464 | tf_op jit(solution)/shard_map/ppermute | solution.py:620
  100.5 5.0 %collective-permute-start.28 = (bf16[192,128]{1,0:T(8,128)(2,1)S(1)}, bf16[192,128]{1,0:T(8,128)(2,1)S(1)}, u32[]{:S(2)}, u32[]{:S(2)}) collective-permute-start(bf16[192,128]{1,0:T(8,128)(2,1)S(1)} %get-tuple-element.149.refs_0_), channel_id=1, source_target_pairs={{0,24},{8,16},{16,8},{24,0},{1,25},{9,17},{17,9},{25,1},{2,26},{10... | collective-permute-start | bytes 147464 | tf_op jit(solution)/shard_map/ppermute | solution.py:620
  101.0 6.6 %collective-permute-start.29 = (bf16[192,128]{1,0:T(8,128)(2,1)S(1)}, bf16[192,128]{1,0:T(8,128)(2,1)S(1)}, u32[]{:S(2)}, u32[]{:S(2)}) collective-permute-start(bf16[192,128]{1,0:T(8,128)(2,1)S(1)} %get-tuple-element.149.refs_0_), channel_id=1, source_target_pairs={{0,1},{1,0},{2,3},{3,2},{4,5},{5,4},{6,7},{7,6},{8,9},{9,8},{10,11... | collective-permute-start | bytes 147464 | tf_op jit(solution)/shard_map/ppermute | solution.py:614
  (22 other events, 131.7 us)

commit v2 on v1

--- a/solution.py
+++ b/solution.py
@@ -154,24 +154,18 @@
 
 
 def forward_kernel(chips, where, *refs):
-    far = refs[:7]
-    pack_own, pack_sib, radial_sib, feats_sib = refs[7:11]
-    firsts = refs[11 : 11 + chips]
-    refs = refs[11 + chips :]
-    table, scaled, mixed, gating, pack, radial, weight, stats, query = refs[:9]
-    parts = refs[9 : 9 + chips]
-    incoming, scaled_rows, back = refs[9 + chips : 12 + chips]
-    near = refs[12 + chips : 19 + chips]
-    sems = refs[19 + chips]
+    far, refs = refs[:6], refs[6:]
+    pack_own, pack_sib, radial_sib, feats_sib, *refs = refs
+    table, scaled, mixed, gating, pack, radial, incoming, *refs = refs
+    near, sems = refs[:6], refs[6]
     copies = [pltpu.make_async_copy(a, b, sems.at[i]) for i, (a, b) in enumerate(zip(far, near))]
     for c in copies:
         c.start()
-    radial_own, w_radial, rot, feats_own, w_value, w_mix, w_query = near
+    radial_own, w_radial, rot, feats_own, w_value, w_mix = near
     core, chip = where[0], where[1]
     slots = pack_own.shape[1]
     cap = slots // (2 * chips)
     nodes = feats_sib.shape[1]
-    targets = chips * nodes
     bins = rot.shape[2]
 
     edge = lax.broadcasted_iota(jnp.int32, (2 * slots, slots), 1)
@@ -179,17 +173,24 @@
     side = (edge // cap) % 2
     origin = side * slots + (2 * ((edge // (2 * cap)) ^ chip) + core) * cap + edge % cap
     pick = jnp.where(place == origin, 1.0, 0.0).astype(BF)
-    node_shift = jnp.where(
-        (lax.broadcasted_iota(jnp.int32, (16, slots), 0) == 0), float(nodes), 0.0
-    )
-    packs = jnp.concatenate([pack_own[...], pack_sib[...] + node_shift], axis=1).astype(BF)
+
+    def relative(raw):
+        ids = raw[0:2].astype(jnp.int32)
+        owner = ids[1:2] // nodes
+        source = ids[0:1] - 2 * chip * nodes
+        swapped = jnp.where(source < nodes, source + nodes, source - nodes)
+        rows_ = [jnp.where(core == 0, source, swapped), ids[1:2] - owner * nodes]
+        rows_ = [a.astype(F32) for a in rows_ + [(owner // 2) ^ chip]]
+        return jnp.concatenate([rows_[0], rows_[1], raw[2:4], rows_[2], raw[5:]], axis=0)
+
+    packs = [relative(pack_own[...]), relative(pack_sib[...])]
+    packs = jnp.concatenate(packs, axis=1).astype(BF)
     rows = dot(packs, pick)
     lines = rows[4:5] * float(nodes) + rows[1:2]
     pack[...] = rows
     pack[1:2, :] = lines
     bin_hit = hits(rows[2:3], bins, BF)
     source_hit = hits(rows[0:1], 2 * nodes, BF)
-    target_hit = hits(lines, targets, BF)
     for c in copies[:2]:
         c.wait()
     radial[...] = dot(pick, rows_of([radial_own[...], radial_sib[...]]), 0, 0).astype(BF)
@@ -228,12 +229,27 @@
         mixed[plus] = out[: H * VH]
         mixed[minus] = out[H * VH :]
 
+
+def attend_kernel(chips, *refs):
+    far, refs = refs[0], refs[1:]
+    firsts, refs = refs[:chips], refs[chips:]
+    pack, table, mixed, weight, stats, query, *refs = refs
+    parts, refs = refs[:chips], refs[chips:]
+    scaled_rows, back, w_query, sems = refs
+    copy = pltpu.make_async_copy(far, w_query, sems.at[0])
+    copy.start()
+    slots = pack.shape[1]
+    nodes = firsts[0].shape[0]
+    targets = chips * nodes
+    rows = pack[...]
+    target_hit = hits(rows[1:2], targets, BF)
     first = rows_of([f[...] for f in firsts])
+    copy.wait()
     queries = dot(flip(w_query[...]), first, 1, 1).astype(BF)
     query[...] = dot(queries, target_hit)
     scores = head_sum(mixed[0].astype(F32) * query[...]) * (1.0 / VH**0.5) + rows[8:16]
     live = rows[3:4] > 0.5
-    columns = jnp.transpose(pack[...])
+    columns = jnp.transpose(rows)
     score_columns = jnp.transpose(scores)
     line = lax.broadcasted_iota(jnp.int32, (slots, targets), 1)
     chosen = (line == columns[:, 1:2].astype(jnp.int32)) & (columns[:, 3:4] > 0.5)
@@ -265,38 +281,13 @@
     each_k(collect)
 
 
-def pull_kernel(chips, second, *refs):
-    some = chips // 2
-    stats = refs[:chips]
-    cots = refs[chips : chips + some]
-    refs = refs[chips + some :]
-    if second:
-        before, refs = refs[0], refs[1:]
-    else:
-        raw, refs = refs[:chips], refs[chips:]
-    w_out, pack, weight, table, mixed = refs[:5]
-    pulled, pulled0, dalpha, share, dots = refs[5:10]
-    parts, refs = ((), refs[10:]) if second else (refs[10 : 10 + chips], refs[10 + chips :])
-    incoming, total_ref, wide_ref = refs
-    nodes = cots[0].shape[1]
-    edges = pulled.shape[2]
-    base = edges if second else 0
-    span = some * nodes
-    lines = pack[1:2, base : base + edges] - (span if second else 0)
-    target_hit = hits(lines, span, BF)
-    target_hit32 = target_hit.astype(F32)
-    out_w = w_out[...]
-
-    def gather(k):
-        backs = [
-            dot(out_w, rows_of([c[k + j] for c in cots]), 1, 1).astype(BF) for j in range(LMAX + 1)
-        ]
-        got = dot(rows_of(backs), target_hit).astype(BF)
-        for j in range(LMAX + 1):
-            incoming[k + j] = got[j * H * VH : (j + 1) * H * VH]
-
-    by_sevens(gather)
-
+def share_kernel(chips, *refs):
+    stats, raw = refs[:chips], refs[chips : 2 * chips]
+    weight, pack, share = refs[2 * chips : 2 * chips + 3]
+    parts = refs[2 * chips + 3 :]
+    targets = stats[0].shape[1]
+    nodes = targets // chips
+    target_hit32 = hits(pack[1:2], targets, F32)
     wholes = [
         jnp.concatenate(whole_order(stats[p], chips, p, nodes), axis=1) for p in range(chips)
     ]
@@ -305,59 +296,81 @@
     for w in wholes:
         bottom = bottom + w[H : 2 * H] * jnp.exp(w[0:H] - top)
     factor = jnp.exp(wholes[0][0:H] - top) / bottom
-    mine = factor[:, (span if second else 0) : (2 * span if second else span)]
-    shares = weight[:, base : base + edges] * dot(mine, target_hit32, exact=True)
-    share[...] = shares
-    wide_ref[...] = spread(shares)
+    share[...] = weight[...] * dot(factor, target_hit32, exact=True)
+    scale = jnp.transpose(spread(factor))
+
+    def normalize(k):
+        for p in range(chips):
+            parts[p][k] = (raw[p][k] * scale[p * nodes : (p + 1) * nodes]).astype(BF)
+
+    each_k(normalize)
+
+
+def pull_kernel(chips, second, *refs):
+    some = chips // 2
+    cots, refs = refs[:some], refs[some:]
+    w_out, pack, table, mixed, *refs = refs
+    if second:
+        before, share, pulled, pulled0, dalpha, dots, *refs = refs
+    else:
+        pulled, pulled0, dalpha, *refs = refs
+    incoming, total_ref = refs
+    nodes = cots[0].shape[1]
+    edges = pulled.shape[2]
+    base = edges if second else 0
+    span = some * nodes
+    lines = pack[1:2, base : base + edges] - (span if second else 0)
+    target_hit = hits(lines, span, BF)
+    out_w = w_out[...]
+
+    def gather(k):
+        backs = [
+            dot(out_w, rows_of([c[k + j] for c in cots]), 1, 1).astype(BF) for j in range(LMAX + 1)
+        ]
+        got = dot(rows_of(backs), target_hit).astype(BF)
+        for j in range(LMAX + 1):
+            incoming[k + j] = got[j * H * VH : (j + 1) * H * VH]
+
+    by_sevens(gather)
 
     def emit(r, rows, lanes, total, carried):
-        if carried is None:
-            carried = (wide_ref[rows, lanes], None)
-        wide, sums = carried
         far = pl.ds(base + lanes.start, lanes.size)
         term = total * mixed[r, rows, far].astype(F32)
-        pulled[r, rows, lanes] = (total * wide).astype(BF)
-        return (wide, term if sums is None else sums + term)
+        pulled[r, rows, lanes] = total.astype(BF)
+        return term if carried is None else carried + term
 
     def finish(rows, lanes, carried):
-        total_ref[rows, lanes] = carried[1]
+        total_ref[rows, lanes] = carried
 
     turn(table, incoming, base, range(LMAX + 1), emit, finish)
     sums = head_sum(total_ref[...])
     dalpha[...] = sums
-    here = dot(shares * sums, target_hit32, 1, 1, exact=True)
+    pulled0[...] = table[0, 0:1, base : base + edges] * incoming[0].astype(F32)
     if second:
-        dots[...] = jnp.concatenate([before[...], here], axis=1)
-    else:
-        dots[...] = here
-    pulled0[...] = table[0, 0:1, base : base + edges] * incoming[0].astype(F32) * wide_ref[...]
-    if not second:
-        scale = jnp.transpose(spread(factor))
-
-        def normalize(k):
-            for p in range(chips):
-                parts[p][k] = (raw[p][k] * scale[p * nodes : (p + 1) * nodes]).astype(BF)
-
-        each_k(normalize)
+        every = share[...] * jnp.concatenate([before[...], sums], axis=1)
+        target_hit32 = hits(pack[1:2], dots.shape[1], F32)
+        dots[...] = dot(every, target_hit32, 1, 1, exact=True)
 
 
 def back_kernel(chips, *refs):
     parts = refs[:chips]
     cots = refs[chips : 2 * chips]
-    (feats_own, feats_sib, pulled_a, pulled_b, scaled, gating, table, pack, w_mix) = refs[
-        2 * chips : 2 * chips + 9
+    (feats_own, feats_sib, pulled_a, pulled_b, share, scaled, gating, table, pack, w_mix) = refs[
+        2 * chips : 2 * chips + 10
     ]
-    (gate_sum, dv_own, dv_sib, g_mix, g_value, g_out) = refs[2 * chips + 9 : 2 * chips + 15]
-    turned, spread_back = refs[2 * chips + 15 :]
+    (gate_sum, dv_own, dv_sib, g_mix, g_value, g_out) = refs[2 * chips + 10 : 2 * chips + 16]
+    turned, spread_back = refs[2 * chips + 16 :]
     nodes = feats_own.shape[1]
     wide = H * VH
     gate = gating[...]
     zero = w_mix[0]
+    shares = spread(share[...])
     gates = jnp.zeros_like(gate)
     grad = jnp.zeros((wide, wide), F32)
 
     def pulled(r):
-        return jnp.concatenate([pulled_a[r], pulled_b[r]], axis=1)
+        whole = jnp.concatenate([pulled_a[r], pulled_b[r]], axis=1)
+        return (whole.astype(F32) * shares).astype(BF)
 
     for r in range(1, LMAX + 1):
         here = scaled[r]
@@ -418,14 +431,14 @@
     dots = refs[:chips]
     firsts = refs[chips : 2 * chips]
     refs = refs[2 * chips :]
-    feat0_sib = refs[0]
-    dalphas, shares, pulled0s = refs[1:3], refs[3:5], refs[5:7]
-    query, mixed, scaled, gating, table, gate_sum, radial, pack, w_zero = refs[7:16]
-    g_mix, g_value, g_out = refs[16:19]
-    keep, send, dv_own = refs[19:22]
-    dqs = refs[22 : 22 + chips]
-    (grads,) = refs[22 + chips :]
-    nodes = feat0_sib.shape[0]
+    feats_sib = refs[0]
+    dalphas, share, pulled0s = refs[1:3], refs[3], refs[4:6]
+    query, mixed, scaled, gating, table, gate_sum, radial, pack, w_mix = refs[6:15]
+    g_mix, g_value, g_out = refs[15:18]
+    keep, send, dv_own = refs[18:21]
+    dqs = refs[21 : 21 + chips]
+    (grads,) = refs[21 + chips :]
+    nodes = feats_sib.shape[1]
     targets = chips * nodes
     wide = H * VH
     target_hit = hits(pack[1:2], targets, F32)
@@ -436,12 +449,13 @@
     total = dots[0][...]
     for p in range(1, chips):
         total = total + jnp.concatenate(whole_order(dots[p], chips, p, nodes), axis=1)
-    dscore = both(shares) * (both(dalphas) - dot(total, target_hit, exact=True))
+    dscore = share[...] * (both(dalphas) - dot(total, target_hit, exact=True))
     dlogit = spread(dscore) * (1.0 / VH**0.5)
-    down = (both(pulled0s) + dlogit * query[...]).astype(BF)
+    pulled0 = both(pulled0s) * spread(share[...])
+    down = (pulled0 + dlogit * query[...]).astype(BF)
     here = scaled[0]
     gate = gating[...]
-    out = dot(w_zero[...], down)
+    out = dot(w_mix[0], down)
     dgate = ((gate_sum[...] + out * here.astype(F32)) * (1.0 - gate)).astype(BF)
     back = (table[0, 0:1, :] * (out * gate).astype(BF).astype(F32)).astype(BF)
     source_hit = hits(pack[0:1], 2 * nodes, BF)
@@ -453,7 +467,7 @@
         dqs[p][:nodes] = some.astype(BF)
         dqs[p][nodes:] = (some - some.astype(BF).astype(F32)).astype(BF)
     first = rows_of([f[...] for f in firsts])
-    node0 = rows_of([firsts[0][...], feat0_sib[...]])
+    node0 = rows_of([firsts[0][...], feats_sib[0]])
     pieces = [g_value[...] + dot(node0, dv, 0, 0), dot(first, dq.astype(BF), 0, 0), g_out[...]]
     pieces += [g_mix[0] + dot(here, down, 1, 1)]
     pieces += [g_mix[i] for i in range(1, 2 * MMAX + 1)]
@@ -562,6 +576,9 @@
     if far:
         buffers += [pltpu.VMEM(a.shape, a.dtype) for a in args[smem : smem + far]]
         buffers += [pltpu.SemaphoreType.DMA((far,))]
+    args = list(args)
+    for i in range(smem, smem + far):
+        args[i] = pltpu.with_memory_space_constraint(args[i], pltpu.HBM)
     return pl.pallas_call(
         kernel,
         out_shape=[jax.ShapeDtypeStruct(s, d) for s, d in outs],
@@ -622,35 +639,30 @@
     def direct(a):
         return [a] + [along(a, step) for step in range(1, chips)]
 
-    def doubled(a):
-        have = {0: a}
-        step = chips // 2
-        while step:
-            for p in list(have):
-                have[p ^ step] = along(have[p], step)
-            step //= 2
-        return [have[p] for p in range(chips)]
-
-    owner = targets // nodes
     line = lax.broadcasted_iota(jnp.int32, (16, slots), 0)
-    ids = jnp.where(line == 0, sources - rank * nodes, 0)
-    ids = jnp.where(line == 1, targets - owner * nodes, ids)
-    ids = jnp.where(line == 2, bins, ids)
-    ids = jnp.where(line == 3, live_mask, ids)
-    ids = jnp.where(line == 4, (owner // 2) ^ chip, ids)
-    pack_own = ids.astype(F32) + jnp.pad(bias.astype(F32), ((8, 0), (0, 0)))
-    cots = doubled(cot)
+    ids = jnp.where(line < 2, jnp.where(line == 0, sources, targets), jnp.where(line == 2, bins, live_mask))
+    pack_own = jnp.where(
+        line < 4, ids.astype(F32), jnp.pad(bias.astype(F32), ((8, 0), (0, 0)))
+    )
+    have = {0: cot}
+    step = some
+    while step > 1:
+        for p in list(have):
+            have[p ^ step] = along(have[p], step)
+        step //= 2
+    neighbour = along(cot, 1)
     pack_sib = other_core(pack_own)
     radial_sib = other_core(radial[0])
     feats_sib = other_core(feats)
     firsts = direct(feats[0])
+    radial_sib, firsts = lax.optimization_barrier((radial_sib, firsts))
 
     edge_f32 = ((wide, slots), F32)
     half_f32 = ((wide, slots // 2), F32)
     block = ((K, nodes, wide), BF)
-    table, scaled, mixed, gating, pack, radial_here, weight, stats, query, *raw = call(
+    table, scaled, mixed, gating, pack, radial_here = call(
         "forward",
-        15,
+        9,
         functools.partial(forward_kernel, chips),
         [
             where,
@@ -660,12 +672,10 @@
             feats,
             w_value,
             w_mix,
-            w_query,
             pack_own,
             pack_sib,
             radial_sib,
             feats_sib,
-            *firsts,
         ],
         [
             ((R, 56, slots), F32),
@@ -674,42 +684,57 @@
             edge_f32,
             ((16, slots), F32),
             ((slots, radial.shape[2]), BF),
+        ],
+        [((K, wide, slots), BF)],
+        smem=1,
+        far=6,
+        limit=32,
+    )
+    weight, stats, query, *raw = call(
+        "attend",
+        1,
+        functools.partial(attend_kernel, chips),
+        [w_query, *firsts, pack, table, mixed],
+        [
             ((H, slots), F32),
             ((2 * H, spot), F32),
             edge_f32,
             *([((K, nodes, wide), F32)] * chips),
         ],
-        [((K, wide, slots), BF), ((R, wide, slots), BF), ((K, wide, slots), BF)],
-        smem=1,
-        far=7,
-        limit=32,
-    )
+        [((R, wide, slots), BF), ((K, wide, slots), BF)],
+        far=1,
+    )
+    del have[0]
+    stats, have = lax.optimization_barrier((stats, have))
+    have[0] = cot
+    have.update({p ^ 1: along(a, 1) if p else neighbour for p, a in have.items()})
+    cots = [have[p] for p in range(chips)]
     all_stats = direct(stats)
 
-    def pull(second, extra):
+    def pull(second, extra, sums):
         mine = slice(some, chips) if second else slice(0, some)
         return call(
-        "pull",
-        4.5,
+            "pull",
+            4 if second else 1,
             functools.partial(pull_kernel, chips, second),
-            [*all_stats, *cots[mine], *extra, w_out, pack, weight, table, mixed],
-            [
-                ((R, wide, slots // 2), BF),
-                half_f32,
-                ((H, slots // 2), F32),
-                ((H, slots // 2), F32),
-                ((H, spot if second else spot // 2), F32),
-                *([] if second else [block] * chips),
-            ],
-            [((K, wide, slots // 2), BF), half_f32, half_f32],
+            [*cots[mine], w_out, pack, table, mixed, *extra],
+            [((R, wide, slots // 2), BF), half_f32, ((H, slots // 2), F32), *sums],
+            [((K, wide, slots // 2), BF), half_f32],
         )
 
-    pulled_a, pulled0_a, dalpha_a, share_a, dots_a, *parts = pull(False, raw)
+    pulled_a, pulled0_a, dalpha_a = pull(False, [], [])
+    share, *parts = call(
+        "share",
+        0.3,
+        functools.partial(share_kernel, chips),
+        [*all_stats, *raw, weight, pack],
+        [((H, slots), F32), *([block] * chips)],
+    )
 
     parts, cots[-1] = lax.optimization_barrier((parts, cots[-1]))
     pending = {p: [parts[p]] for p in range(chips)}
-    near = {p: along(parts[p], 1) for p in range(chips) if p & 1}
-    pulled_b, pulled0_b, dalpha_b, share_b, dots = pull(True, [dots_a])
+    near = {p: along(parts[p], 1) for p in range(chips) if p & 1 and p > 1}
+    pulled_b, pulled0_b, dalpha_b, dots = pull(True, [dalpha_a, share], [((H, spot), F32)])
     all_dots = direct(dots)
     for p, got in near.items():
         del pending[p]
@@ -718,7 +743,9 @@
     for p in pending:
         if p:
             (summed[p],) = call("add", 1, add_kernel, pending[p], [block])
-    summed, pulled_b = lax.optimization_barrier((summed, pulled_b))
+    pulled_b, summed, last = lax.optimization_barrier((pulled_b, summed, parts[1]))
+    del pending[1]
+    pending[0].append(along(last, 1))
     step = 2
     while step < chips:
         for p in [p for p in summed if p & step]:
@@ -732,7 +759,20 @@
         "back",
         7.5,
         functools.partial(back_kernel, chips),
-        [*parts, *cots, feats, feats_sib, pulled_a, pulled_b, scaled, gating, table, pack, w_mix],
+        [
+            *parts,
+            *cots,
+            feats,
+            feats_sib,
+            pulled_a,
+            pulled_b,
+            share,
+            scaled,
+            gating,
+            table,
+            pack,
+            w_mix,
+        ],
         [edge_f32, block, block, (w_mix.shape, F32), ((wide, wide), F32), ((wide, wide), F32)],
         [((R, wide, slots), BF), ((K, wide, slots), BF)],
         limit=32,
@@ -750,11 +790,10 @@
             where_sum,
             *all_dots,
             *firsts,
-            feats_sib[0],
+            feats_sib,
             dalpha_a,
             dalpha_b,
-            share_a,
-            share_b,
+            share,
             pulled0_a,
             pulled0_b,
             query,
@@ -765,7 +804,7 @@
             gate_sum,
             radial_here,
             pack,
-            w_mix[0],
+            w_mix,
             g_mix,
             g_value,
             g_out,
@@ -791,7 +830,7 @@
         smem=1,
     )
     got = [beside(sends[step - 1], step) for step in range(1, planes)]
-    got, pending[0][1] = lax.optimization_barrier((got, pending[0][1]))
+    got, pending[0] = lax.optimization_barrier((got, pending[0]))
     letters = call(
         "address",
         0.6,
@@ -800,9 +839,9 @@
         [((cut + 2 * nodes, wide), BF)] * chips,
     )
     terms = [letters[0]] + [along(letters[step], step) for step in range(1, chips)]
-    terms, pending[0] = lax.optimization_barrier((terms, pending[0]))
+    (updated,) = call("update", 2, update_kernel, [*pending[0], feats, w_out], [block])
+    terms, updated = lax.optimization_barrier((terms, updated))
     piece, dquery = call("settle", 0.6, settle_kernel, terms, [((cut, wide), BF), small])
-    (updated,) = call("update", 2, update_kernel, [*pending[0], feats, w_out], [block])
     mine = [piece] + [beside(piece, step) for step in range(1, planes)]
     theirs = [other_core(a) for a in mine]
     grads = call(

time: 110 us -> 95.5 us (0.87)
  local copies, waits for them, and re-layouts: 7.87 us -> 0.73 us
  waiting for transfers between devices: 23.4 us -> 19.2 us
  other arithmetic: 3.02 us -> 0.99 us
    ppermute x18, waiting for transfers between devices: 17.3 us -> 10.7 us  [along(): return lax.ppermute(a, 'graph', [(i, i ^ 2 * step) for i in range(ranks)])]
    unnamed x26 -> x12, local copies, waits for them, and re-layouts: 6.41 us -> 0.03 us
    sub x2 -> x0, other arithmetic: 1.37 us -> none  [the longest x1 0.68 us: shards(): ids = jnp.where(line == 1, targets - owner * nodes, ids)]
    ppermute x6, waiting for transfers between devices: 5.77 us -> 7.04 us  [beside(): return lax.ppermute(a, 'dp', [(i, i ^ step) for i in range(planes)])]
    ppermute x9, waiting for transfers between devices: 0.33 us -> 1.46 us  [other_core(): return lax.ppermute(a, 'graph', [(i, i ^ 1) for i in range(ranks)])]
    pallas_call x12 -> x14, Pallas kernels: 40.2 us -> 40.5 us  [call(): pl.pallas_call(kernel, out_shape=[jax.ShapeDtypeStruct(s, d) for s, d in...]
  transfers between devices with their start and end apart: 33 -> 33, of which waited for: 11 -> 15; matrix products, arithmetic and copies ran while one was open for 3% -> 1% of each run, Pallas kernels for 35% -> 41%
where the time goes in v2:
time: 95.5 us; the launch traced here: 95.2 us
  Pallas kernels  40.5 us (42%)
  starting transfers between devices  33 us (35%)
  waiting for transfers between devices  19.2 us (20%)
  other arithmetic  0.99 us (1%)
    pallas_call x14, Pallas kernels, call(): pl.pallas_call(kernel, out_shape=[jax.ShapeDtypeStruct(s, d) for s, d in...  40.5 us
    ppermute x18, starting transfers between devices, along(): return lax.ppermute(a, 'graph', [(i, i ^ 2 * step) for i in range(ranks)])  25.2 us
    ppermute x18, waiting for transfers between devices, along(): return lax.ppermute(a, 'graph', [(i, i ^ 2 * step) for i in range(ranks)])  10.7 us
    ppermute x6, starting transfers between devices, beside(): return lax.ppermute(a, 'dp', [(i, i ^ step) for i in range(planes)])  7.11 us
    ppermute x6, waiting for transfers between devices, beside(): return lax.ppermute(a, 'dp', [(i, i ^ step) for i in range(planes)])  7.04 us
  transfers between devices with their start and end apart: 33, of which 15 were waited for; matrix products, arithmetic and copies ran while one was open for 1% of the time, Pallas kernels for 41%

profile of v2, /device:TPU:0, one launch (start us, length us, event | category | flops | bytes accessed | tf_op | source)
XLA Modules:
  0.0 95.2 jit_solution(4245837440108271587)
XLA Ops:
  1.3 3.0 %collective-permute-start.1 = (bf16[32,128]{1,0:T(8,128)(2,1)S(1)}, bf16[32,128]{1,0:T(8,128)(2,1)S(1)}, u32[]{:S(2)}, u32[]{:S(2)}) collective-permute-start(bf16[32,128]{1,0:T(8,128)(2,1)S(1)} %slice_bitcast_fusion.refs_1_.refs_4_), channel_id=1, source_target_pairs={{0,2},{1,3},{2,0},{3,1},{4,6},{5,7},{6,4},{7,5},{8,10},{9,11},{10,... | collective-permute-start | bytes 24584 | tf_op jit(solution)/shard_map/ppermute | solution.py:634
  4.4 2.6 %collective-permute-start.2 = (bf16[32,128]{1,0:T(8,128)(2,1)S(1)}, bf16[32,128]{1,0:T(8,128)(2,1)S(1)}, u32[]{:S(2)}, u32[]{:S(2)}) collective-permute-start(bf16[32,128]{1,0:T(8,128)(2,1)S(1)} %slice_bitcast_fusion.refs_1_.refs_4_), channel_id=1, source_target_pairs={{0,4},{1,5},{2,6},{3,7},{4,0},{5,1},{6,2},{7,3},{8,12},{9,13},{10,... | collective-permute-start | bytes 24584 | tf_op jit(solution)/shard_map/ppermute | solution.py:634
  8.9 2.6 %collective-permute-start.6 = (bf16[49,32,128]{2,1,0:T(8,128)(2,1)}, bf16[49,32,128]{2,1,0:T(8,128)(2,1)S(1)}, u32[]{:S(2)}, u32[]{:S(2)}) collective-permute-start(bf16[49,32,128]{2,1,0:T(8,128)(2,1)} %bitcast.26), channel_id=1, source_target_pairs={{0,4},{1,5},{2,6},{3,7},{4,0},{5,1},{6,2},{7,3},{8,12},{9,13},{10,... | collective-permute-start | bytes 1204232 | tf_op jit(solution)/shard_map/ppermute | solution.py:634
  12.9 8.9 %forward.1 = (f32[29,56,256]{2,1,0:T(8,128)S(1)}, bf16[29,128,256]{2,1,0:T(8,128)(2,1)S(1)}, bf16[29,128,256]{2,1,0:T(8,128)(2,1)S(1)}, f32[128,256]{1,0:T(8,128...) custom-call(s32[3]{0:T(128)S(1)} %pad_add_fusion.1.where, bf16[256,512]{1,0:T(8,128)(2,1)} %bitcast.43, ...), custom_call_target="tpu_custom_call" | custom-call | flops 10350000128 | bytes 1000 | tf_op jit(solution)/shard_map/forward/pallas_call | solution.py:582
  21.8 6.8 %attend.1 = (f32[8,256]{1,0:T(8,128)S(1)}, f32[16,128]{1,0:T(8,128)S(1)}, f32[128,256]{1,0:T(8,128)S(1)}, f32[49,32,128]{2,1,0:T(8,128)S(1)}, f32[49,32,128]{2,1...) custom-call(bf16[128,128]{1,0:T(8,128)(2,1)} %w_query.1, ...), custom_call_target="tpu_custom_call" | custom-call | flops 1150000000 | bytes 1000 | tf_op jit(solution)/shard_map/attend/pallas_call | solution.py:582
  30.3 1.7 %collective-permute-start.7 = (f32[16,128]{1,0:T(8,128)S(1)}, f32[16,128]{1,0:T(8,128)S(1)}, u32[]{:S(2)}, u32[]{:S(2)}) collective-permute-start(f32[16,128]{1,0:T(8,128)S(1)} %get-tuple-element.97.refs_0_), channel_id=1, source_target_pairs={{0,2},{1,3},{2,0},{3,1},{4,6},{5,7},{6,4},{7,5},{8,10},{9,11},{10,... | collective-permute-start | bytes 24584 | tf_op jit(solution)/shard_map/ppermute | solution.py:634
  34.9 3.8 %pull.2 = (bf16[29,128,128]{2,1,0:T(8,128)(2,1)S(1)}, f32[128,128]{1,0:T(8,128)S(1)}, f32[8,128]{1,0:T(8,128)S(1)}) custom-call(bf16[49,32,128]{2,1,0:T(8,128)(2,1)S(1)} %bitcast.28, bf16[49,32,128]{2,1,0:T(8,128)(2,1)S(1)} %collective-permute-done.11.refs_1_.refs_5_, bf16[128,128]{1,0:T(8,128)(2,1)S(1)} %copy-done.1, ...), custom_call_target="tpu_custom_call" | custom-call | flops 1150000000 | bytes 1000 | tf_op jit(solution)/shard_map/pull/pallas_call | solution.py:582
  38.7 1.9 %collective-permute-done.7.refs_1_ = f32[16,128]{1,0:T(8,128)S(1)} collective-permute-done((f32[16,128]{1,0:T(8,128)S(1)}, f32[16,128]{1,0:T(8,128)S(1)}, u32[]{:S(2)}, u32[]{:S(2)}) %collective-permute-start.7) | collective-permute-done | bytes 8224 | tf_op jit(solution)/shard_map/ppermute | solution.py:634
  40.7 2.1 %collective-permute-done.9.refs_3_ = f32[16,128]{1,0:T(8,128)S(1)} collective-permute-done((f32[16,128]{1,0:T(8,128)S(1)}, f32[16,128]{1,0:T(8,128)S(1)}, u32[]{:S(2)}, u32[]{:S(2)}) %collective-permute-start.9) | collective-permute-done | bytes 8224 | tf_op jit(solution)/shard_map/ppermute | solution.py:634
  43.8 4.0 %pull.3 = (bf16[29,128,128]{2,1,0:T(8,128)(2,1)S(1)}, f32[128,128]{1,0:T(8,128)S(1)}, f32[8,128]{1,0:T(8,128)S(1)}, f32[8,128]{1,0:T(8,128)S(1)}) custom-call(bf16[49,32,128]{2,1,0:T(8,128)(2,1)S(1)} %collective-permute-done.6.refs_0_.refs_6_, bf16[49,32,128]{2,1,0:T(8,128)(2,1)S(1)} %collective-permute-done.10.refs_1_.refs_7_, ...), custom_call_target="tpu_custom_call" | custom-call | flops 4600000000 | bytes 1000 | tf_op jit(solution)/shard_map/pull/pallas_call | solution.py:582
  47.8 1.6 %collective-permute-start.12 = (f32[8,128]{1,0:T(8,128)S(1)}, f32[8,128]{1,0:T(8,128)S(1)}, u32[]{:S(2)}, u32[]{:S(2)}) collective-permute-start(f32[8,128]{1,0:T(8,128)S(1)} %get-tuple-element.110.refs_0_), channel_id=1, source_target_pairs={{0,2},{1,3},{2,0},{3,1},{4,6},{5,7},{6,4},{7,5},{8,10},{9,11},{10,... | collective-permute-start | bytes 12296 | tf_op jit(solution)/shard_map/ppermute | solution.py:634
  49.8 2.5 %collective-permute-start.14 = (f32[8,128]{1,0:T(8,128)S(1)}, f32[8,128]{1,0:T(8,128)S(1)}, u32[]{:S(2)}, u32[]{:S(2)}) collective-permute-start(f32[8,128]{1,0:T(8,128)S(1)} %get-tuple-element.110.refs_0_), channel_id=1, source_target_pairs={{0,6},{1,7},{2,4},{3,5},{4,2},{5,3},{6,0},{7,1},{8,14},{9,15},{10,... | collective-permute-start | bytes 12296 | tf_op jit(solution)/shard_map/ppermute | solution.py:634
  52.2 1.6 %collective-permute-done.15.refs_1_ = bf16[49,32,128]{2,1,0:T(8,128)(2,1)S(1)} collective-permute-done((bf16[49,32,128]{2,1,0:T(8,128)(2,1)S(1)}, bf16[49,32,128]{2,1,0:T(8,128)(2,1)S(1)}, u32[]{:S(2)}, u32[]{:S(2)}) %collective-permute-start.15) | collective-permute-done | bytes 401440 | tf_op jit(solution)/shard_map/ppermute | solution.py:634
  54.4 1.8 %collective-permute-start.21 = (bf16[49,32,128]{2,1,0:T(8,128)(2,1)S(1)}, bf16[49,32,128]{2,1,0:T(8,128)(2,1)S(1)}, u32[]{:S(2)}, u32[]{:S(2)}) collective-permute-start(bf16[49,32,128]{2,1,0:T(8,128)(2,1)S(1)} %add.16), channel_id=1, source_target_pairs={{0,4},{1,5},{2,6},{3,7},{4,0},{5,1},{6,2},{7,3},{8,12},{9,13},{10,... | collective-permute-start | bytes 1204232 | tf_op jit(solution)/shard_map/ppermute | solution.py:634
  56.2 7.8 %back.1 = (f32[128,256]{1,0:T(8,128)S(1)}, bf16[49,32,128]{2,1,0:T(8,128)(2,1)S(1)}, bf16[49,32,128]{2,1,0:T(8,128)(2,1)S(1)}, f32[5,128,128]{2,1,0:T(8,128)S(1)...) custom-call(bf16[49,32,128]{2,1,0:T(8,128)(2,1)S(1)} %get-tuple-element.148.refs_0_, ...), custom_call_target="tpu_custom_call" | custom-call | flops 8625000448 | bytes 1000 | tf_op jit(solution)/shard_map/back/pallas_call | solution.py:582
  64.0 1.8 %tail.1 = (f32[768,128]{1,0:T(8,128)S(1)}, bf16[800,128]{1,0:T(8,128)(2,1)S(1)}, bf16[32,128]{1,0:T(8,128)(2,1)S(1)}, bf16[64,128]{1,0:T(8,128)(2,1)S(1)}, bf16[...) custom-call(s32[2]{0:T(128)S(1)} %pad_add_fusion.where, ...), custom_call_target="tpu_custom_call" | custom-call | flops 2070000000 | bytes 1000 | tf_op jit(solution)/shard_map/tail/pallas_call | solution.py:582
  67.9 1.6 %collective-permute-start.17 = (bf16[192,128]{1,0:T(8,128)(2,1)S(1)}, bf16[192,128]{1,0:T(8,128)(2,1)S(1)}, u32[]{:S(2)}, u32[]{:S(2)}) collective-permute-start(bf16[192,128]{1,0:T(8,128)(2,1)S(1)} %get-tuple-element.132), channel_id=1, source_target_pairs={{0,8},{8,0},{16,24},{24,16},{1,9},{9,1},{17,25},{25,17},{2,10},{10... | collective-permute-start | bytes 147464 | tf_op jit(solution)/shard_map/ppermute | solution.py:637
  73.6 2.4 %collective-permute-done.19.refs_2_ = bf16[192,128]{1,0:T(8,128)(2,1)S(1)} collective-permute-done((bf16[192,128]{1,0:T(8,128)(2,1)S(1)}, bf16[192,128]{1,0:T(8,128)(2,1)S(1)}, u32[]{:S(2)}, u32[]{:S(2)}) %collective-permute-start.19) | collective-permute-done | bytes 49184 | tf_op jit(solution)/shard_map/ppermute | solution.py:637
  76.4 2.4 %collective-permute-start.23 = (bf16[256,128]{1,0:T(8,128)(2,1)S(1)}, bf16[256,128]{1,0:T(8,128)(2,1)S(1)}, u32[]{:S(2)}, u32[]{:S(2)}) collective-permute-start(bf16[256,128]{1,0:T(8,128)(2,1)S(1)} %get-tuple-element.146), channel_id=1, source_target_pairs={{0,4},{1,5},{2,6},{3,7},{4,0},{5,1},{6,2},{7,3},{8,12},{9,13},{10,... | collective-permute-start | bytes 196616 | tf_op jit(solution)/shard_map/ppermute | solution.py:634
  78.9 1.6 %collective-permute-start.24 = (bf16[256,128]{1,0:T(8,128)(2,1)S(1)}, bf16[256,128]{1,0:T(8,128)(2,1)S(1)}, u32[]{:S(2)}, u32[]{:S(2)}) collective-permute-start(bf16[256,128]{1,0:T(8,128)(2,1)S(1)} %get-tuple-element.147), channel_id=1, source_target_pairs={{0,6},{1,7},{2,4},{3,5},{4,2},{5,3},{6,0},{7,1},{8,14},{9,15},{10,... | collective-permute-start | bytes 196616 | tf_op jit(solution)/shard_map/ppermute | solution.py:634
  80.5 2.1 %update.1 = bf16[49,32,128]{2,1,0:T(8,128)(2,1)} custom-call(bf16[49,32,128]{2,1,0:T(8,128)(2,1)S(1)} %get-tuple-element.148.refs_0_, bf16[49,32,128]{2,1,0:T(8,128)(2,1)S(1)} %collective-permute-done.20.refs_1_, bf16[49,32,128]{2,1,0:T(8,128)(2,1)S(1)} %collective-permute-done.21.refs_2_, bf16[49,32,128]{2,1,0:T(8,128)(2,1)S(1)} %bitcast.35, ...), custom_call_target="tpu_custom_call" | custom-call | flops 2300000000 | bytes 1000 | tf_op jit(solution)/shard_map/update/pallas_call | solution.py:582
  83.0 1.9 %collective-permute-done.24.refs_3_ = bf16[256,128]{1,0:T(8,128)(2,1)S(1)} collective-permute-done((bf16[256,128]{1,0:T(8,128)(2,1)S(1)}, bf16[256,128]{1,0:T(8,128)(2,1)S(1)}, u32[]{:S(2)}, u32[]{:S(2)}) %collective-permute-start.24) | collective-permute-done | bytes 65568 | tf_op jit(solution)/shard_map/ppermute | solution.py:634
  86.1 2.4 %collective-permute-start.28 = (bf16[192,128]{1,0:T(8,128)(2,1)S(1)}, bf16[192,128]{1,0:T(8,128)(2,1)S(1)}, u32[]{:S(2)}, u32[]{:S(2)}) collective-permute-start(bf16[192,128]{1,0:T(8,128)(2,1)S(1)} %get-tuple-element.161.refs_0_), channel_id=1, source_target_pairs={{0,24},{8,16},{16,8},{24,0},{1,25},{9,17},{17,9},{25,1},{2,26},{10... | collective-permute-start | bytes 147464 | tf_op jit(solution)/shard_map/ppermute | solution.py:637
  91.1 2.6 %nodes.1 = bf16[49,32,128]{2,1,0:T(8,128)(2,1)} custom-call(bf16[32,128]{1,0:T(8,128)(2,1)S(1)} %get-tuple-element.156.dquery, bf16[49,32,128]{2,1,0:T(8,128)(2,1)S(1)} %get-tuple-element.157.dv_own, bf16[49,32,128]{2,1,0:T(8,128)(2,1)S(1)} %collective-permute-done.25.dv_sib, bf16[32,128]{1,0:T(8,128)(2,1)S(1)} %get-tuple-element.159.dv0_own, ...), custom_call_target="tpu_custom_call" | custom-call | flops 2990000128 | bytes 1000 | tf_op jit(solution)/shard_map/nodes/pallas_call | solution.py:582
  (74 shorter events, 22.8 us)
Async XLA Ops:
  1.3 7.0 %collective-permute-start.1 = (bf16[32,128]{1,0:T(8,128)(2,1)S(1)}, bf16[32,128]{1,0:T(8,128)(2,1)S(1)}, u32[]{:S(2)}, u32[]{:S(2)}) collective-permute-start(bf16[32,128]{1,0:T(8,128)(2,1)S(1)} %slice_bitcast_fusion.refs_1_.refs_4_), channel_id=1, source_target_pairs={{0,2},{1,3},{2,0},{3,1},{4,6},{5,7},{6,4},{7,5},{8,10},{9,11},{10,... | collective-permute-start | bytes 24584 | tf_op jit(solution)/shard_map/ppermute | solution.py:634
  6.9 5.4 %collective-permute-start.3 = (bf16[32,128]{1,0:T(8,128)(2,1)S(1)}, bf16[32,128]{1,0:T(8,128)(2,1)S(1)}, u32[]{:S(2)}, u32[]{:S(2)}) collective-permute-start(bf16[32,128]{1,0:T(8,128)(2,1)S(1)} %slice_bitcast_fusion.refs_1_.refs_4_), channel_id=1, source_target_pairs={{0,6},{1,7},{2,4},{3,5},{4,2},{5,3},{6,0},{7,1},{8,14},{9,15},{10,... | collective-permute-start | bytes 24584 | tf_op jit(solution)/shard_map/ppermute | solution.py:634
  6.9 5.9 %collective-permute-start.5 = (bf16[49,32,128]{2,1,0:T(8,128)(2,1)}, bf16[49,32,128]{2,1,0:T(8,128)(2,1)S(1)}, u32[]{:S(2)}, u32[]{:S(2)}) collective-permute-start(bf16[49,32,128]{2,1,0:T(8,128)(2,1)} %bitcast.32), channel_id=1, source_target_pairs={{0,1},{1,0},{2,3},{3,2},{4,5},{5,4},{6,7},{7,6},{8,9},{9,8},{10,11... | collective-permute-start | bytes 1204232 | tf_op jit(solution)/shard_map/ppermute | solution.py:631
  7.0 5.9 %collective-permute-start = (bf16[256,512]{1,0:T(8,128)(2,1)}, bf16[256,512]{1,0:T(8,128)(2,1)S(1)}, u32[]{:S(2)}, u32[]{:S(2)}) collective-permute-start(bf16[256,512]{1,0:T(8,128)(2,1)} %bitcast.42), channel_id=1, source_target_pairs={{0,1},{1,0},{2,3},{3,2},{4,5},{5,4},{6,7},{7,6},{8,9},{9,8},{10,11... | collective-permute-start | bytes 786440 | tf_op jit(solution)/shard_map/ppermute | solution.py:631
  8.9 21.1 %collective-permute-start.6 = (bf16[49,32,128]{2,1,0:T(8,128)(2,1)}, bf16[49,32,128]{2,1,0:T(8,128)(2,1)S(1)}, u32[]{:S(2)}, u32[]{:S(2)}) collective-permute-start(bf16[49,32,128]{2,1,0:T(8,128)(2,1)} %bitcast.26), channel_id=1, source_target_pairs={{0,4},{1,5},{2,6},{3,7},{4,0},{5,1},{6,2},{7,3},{8,12},{9,13},{10,... | collective-permute-start | bytes 1204232 | tf_op jit(solution)/shard_map/ppermute | solution.py:634
  12.4 22.5 %collective-permute-start.11 = (bf16[49,32,128]{2,1,0:T(8,128)(2,1)}, bf16[49,32,128]{2,1,0:T(8,128)(2,1)S(1)}, u32[]{:S(2)}, u32[]{:S(2)}) collective-permute-start(bf16[49,32,128]{2,1,0:T(8,128)(2,1)} %bitcast.27), channel_id=1, source_target_pairs={{0,2},{1,3},{2,0},{3,1},{4,6},{5,7},{6,4},{7,5},{8,10},{9,11},{10,... | collective-permute-start | bytes 1204232 | tf_op jit(solution)/shard_map/ppermute | solution.py:634
  30.0 13.2 %collective-permute-start.10 = (bf16[49,32,128]{2,1,0:T(8,128)(2,1)S(1)}, bf16[49,32,128]{2,1,0:T(8,128)(2,1)S(1)}, u32[]{:S(2)}, u32[]{:S(2)}) collective-permute-start(bf16[49,32,128]{2,1,0:T(8,128)(2,1)S(1)} %collective-permute-done.6.refs_0_.refs_6_), channel_id=1, source_target_pairs={{0,2},{1,3},{2,0},{3,1},{4,6},{5,7},{6,4},{7,5},{8,10},{9,11},{10,... | collective-permute-start | bytes 1204232 | tf_op jit(solution)/shard_map/ppermute | solution.py:634
  30.3 10.4 %collective-permute-start.7 = (f32[16,128]{1,0:T(8,128)S(1)}, f32[16,128]{1,0:T(8,128)S(1)}, u32[]{:S(2)}, u32[]{:S(2)}) collective-permute-start(f32[16,128]{1,0:T(8,128)S(1)} %get-tuple-element.97.refs_0_), channel_id=1, source_target_pairs={{0,2},{1,3},{2,0},{3,1},{4,6},{5,7},{6,4},{7,5},{8,10},{9,11},{10,... | collective-permute-start | bytes 24584 | tf_op jit(solution)/shard_map/ppermute | solution.py:634
  32.1 8.6 %collective-permute-start.8 = (f32[16,128]{1,0:T(8,128)S(1)}, f32[16,128]{1,0:T(8,128)S(1)}, u32[]{:S(2)}, u32[]{:S(2)}) collective-permute-start(f32[16,128]{1,0:T(8,128)S(1)} %get-tuple-element.97.refs_0_), channel_id=1, source_target_pairs={{0,4},{1,5},{2,6},{3,7},{4,0},{5,1},{6,2},{7,3},{8,12},{9,13},{10,... | collective-permute-start | bytes 24584 | tf_op jit(solution)/shard_map/ppermute | solution.py:634
  33.5 9.3 %collective-permute-start.9 = (f32[16,128]{1,0:T(8,128)S(1)}, f32[16,128]{1,0:T(8,128)S(1)}, u32[]{:S(2)}, u32[]{:S(2)}) collective-permute-start(f32[16,128]{1,0:T(8,128)S(1)} %get-tuple-element.97.refs_0_), channel_id=1, source_target_pairs={{0,6},{1,7},{2,4},{3,5},{4,2},{5,3},{6,0},{7,1},{8,14},{9,15},{10,... | collective-permute-start | bytes 24584 | tf_op jit(solution)/shard_map/ppermute | solution.py:634
  43.2 10.6 %collective-permute-start.15 = (bf16[49,32,128]{2,1,0:T(8,128)(2,1)S(1)}, bf16[49,32,128]{2,1,0:T(8,128)(2,1)S(1)}, u32[]{:S(2)}, u32[]{:S(2)}) collective-permute-start(bf16[49,32,128]{2,1,0:T(8,128)(2,1)S(1)} %get-tuple-element.120.refs_3_), channel_id=1, source_target_pairs={{0,2},{1,3},{2,0},{3,1},{4,6},{5,7},{6,4},{7,5},{8,10},{9,11},{10,... | collective-permute-start | bytes 1204232 | tf_op jit(solution)/shard_map/ppermute | solution.py:634
  47.8 16.2 %collective-permute-start.12 = (f32[8,128]{1,0:T(8,128)S(1)}, f32[8,128]{1,0:T(8,128)S(1)}, u32[]{:S(2)}, u32[]{:S(2)}) collective-permute-start(f32[8,128]{1,0:T(8,128)S(1)} %get-tuple-element.110.refs_0_), channel_id=1, source_target_pairs={{0,2},{1,3},{2,0},{3,1},{4,6},{5,7},{6,4},{7,5},{8,10},{9,11},{10,... | collective-permute-start | bytes 12296 | tf_op jit(solution)/shard_map/ppermute | solution.py:634
  49.4 14.6 %collective-permute-start.13 = (f32[8,128]{1,0:T(8,128)S(1)}, f32[8,128]{1,0:T(8,128)S(1)}, u32[]{:S(2)}, u32[]{:S(2)}) collective-permute-start(f32[8,128]{1,0:T(8,128)S(1)} %get-tuple-element.110.refs_0_), channel_id=1, source_target_pairs={{0,4},{1,5},{2,6},{3,7},{4,0},{5,1},{6,2},{7,3},{8,12},{9,13},{10,... | collective-permute-start | bytes 12296 | tf_op jit(solution)/shard_map/ppermute | solution.py:634
  49.8 14.2 %collective-permute-start.14 = (f32[8,128]{1,0:T(8,128)S(1)}, f32[8,128]{1,0:T(8,128)S(1)}, u32[]{:S(2)}, u32[]{:S(2)}) collective-permute-start(f32[8,128]{1,0:T(8,128)S(1)} %get-tuple-element.110.refs_0_), channel_id=1, source_target_pairs={{0,6},{1,7},{2,4},{3,5},{4,2},{5,3},{6,0},{7,1},{8,14},{9,15},{10,... | collective-permute-start | bytes 12296 | tf_op jit(solution)/shard_map/ppermute | solution.py:634
  54.0 22.1 %collective-permute-start.20 = (bf16[49,32,128]{2,1,0:T(8,128)(2,1)S(1)}, bf16[49,32,128]{2,1,0:T(8,128)(2,1)S(1)}, u32[]{:S(2)}, u32[]{:S(2)}) collective-permute-start(bf16[49,32,128]{2,1,0:T(8,128)(2,1)S(1)} %get-tuple-element.135.refs_1_), channel_id=1, source_target_pairs={{0,2},{1,3},{2,0},{3,1},{4,6},{5,7},{6,4},{7,5},{8,10},{9,11},{10,... | collective-permute-start | bytes 1204232 | tf_op jit(solution)/shard_map/ppermute | solution.py:634
  54.4 21.6 %collective-permute-start.21 = (bf16[49,32,128]{2,1,0:T(8,128)(2,1)S(1)}, bf16[49,32,128]{2,1,0:T(8,128)(2,1)S(1)}, u32[]{:S(2)}, u32[]{:S(2)}) collective-permute-start(bf16[49,32,128]{2,1,0:T(8,128)(2,1)S(1)} %add.16), channel_id=1, source_target_pairs={{0,4},{1,5},{2,6},{3,7},{4,0},{5,1},{6,2},{7,3},{8,12},{9,13},{10,... | collective-permute-start | bytes 1204232 | tf_op jit(solution)/shard_map/ppermute | solution.py:634
  71.0 5.0 %collective-permute-start.19 = (bf16[192,128]{1,0:T(8,128)(2,1)S(1)}, bf16[192,128]{1,0:T(8,128)(2,1)S(1)}, u32[]{:S(2)}, u32[]{:S(2)}) collective-permute-start(bf16[192,128]{1,0:T(8,128)(2,1)S(1)} %get-tuple-element.134), channel_id=1, source_target_pairs={{0,24},{8,16},{16,8},{24,0},{1,25},{9,17},{17,9},{25,1},{2,26},{10... | collective-permute-start | bytes 147464 | tf_op jit(solution)/shard_map/ppermute | solution.py:637
  72.1 19.0 %collective-permute-start.25 = (bf16[49,32,128]{2,1,0:T(8,128)(2,1)S(1)}, bf16[49,32,128]{2,1,0:T(8,128)(2,1)S(1)}, u32[]{:S(2)}, u32[]{:S(2)}) collective-permute-start(bf16[49,32,128]{2,1,0:T(8,128)(2,1)S(1)} %get-tuple-element.158), channel_id=1, source_target_pairs={{0,1},{1,0},{2,3},{3,2},{4,5},{5,4},{6,7},{7,6},{8,9},{9,8},{10,11... | collective-permute-start | bytes 1204232 | tf_op jit(solution)/shard_map/ppermute | solution.py:631
  76.0 6.5 %collective-permute-start.22 = (bf16[256,128]{1,0:T(8,128)(2,1)S(1)}, bf16[256,128]{1,0:T(8,128)(2,1)S(1)}, u32[]{:S(2)}, u32[]{:S(2)}) collective-permute-start(bf16[256,128]{1,0:T(8,128)(2,1)S(1)} %get-tuple-element.145), channel_id=1, source_target_pairs={{0,2},{1,3},{2,0},{3,1},{4,6},{5,7},{6,4},{7,5},{8,10},{9,11},{10,... | collective-permute-start | bytes 196616 | tf_op jit(solution)/shard_map/ppermute | solution.py:634
  76.4 6.6 %collective-permute-start.23 = (bf16[256,128]{1,0:T(8,128)(2,1)S(1)}, bf16[256,128]{1,0:T(8,128)(2,1)S(1)}, u32[]{:S(2)}, u32[]{:S(2)}) collective-permute-start(bf16[256,128]{1,0:T(8,128)(2,1)S(1)} %get-tuple-element.146), channel_id=1, source_target_pairs={{0,4},{1,5},{2,6},{3,7},{4,0},{5,1},{6,2},{7,3},{8,12},{9,13},{10,... | collective-permute-start | bytes 196616 | tf_op jit(solution)/shard_map/ppermute | solution.py:634
  78.9 6.1 %collective-permute-start.24 = (bf16[256,128]{1,0:T(8,128)(2,1)S(1)}, bf16[256,128]{1,0:T(8,128)(2,1)S(1)}, u32[]{:S(2)}, u32[]{:S(2)}) collective-permute-start(bf16[256,128]{1,0:T(8,128)(2,1)S(1)} %get-tuple-element.147), channel_id=1, source_target_pairs={{0,6},{1,7},{2,4},{3,5},{4,2},{5,3},{6,0},{7,1},{8,14},{9,15},{10,... | collective-permute-start | bytes 196616 | tf_op jit(solution)/shard_map/ppermute | solution.py:634
  86.1 5.0 %collective-permute-start.28 = (bf16[192,128]{1,0:T(8,128)(2,1)S(1)}, bf16[192,128]{1,0:T(8,128)(2,1)S(1)}, u32[]{:S(2)}, u32[]{:S(2)}) collective-permute-start(bf16[192,128]{1,0:T(8,128)(2,1)S(1)} %get-tuple-element.161.refs_0_), channel_id=1, source_target_pairs={{0,24},{8,16},{16,8},{24,0},{1,25},{9,17},{17,9},{25,1},{2,26},{10... | collective-permute-start | bytes 147464 | tf_op jit(solution)/shard_map/ppermute | solution.py:637
  88.5 5.2 %collective-permute-start.29 = (bf16[192,128]{1,0:T(8,128)(2,1)S(1)}, bf16[192,128]{1,0:T(8,128)(2,1)S(1)}, u32[]{:S(2)}, u32[]{:S(2)}) collective-permute-start(bf16[192,128]{1,0:T(8,128)(2,1)S(1)} %get-tuple-element.161.refs_0_), channel_id=1, source_target_pairs={{0,1},{1,0},{2,3},{3,2},{4,5},{5,4},{6,7},{7,6},{8,9},{9,8},{10,11... | collective-permute-start | bytes 147464 | tf_op jit(solution)/shard_map/ppermute | solution.py:631
  89.1 4.6 %collective-permute-start.30 = (bf16[192,128]{1,0:T(8,128)(2,1)S(1)}, bf16[192,128]{1,0:T(8,128)(2,1)S(1)}, u32[]{:S(2)}, u32[]{:S(2)}) collective-permute-start(bf16[192,128]{1,0:T(8,128)(2,1)S(1)} %collective-permute-done.26.refs_1_), channel_id=1, source_target_pairs={{0,1},{1,0},{2,3},{3,2},{4,5},{5,4},{6,7},{7,6},{8,9},{9,8},{10,11... | collective-permute-start | bytes 147464 | tf_op jit(solution)/shard_map/ppermute | solution.py:631
  (15 other events, 94.0 us)

commit v3 on v2

--- a/solution.py
+++ b/solution.py
@@ -72,7 +72,7 @@
     channels, edges = source.shape[1], source.shape[2]
 
     def step(i, carry):
-        rows = pl.ds(pl.multiple_of(i * CHUNK, CHUNK), CHUNK)
+        rows = pl.ds(i * CHUNK, CHUNK)
         for start in range(0, edges, LANES):
             lanes = pl.ds(start, LANES)
             carried = None
@@ -90,14 +90,15 @@
                 finish(rows, lanes, carried)
         return carry
 
-    lax.fori_loop(0, channels // CHUNK, step, 0)
+    for i in range(channels // CHUNK):
+        step(i, 0)
 
 
 def turn_back(table, source, degrees, out):
     channels, edges = source.shape[1], source.shape[2]
 
     def step(i, carry):
-        rows = pl.ds(pl.multiple_of(i * CHUNK, CHUNK), CHUNK)
+        rows = pl.ds(i * CHUNK, CHUNK)
         for start in range(0, edges, LANES):
             lanes = pl.ds(start, LANES)
             for degree in degrees:
@@ -110,19 +111,21 @@
                     out[k, rows, lanes] = total.astype(out.dtype)
         return carry
 
-    lax.fori_loop(0, channels // CHUNK, step, 0)
+    for i in range(channels // CHUNK):
+        step(i, 0)
 
 
 def by_sevens(body):
-    def step(i, carry):
+    for i in range(LMAX + 1):
         body(i * (LMAX + 1))
-        return carry
-
-    lax.fori_loop(0, LMAX + 1, step, 0)
 
 
 def each_k(body):
     by_sevens(lambda k: [body(k + j) for j in range(LMAX + 1)] and None)
+
+
+def flat(ref, k):
+    return ref[pl.ds(k, LMAX + 1)].reshape((LMAX + 1) * ref.shape[1], ref.shape[2])
 
 
 def rows_of(pieces):
@@ -274,17 +277,20 @@
     turn_back(table, scaled_rows, range(LMAX + 1), back)
 
     def collect(k):
-        out = dot(target_hit, back[k], 1, 1)
-        for p in range(chips):
-            parts[p][k] = out[p * nodes : (p + 1) * nodes].astype(parts[p].dtype)
-
-    each_k(collect)
+        out = dot(target_hit, flat(back, k), 1, 1).astype(BF)
+        for j in range(LMAX + 1):
+            for p in range(chips):
+                parts[p][k + j] = out[p * nodes : (p + 1) * nodes, j * LANES : (j + 1) * LANES]
+
+    by_sevens(collect)
 
 
 def share_kernel(chips, *refs):
-    stats, raw = refs[:chips], refs[chips : 2 * chips]
-    weight, pack, share = refs[2 * chips : 2 * chips + 3]
-    parts = refs[2 * chips + 3 :]
+    stats, raw, refs = refs[:chips], refs[chips : 2 * chips], refs[2 * chips :]
+    handed = range(2, chips, 2)
+    got, refs = dict(zip(handed, refs)), refs[len(handed) :]
+    weight, pack, sums_a, sums_b, share, dscore = refs[:6]
+    parts, summed = refs[6 : 6 + chips], dict(zip(handed, refs[6 + chips :]))
     targets = stats[0].shape[1]
     nodes = targets // chips
     target_hit32 = hits(pack[1:2], targets, F32)
@@ -293,15 +299,28 @@
     ]
     top = functools.reduce(jnp.maximum, [w[0:H] for w in wholes])
     bottom = jnp.exp(-top)
+    dots = jnp.zeros_like(top)
     for w in wholes:
-        bottom = bottom + w[H : 2 * H] * jnp.exp(w[0:H] - top)
-    factor = jnp.exp(wholes[0][0:H] - top) / bottom
-    share[...] = weight[...] * dot(factor, target_hit32, exact=True)
-    scale = jnp.transpose(spread(factor))
+        level = jnp.exp(w[0:H] - top)
+        bottom = bottom + w[H : 2 * H] * level
+        dots = dots + w[2 * H :] * level
+    factors = [jnp.exp(w[0:H] - top) / bottom for w in wholes[:2]]
+    at_edges = dot(
+        jnp.concatenate([factors[0], dots / bottom], axis=0), target_hit32, exact=True
+    )
+    shares = weight[...] * at_edges[0:H]
+    share[...] = shares
+    sums = jnp.concatenate([sums_a[...], sums_b[...]], axis=1)
+    dscore[...] = shares * (sums - at_edges[H:])
+    scales = [jnp.transpose(spread(f)) for f in factors]
 
     def normalize(k):
         for p in range(chips):
-            parts[p][k] = (raw[p][k] * scale[p * nodes : (p + 1) * nodes]).astype(BF)
+            rows = slice(p * nodes, (p + 1) * nodes)
+            here = raw[p][k].astype(F32) * scales[0][rows]
+            parts[p][k] = here.astype(BF)
+            if p in got:
+                summed[p][k] = (here + got[p][k].astype(F32) * scales[1][rows]).astype(BF)
 
     each_k(normalize)
 
@@ -311,7 +330,7 @@
     cots, refs = refs[:some], refs[some:]
     w_out, pack, table, mixed, *refs = refs
     if second:
-        before, share, pulled, pulled0, dalpha, dots, *refs = refs
+        before, weight, own_stats, pulled, pulled0, dalpha, stats, *refs = refs
     else:
         pulled, pulled0, dalpha, *refs = refs
     incoming, total_ref = refs
@@ -347,39 +366,50 @@
     dalpha[...] = sums
     pulled0[...] = table[0, 0:1, base : base + edges] * incoming[0].astype(F32)
     if second:
-        every = share[...] * jnp.concatenate([before[...], sums], axis=1)
-        target_hit32 = hits(pack[1:2], dots.shape[1], F32)
-        dots[...] = dot(every, target_hit32, 1, 1, exact=True)
-
-
-def back_kernel(chips, *refs):
-    parts = refs[:chips]
-    cots = refs[chips : 2 * chips]
-    (feats_own, feats_sib, pulled_a, pulled_b, share, scaled, gating, table, pack, w_mix) = refs[
-        2 * chips : 2 * chips + 10
-    ]
-    (gate_sum, dv_own, dv_sib, g_mix, g_value, g_out) = refs[2 * chips + 10 : 2 * chips + 16]
-    turned, spread_back = refs[2 * chips + 16 :]
+        every = weight[...] * jnp.concatenate([before[...], sums], axis=1)
+        stats[: 2 * H] = own_stats[...]
+        stats[2 * H :] = dot(every, hits(pack[1:2], stats.shape[1], F32), 1, 1, exact=True)
+
+
+def back_kernel(chips, where, *refs):
+    parts, cots, firsts = refs[:chips], refs[chips : 2 * chips], refs[2 * chips : 3 * chips]
+    refs = refs[3 * chips :]
+    feats_own, feats_sib, pulled_a, pulled_b, pulled0_a, pulled0_b = refs[:6]
+    share, dscore, query, mixed, scaled, gating, table, radial, pack, w_mix = refs[6:16]
+    keep, send, dv_own, dv_sib = refs[16:20]
+    dqs = refs[20 : 20 + chips]
+    turned, spread_back, grads = refs[20 + chips :]
     nodes = feats_own.shape[1]
+    targets = chips * nodes
     wide = H * VH
+    half = grads.shape[1]
+
+    def put(i, value):
+        at = i * wide
+        grads[at // half, at % half : at % half + value.shape[0]] = value
+
     gate = gating[...]
     zero = w_mix[0]
     shares = spread(share[...])
+    dlogit = spread(dscore[...]) * (1.0 / VH**0.5)
     gates = jnp.zeros_like(gate)
-    grad = jnp.zeros((wide, wide), F32)
 
     def pulled(r):
+        if r == 0:
+            whole = jnp.concatenate([pulled0_a[...], pulled0_b[...]], axis=1) * shares
+            return (whole + dlogit * query[...]).astype(BF)
         whole = jnp.concatenate([pulled_a[r], pulled_b[r]], axis=1)
         return (whole.astype(F32) * shares).astype(BF)
 
-    for r in range(1, LMAX + 1):
+    grad = jnp.zeros((wide, wide), F32)
+    for r in range(LMAX + 1):
         here = scaled[r]
         down = pulled(r)
         grad = grad + dot(here, down, 1, 1)
         out = dot(zero, down)
         gates = gates + out * here.astype(F32)
         turned[r] = (out * gate).astype(BF)
-    g_mix[0] = grad
+    put(3, grad)
     for order in range(1, MMAX + 1):
         block = mix_block(w_mix, order, True)
         grad = jnp.zeros((2 * wide, 2 * wide), F32)
@@ -394,100 +424,49 @@
             gates = gates + prod[:wide] + prod[wide:]
             turned[plus] = (out[:wide] * gate).astype(BF)
             turned[minus] = (out[wide:] * gate).astype(BF)
-        g_mix[2 * order - 1] = grad[:wide, :wide] + grad[wide:, wide:]
-        g_mix[2 * order] = grad[:wide, wide:] - grad[wide:, :wide]
-    gate_sum[...] = gates
-    turn_back(table, turned, range(1, LMAX + 1), spread_back)
-    spread_back[0] = jnp.zeros_like(spread_back[0])
-    source_hit = hits(pack[0:1], 2 * nodes, BF)
-
-    def collect(k):
-        out = dot(source_hit, spread_back[k], 1, 1).astype(BF)
-        dv_own[k] = out[:nodes]
-        dv_sib[k] = out[nodes:]
-
-    each_k(collect)
-    g_value[...] = jnp.zeros_like(g_value)
-    g_out[...] = jnp.zeros_like(g_out)
-
-    def weigh(k):
-        some = pl.ds(k, LMAX + 1)
-
-        def flat(ref):
-            return ref[some].reshape((LMAX + 1) * nodes, wide)
-
-        g_value[...] += dot(flat(feats_own), flat(dv_own), 0, 0) + dot(
-            flat(feats_sib), flat(dv_sib), 0, 0
-        )
-        total = dot(flat(parts[0]), flat(cots[0]), 0, 0)
-        for p in range(1, chips):
-            total = total + dot(flat(parts[p]), flat(cots[p]), 0, 0)
-        g_out[...] += total
-
-    by_sevens(weigh)
-
-
-def tail_kernel(chips, where, *refs):
-    dots = refs[:chips]
-    firsts = refs[chips : 2 * chips]
-    refs = refs[2 * chips :]
-    feats_sib = refs[0]
-    dalphas, share, pulled0s = refs[1:3], refs[3], refs[4:6]
-    query, mixed, scaled, gating, table, gate_sum, radial, pack, w_mix = refs[6:15]
-    g_mix, g_value, g_out = refs[15:18]
-    keep, send, dv_own = refs[18:21]
-    dqs = refs[21 : 21 + chips]
-    (grads,) = refs[21 + chips :]
-    nodes = feats_sib.shape[1]
-    targets = chips * nodes
-    wide = H * VH
-    target_hit = hits(pack[1:2], targets, F32)
-
-    def both(pair):
-        return jnp.concatenate([pair[0][...], pair[1][...]], axis=1)
-
-    total = dots[0][...]
-    for p in range(1, chips):
-        total = total + jnp.concatenate(whole_order(dots[p], chips, p, nodes), axis=1)
-    dscore = share[...] * (both(dalphas) - dot(total, target_hit, exact=True))
-    dlogit = spread(dscore) * (1.0 / VH**0.5)
-    pulled0 = both(pulled0s) * spread(share[...])
-    down = (pulled0 + dlogit * query[...]).astype(BF)
-    here = scaled[0]
-    gate = gating[...]
-    out = dot(w_mix[0], down)
-    dgate = ((gate_sum[...] + out * here.astype(F32)) * (1.0 - gate)).astype(BF)
-    back = (table[0, 0:1, :] * (out * gate).astype(BF).astype(F32)).astype(BF)
-    source_hit = hits(pack[0:1], 2 * nodes, BF)
-    dv = dot(source_hit, back, 1, 1).astype(BF)
-    dv_own[...] = dv[:nodes]
-    dq = dot(target_hit, dlogit * mixed[0].astype(F32), 1, 1, exact=True)
+        put(2 + 2 * order, grad[:wide, :wide] + grad[wide:, wide:])
+        put(3 + 2 * order, grad[:wide, wide:] - grad[wide:, :wide])
+    dgate = (gates * (1.0 - gate)).astype(BF)
+    radial_grad = dot(dgate, radial[...])
+    for i in range(radial.shape[1] // wide):
+        put(4 + 2 * MMAX + i, jnp.transpose(radial_grad[:, i * wide : (i + 1) * wide]))
+    dq = dot(hits(pack[1:2], targets, F32), dlogit * mixed[0].astype(F32), 1, 1, exact=True)
     for p in range(chips):
         some = dq[p * nodes : (p + 1) * nodes]
         dqs[p][:nodes] = some.astype(BF)
         dqs[p][nodes:] = (some - some.astype(BF).astype(F32)).astype(BF)
-    first = rows_of([f[...] for f in firsts])
-    node0 = rows_of([firsts[0][...], feats_sib[0]])
-    pieces = [g_value[...] + dot(node0, dv, 0, 0), dot(first, dq.astype(BF), 0, 0), g_out[...]]
-    pieces += [g_mix[0] + dot(here, down, 1, 1)]
-    pieces += [g_mix[i] for i in range(1, 2 * MMAX + 1)]
-    turned = dot(dgate, radial[...])
-    for i in range(radial.shape[1] // wide):
-        pieces.append(jnp.transpose(turned[:, i * wide : (i + 1) * wide]))
-    half = grads.shape[1]
-    for i, piece in enumerate(pieces):
-        at = i * wide
-        grads[at // half, at % half : at % half + wide] = piece
+    put(1, dot(rows_of([f[...] for f in firsts]), dq.astype(BF), 0, 0))
+
+    turn_back(table, turned, range(LMAX + 1), spread_back)
+    source_hit = hits(pack[0:1], 2 * nodes, BF)
+
+    def collect(k):
+        out = dot(source_hit, flat(spread_back, k), 1, 1).astype(BF)
+        for j in range(LMAX + 1):
+            dv_own[k + j] = out[:nodes, j * LANES : (j + 1) * LANES]
+            dv_sib[k + j] = out[nodes:, j * LANES : (j + 1) * LANES]
+
+    by_sevens(collect)
+    put(0, jnp.zeros((wide, wide), F32))
+    put(2, jnp.zeros((wide, wide), F32))
+
+    def weigh(k):
+        grads[0, 0:wide] += dot(flat(feats_own, k), flat(dv_own, k), 0, 0) + dot(
+            flat(feats_sib, k), flat(dv_sib, k), 0, 0
+        )
+        total = dot(flat(parts[0], k), flat(cots[0], k), 0, 0)
+        for p in range(1, chips):
+            total = total + dot(flat(parts[p], k), flat(cots[p], k), 0, 0)
+        grads[0, 2 * wide : 3 * wide] += total
+
+    by_sevens(weigh)
     keep[...] = grads[where[0]]
-    send[: keep.shape[0]] = grads[1 - where[0]].astype(BF)
-    send[keep.shape[0] :] = dv[nodes:]
-
-
-def split_kernel(planes, where, keep, got, own, dv0, *outs):
+    send[...] = grads[1 - where[0]].astype(BF)
+
+
+def split_kernel(planes, where, keep, got, own, *outs):
     *sends, total = outs
-    rows = keep.shape[0]
-    total[...] = (keep[...] + got[:rows].astype(F32)).reshape(total.shape)
-    dv0[...] = got[rows:]
+    total[...] = (keep[...] + got[...].astype(F32)).reshape(total.shape)
     own[...] = total[where[1]]
     for step in range(1, planes):
         sends[step - 1][...] = total[where[1] ^ step].astype(BF)
@@ -534,17 +513,19 @@
         g_radial[i * wide : (i + 1) * wide] = pieces[at + i]
 
 
-def nodes_kernel(dquery, dv_own, dv_sib, dv0_own, dv0_sib, cot, w_value, w_query, out):
+def nodes_kernel(dquery, dv_own, dv_sib, cot, w_value, w_query, out):
     value_w = w_value[...]
 
+    def back(k):
+        dv = (dv_own[k].astype(F32) + dv_sib[k].astype(F32)).astype(BF)
+        return dot(dv, value_w, 1, 1)
+
     def one(k):
-        dv = (dv_own[k].astype(F32) + dv_sib[k].astype(F32)).astype(BF)
-        out[k] = (cot[k].astype(F32) + dot(dv, value_w, 1, 1)).astype(BF)
+        out[k] = (cot[k].astype(F32) + back(k)).astype(BF)
 
     each_k(one)
-    dv = (dv0_own[...].astype(F32) + dv0_sib[...].astype(F32)).astype(BF)
     query_part = dot(dquery[...], w_query[...], 1, 1)
-    out[0] = (cot[0].astype(F32) + dot(dv, value_w, 1, 1) + query_part).astype(BF)
+    out[0] = (cot[0].astype(F32) + back(0) + query_part).astype(BF)
 
 
 def add_kernel(*refs):
@@ -654,8 +635,6 @@
     pack_sib = other_core(pack_own)
     radial_sib = other_core(radial[0])
     feats_sib = other_core(feats)
-    firsts = direct(feats[0])
-    radial_sib, firsts = lax.optimization_barrier((radial_sib, firsts))
 
     edge_f32 = ((wide, slots), F32)
     half_f32 = ((wide, slots // 2), F32)
@@ -690,6 +669,13 @@
         far=6,
         limit=32,
     )
+    first, mixed = lax.optimization_barrier((feats[0], mixed))
+    firsts = direct(first)
+    del have[0]
+    firsts, have = lax.optimization_barrier((firsts, have))
+    have[0] = cot
+    have.update({p ^ 1: along(a, 1) if p else neighbour for p, a in have.items()})
+    cots = [have[p] for p in range(chips)]
     weight, stats, query, *raw = call(
         "attend",
         1,
@@ -699,17 +685,11 @@
             ((H, slots), F32),
             ((2 * H, spot), F32),
             edge_f32,
-            *([((K, nodes, wide), F32)] * chips),
+            *([block] * chips),
         ],
         [((R, wide, slots), BF), ((K, wide, slots), BF)],
         far=1,
     )
-    del have[0]
-    stats, have = lax.optimization_barrier((stats, have))
-    have[0] = cot
-    have.update({p ^ 1: along(a, 1) if p else neighbour for p, a in have.items()})
-    cots = [have[p] for p in range(chips)]
-    all_stats = direct(stats)
 
     def pull(second, extra, sums):
         mine = slice(some, chips) if second else slice(0, some)
@@ -723,29 +703,21 @@
         )
 
     pulled_a, pulled0_a, dalpha_a = pull(False, [], [])
-    share, *parts = call(
+    raw, cots[-1] = lax.optimization_barrier((raw, cots[-1]))
+    near = [along(raw[p], 1) for p in range(3, chips, 2)]
+    pulled_b, pulled0_b, dalpha_b, stats = pull(
+        True, [dalpha_a, weight, stats], [((3 * H, spot), F32)]
+    )
+    share, dscore, *parts = call(
         "share",
-        0.3,
+        0.6,
         functools.partial(share_kernel, chips),
-        [*all_stats, *raw, weight, pack],
-        [((H, slots), F32), *([block] * chips)],
-    )
-
-    parts, cots[-1] = lax.optimization_barrier((parts, cots[-1]))
-    pending = {p: [parts[p]] for p in range(chips)}
-    near = {p: along(parts[p], 1) for p in range(chips) if p & 1 and p > 1}
-    pulled_b, pulled0_b, dalpha_b, dots = pull(True, [dalpha_a, share], [((H, spot), F32)])
-    all_dots = direct(dots)
-    for p, got in near.items():
-        del pending[p]
-        pending[p ^ 1].append(got)
-    summed = {}
-    for p in pending:
-        if p:
-            (summed[p],) = call("add", 1, add_kernel, pending[p], [block])
-    pulled_b, summed, last = lax.optimization_barrier((pulled_b, summed, parts[1]))
-    del pending[1]
-    pending[0].append(along(last, 1))
+        [*direct(stats), *raw, *near, weight, pack, dalpha_a, dalpha_b],
+        [((H, slots), F32)] * 2 + [block] * (chips + len(near)),
+    )
+    summed = dict(zip(range(2, chips, 2), parts[chips:]))
+    parts = parts[:chips]
+    pending = [parts[0], along(parts[1], 1)]
     step = 2
     while step < chips:
         for p in [p for p in summed if p & step]:
@@ -753,84 +725,61 @@
             if p ^ step:
                 (summed[p ^ step],) = call("add", 1, add_kernel, [summed[p ^ step], got], [block])
             else:
-                pending[0].append(got)
+                pending.append(got)
         step *= 2
-    gate_sum, dv_own, dv_sib, g_mix, g_value, g_out = call(
+    total_rows = (4 + 2 * MMAX) * wide + radial.shape[2]
+    cut = total_rows // (2 * planes)
+    keep, send, dv_own, dv_sib, *dqs = call(
         "back",
-        7.5,
+        9,
         functools.partial(back_kernel, chips),
         [
+            where_sum,
             *parts,
             *cots,
+            *firsts,
             feats,
             feats_sib,
             pulled_a,
             pulled_b,
-            share,
-            scaled,
-            gating,
-            table,
-            pack,
-            w_mix,
-        ],
-        [edge_f32, block, block, (w_mix.shape, F32), ((wide, wide), F32), ((wide, wide), F32)],
-        [((R, wide, slots), BF), ((K, wide, slots), BF)],
-        limit=32,
-    )
-    dv_got = other_core(dv_sib)
-
-    total_rows = (4 + 2 * MMAX) * wide + radial.shape[2]
-    cut = total_rows // (2 * planes)
-    small = ((nodes, wide), BF)
-    keep, send, dv0_own, *dqs = call(
-        "tail",
-        1.8,
-        functools.partial(tail_kernel, chips),
-        [
-            where_sum,
-            *all_dots,
-            *firsts,
-            feats_sib,
-            dalpha_a,
-            dalpha_b,
-            share,
             pulled0_a,
             pulled0_b,
+            share,
+            dscore,
             query,
             mixed,
             scaled,
             gating,
             table,
-            gate_sum,
             radial_here,
             pack,
             w_mix,
-            g_mix,
-            g_value,
-            g_out,
         ],
         [
             ((total_rows // 2, wide), F32),
-            ((total_rows // 2 + nodes, wide), BF),
-            small,
+            ((total_rows // 2, wide), BF),
+            block,
+            block,
             *([((2 * nodes, wide), BF)] * chips),
         ],
-        [((2, total_rows // 2, wide), F32)],
+        [((R, wide, slots), BF), ((K, wide, slots), BF), ((2, total_rows // 2, wide), F32)],
         smem=1,
-    )
+        limit=32,
+    )
+    dv_got = other_core(dv_sib)
 
     got = other_core(send)
-    own, dv0_got, *sends = call(
+    own, *sends = call(
         "split",
         0.6,
         functools.partial(split_kernel, planes),
         [where_sum, keep, got],
-        [((cut, wide), F32), small, *([((cut, wide), BF)] * (planes - 1))],
+        [((cut, wide), F32), *([((cut, wide), BF)] * (planes - 1))],
         [((planes, cut, wide), F32)],
         smem=1,
     )
     got = [beside(sends[step - 1], step) for step in range(1, planes)]
-    got, pending[0] = lax.optimization_barrier((got, pending[0]))
+    got, pending = lax.optimization_barrier((got, pending))
     letters = call(
         "address",
         0.6,
@@ -839,9 +788,11 @@
         [((cut + 2 * nodes, wide), BF)] * chips,
     )
     terms = [letters[0]] + [along(letters[step], step) for step in range(1, chips)]
-    (updated,) = call("update", 2, update_kernel, [*pending[0], feats, w_out], [block])
+    (updated,) = call("update", 2, update_kernel, [*pending, feats, w_out], [block])
     terms, updated = lax.optimization_barrier((terms, updated))
-    piece, dquery = call("settle", 0.6, settle_kernel, terms, [((cut, wide), BF), small])
+    piece, dquery = call(
+        "settle", 0.6, settle_kernel, terms, [((cut, wide), BF), ((nodes, wide), BF)]
+    )
     mine = [piece] + [beside(piece, step) for step in range(1, planes)]
     theirs = [other_core(a) for a in mine]
     grads = call(
@@ -864,7 +815,7 @@
         "nodes",
         2.6,
         nodes_kernel,
-        [dquery, dv_own, dv_got, dv0_own, dv0_got, cot, w_value, w_query],
+        [dquery, dv_own, dv_got, cot, w_value, w_query],
         [block],
     )
     return (

time: 95.5 us -> 86.1 us (0.902)
  Pallas kernels: 40.5 us -> 29.7 us
  waiting for transfers between devices: 19.2 us -> 23.4 us
  starting transfers between devices: 33 us -> 30.2 us
    pallas_call x14 -> x12, Pallas kernels: 40.5 us -> 29.7 us  [call(): pl.pallas_call(kernel, out_shape=[jax.ShapeDtypeStruct(s, d) for s, d in...]
    ppermute x18 -> x15, waiting for transfers between devices: 10.7 us -> 13.7 us  [along(): return lax.ppermute(a, 'graph', [(i, i ^ 2 * step) for i in range(ranks)])]
    ppermute x18 -> x15, starting transfers between devices: 25.2 us -> 22.3 us  [along(): return lax.ppermute(a, 'graph', [(i, i ^ 2 * step) for i in range(ranks)])]
  transfers between devices with their start and end apart: 33 -> 30, of which waited for: 15 -> 15; matrix products, arithmetic and copies ran while one was open for 1% -> 2% of each run, Pallas kernels for 41% -> 32%
where the time goes in v3:
time: 86.1 us; the launch traced here: 85.8 us
  starting transfers between devices  30.2 us (35%)
  Pallas kernels  29.7 us (34%)
  waiting for transfers between devices  23.4 us (27%)
  other arithmetic  0.98 us (1%)
    pallas_call x12, Pallas kernels, call(): pl.pallas_call(kernel, out_shape=[jax.ShapeDtypeStruct(s, d) for s, d in...  29.7 us
    ppermute x15, starting transfers between devices, along(): return lax.ppermute(a, 'graph', [(i, i ^ 2 * step) for i in range(ranks)])  22.3 us
    ppermute x15, waiting for transfers between devices, along(): return lax.ppermute(a, 'graph', [(i, i ^ 2 * step) for i in range(ranks)])  13.7 us
    ppermute x6, waiting for transfers between devices, beside(): return lax.ppermute(a, 'dp', [(i, i ^ step) for i in range(planes)])  7.35 us
    ppermute x6, starting transfers between devices, beside(): return lax.ppermute(a, 'dp', [(i, i ^ step) for i in range(planes)])  7.11 us
    ppermute x9, waiting for transfers between devices, other_core(): return lax.ppermute(a, 'graph', [(i, i ^ 1) for i in range(ranks)])  2.34 us
  transfers between devices with their start and end apart: 30, of which 15 were waited for; matrix products, arithmetic and copies ran while one was open for 2% of the time, Pallas kernels for 32%

profile of v3, /device:TPU:0, one launch (start us, length us, event | category | flops | bytes accessed | tf_op | source)
XLA Modules:
  0.0 85.8 jit_solution(878816881373963555)
XLA Ops:
  0.6 3.1 %collective-permute-start.8 = (bf16[49,32,128]{2,1,0:T(8,128)(2,1)}, bf16[49,32,128]{2,1,0:T(8,128)(2,1)S(1)}, u32[]{:S(2)}, u32[]{:S(2)}) collective-permute-start(bf16[49,32,128]{2,1,0:T(8,128)(2,1)} %bitcast.26), channel_id=1, source_target_pairs={{0,2},{1,3},{2,0},{3,1},{4,6},{5,7},{6,4},{7,5},{8,10},{9,11},{10,... | collective-permute-start | bytes 1204232 | tf_op jit(solution)/shard_map/ppermute | solution.py:615
  3.7 2.6 %collective-permute-start.6 = (bf16[49,32,128]{2,1,0:T(8,128)(2,1)}, bf16[49,32,128]{2,1,0:T(8,128)(2,1)S(1)}, u32[]{:S(2)}, u32[]{:S(2)}) collective-permute-start(bf16[49,32,128]{2,1,0:T(8,128)(2,1)} %bitcast.27), channel_id=1, source_target_pairs={{0,4},{1,5},{2,6},{3,7},{4,0},{5,1},{6,2},{7,3},{8,12},{9,13},{10,... | collective-permute-start | bytes 1204232 | tf_op jit(solution)/shard_map/ppermute | solution.py:615
  9.5 7.4 %forward.1 = (f32[29,56,256]{2,1,0:T(8,128)S(1)}, bf16[29,128,256]{2,1,0:T(8,128)(2,1)S(1)}, bf16[29,128,256]{2,1,0:T(8,128)(2,1)S(1)}, f32[128,256]{1,0:T(8,128...) custom-call(s32[3]{0:T(128)S(1)} %pad_add_fusion.1.where, bf16[256,512]{1,0:T(8,128)(2,1)} %bitcast.43, ...), custom_call_target="tpu_custom_call" | custom-call | flops 10350000128 | bytes 1000 | tf_op jit(solution)/shard_map/forward/pallas_call | solution.py:563
  16.9 1.9 %collective-permute-start.4 = (bf16[32,128]{1,0:T(8,128)(2,1)S(1)}, bf16[32,128]{1,0:T(8,128)(2,1)S(1)}, u32[]{:S(2)}, u32[]{:S(2)}) collective-permute-start(bf16[32,128]{1,0:T(8,128)(2,1)S(1)} %slice_bitcast_fusion.refs_1_.refs_8_), channel_id=1, source_target_pairs={{0,4},{1,5},{2,6},{3,7},{4,0},{5,1},{6,2},{7,3},{8,12},{9,13},{10,... | collective-permute-start | bytes 24584 | tf_op jit(solution)/shard_map/ppermute | solution.py:615
  18.8 2.5 %collective-permute-start.3 = (bf16[32,128]{1,0:T(8,128)(2,1)S(1)}, bf16[32,128]{1,0:T(8,128)(2,1)S(1)}, u32[]{:S(2)}, u32[]{:S(2)}) collective-permute-start(bf16[32,128]{1,0:T(8,128)(2,1)S(1)} %slice_bitcast_fusion.refs_1_.refs_8_), channel_id=1, source_target_pairs={{0,2},{1,3},{2,0},{3,1},{4,6},{5,7},{6,4},{7,5},{8,10},{9,11},{10,... | collective-permute-start | bytes 24584 | tf_op jit(solution)/shard_map/ppermute | solution.py:615
  21.3 3.3 %collective-permute-done.6.refs_0_.refs_6_ = bf16[49,32,128]{2,1,0:T(8,128)(2,1)S(1)} collective-permute-done((bf16[49,32,128]{2,1,0:T(8,128)(2,1)}, bf16[49,32,128]{2,1,0:T(8,128)(2,1)S(1)}, u32[]{:S(2)}, u32[]{:S(2)}) %collective-permute-start.6) | collective-permute-done | bytes 401440 | tf_op jit(solution)/shard_map/ppermute | solution.py:615
  25.4 2.0 %pull.2 = (bf16[29,128,128]{2,1,0:T(8,128)(2,1)S(1)}, f32[128,128]{1,0:T(8,128)S(1)}, f32[8,128]{1,0:T(8,128)S(1)}) custom-call(bf16[49,32,128]{2,1,0:T(8,128)(2,1)S(1)} %bitcast.28, bf16[49,32,128]{2,1,0:T(8,128)(2,1)S(1)} %collective-permute-done.8.refs_1_.refs_5_, bf16[128,128]{1,0:T(8,128)(2,1)S(1)} %copy-done.1, ...), custom_call_target="tpu_custom_call" | custom-call | flops 1150000000 | bytes 1000 | tf_op jit(solution)/shard_map/pull/pallas_call | solution.py:563
  27.4 5.6 %attend.1 = (f32[8,256]{1,0:T(8,128)S(1)}, f32[16,128]{1,0:T(8,128)S(1)}, f32[128,256]{1,0:T(8,128)S(1)}, bf16[49,32,128]{2,1,0:T(8,128)(2,1)S(1)}, bf16[49,32,1...) custom-call(bf16[128,128]{1,0:T(8,128)(2,1)} %w_query.1, ...), custom_call_target="tpu_custom_call" | custom-call | flops 1150000000 | bytes 1000 | tf_op jit(solution)/shard_map/attend/pallas_call | solution.py:563
  33.0 3.2 %collective-permute-done.7.refs_1_.refs_7_ = bf16[49,32,128]{2,1,0:T(8,128)(2,1)S(1)} collective-permute-done((bf16[49,32,128]{2,1,0:T(8,128)(2,1)S(1)}, bf16[49,32,128]{2,1,0:T(8,128)(2,1)S(1)}, u32[]{:S(2)}, u32[]{:S(2)}) %collective-permute-start.7) | collective-permute-done | bytes 401440 | tf_op jit(solution)/shard_map/ppermute | solution.py:615
  36.6 2.4 %pull.3 = (bf16[29,128,128]{2,1,0:T(8,128)(2,1)S(1)}, f32[128,128]{1,0:T(8,128)S(1)}, f32[8,128]{1,0:T(8,128)S(1)}, f32[24,128]{1,0:T(8,128)S(1)}) custom-call(bf16[49,32,128]{2,1,0:T(8,128)(2,1)S(1)} %collective-permute-done.6.refs_0_.refs_6_, bf16[49,32,128]{2,1,0:T(8,128)(2,1)S(1)} %collective-permute-done.7.refs_1_.refs_7_, ...), custom_call_target="tpu_custom_call" | custom-call | flops 4600000000 | bytes 1000 | tf_op jit(solution)/shard_map/pull/pallas_call | solution.py:563
  40.4 1.8 %collective-permute-start.10 = (f32[24,128]{1,0:T(8,128)S(1)}, f32[24,128]{1,0:T(8,128)S(1)}, u32[]{:S(2)}, u32[]{:S(2)}) collective-permute-start(f32[24,128]{1,0:T(8,128)S(1)} %get-tuple-element.98.refs_0_), channel_id=1, source_target_pairs={{0,4},{1,5},{2,6},{3,7},{4,0},{5,1},{6,2},{7,3},{8,12},{9,13},{10,... | collective-permute-start | bytes 36872 | tf_op jit(solution)/shard_map/ppermute | solution.py:615
  43.5 2.1 %collective-permute-done.11.refs_3_ = f32[24,128]{1,0:T(8,128)S(1)} collective-permute-done((f32[24,128]{1,0:T(8,128)S(1)}, f32[24,128]{1,0:T(8,128)S(1)}, u32[]{:S(2)}, u32[]{:S(2)}) %collective-permute-start.11) | collective-permute-done | bytes 12320 | tf_op jit(solution)/shard_map/ppermute | solution.py:615
  45.6 1.8 %collective-permute-done.9.refs_1_ = f32[24,128]{1,0:T(8,128)S(1)} collective-permute-done((f32[24,128]{1,0:T(8,128)S(1)}, f32[24,128]{1,0:T(8,128)S(1)}, u32[]{:S(2)}, u32[]{:S(2)}) %collective-permute-start.9) | collective-permute-done | bytes 12320 | tf_op jit(solution)/shard_map/ppermute | solution.py:615
  50.5 6.5 %back.1 = (f32[768,128]{1,0:T(8,128)S(1)}, bf16[768,128]{1,0:T(8,128)(2,1)S(1)}, bf16[49,32,128]{2,1,0:T(8,128)(2,1)S(1)}, bf16[49,32,128]{2,1,0:T(8,128)(2,1)S(...) custom-call(s32[2]{0:T(128)S(1)} %pad_add_fusion.where, ...), custom_call_target="tpu_custom_call" | custom-call | flops 10350000128 | bytes 1000 | tf_op jit(solution)/shard_map/back/pallas_call | solution.py:563
  59.2 1.6 %collective-permute-start.14 = (bf16[192,128]{1,0:T(8,128)(2,1)S(1)}, bf16[192,128]{1,0:T(8,128)(2,1)S(1)}, u32[]{:S(2)}, u32[]{:S(2)}) collective-permute-start(bf16[192,128]{1,0:T(8,128)(2,1)S(1)} %get-tuple-element.121), channel_id=1, source_target_pairs={{0,8},{8,0},{16,24},{24,16},{1,9},{9,1},{17,25},{25,17},{2,10},{10... | collective-permute-start | bytes 147464 | tf_op jit(solution)/shard_map/ppermute | solution.py:618
  60.7 1.5 %collective-permute-start.15 = (bf16[192,128]{1,0:T(8,128)(2,1)S(1)}, bf16[192,128]{1,0:T(8,128)(2,1)S(1)}, u32[]{:S(2)}, u32[]{:S(2)}) collective-permute-start(bf16[192,128]{1,0:T(8,128)(2,1)S(1)} %get-tuple-element.122), channel_id=1, source_target_pairs={{0,16},{8,24},{16,0},{24,8},{1,17},{9,25},{17,1},{25,9},{2,18},{10... | collective-permute-start | bytes 147464 | tf_op jit(solution)/shard_map/ppermute | solution.py:618
  63.3 1.5 %collective-permute-done.15.refs_1_ = bf16[192,128]{1,0:T(8,128)(2,1)S(1)} collective-permute-done((bf16[192,128]{1,0:T(8,128)(2,1)S(1)}, bf16[192,128]{1,0:T(8,128)(2,1)S(1)}, u32[]{:S(2)}, u32[]{:S(2)}) %collective-permute-start.15) | collective-permute-done | bytes 49184 | tf_op jit(solution)/shard_map/ppermute | solution.py:618
  64.8 2.4 %collective-permute-done.16.refs_2_ = bf16[192,128]{1,0:T(8,128)(2,1)S(1)} collective-permute-done((bf16[192,128]{1,0:T(8,128)(2,1)S(1)}, bf16[192,128]{1,0:T(8,128)(2,1)S(1)}, u32[]{:S(2)}, u32[]{:S(2)}) %collective-permute-start.16) | collective-permute-done | bytes 49184 | tf_op jit(solution)/shard_map/ppermute | solution.py:618
  68.0 1.8 %collective-permute-start.20 = (bf16[256,128]{1,0:T(8,128)(2,1)S(1)}, bf16[256,128]{1,0:T(8,128)(2,1)S(1)}, u32[]{:S(2)}, u32[]{:S(2)}) collective-permute-start(bf16[256,128]{1,0:T(8,128)(2,1)S(1)} %get-tuple-element.134), channel_id=1, source_target_pairs={{0,4},{1,5},{2,6},{3,7},{4,0},{5,1},{6,2},{7,3},{8,12},{9,13},{10,... | collective-permute-start | bytes 196616 | tf_op jit(solution)/shard_map/ppermute | solution.py:615
  69.9 1.9 %collective-permute-start.21 = (bf16[256,128]{1,0:T(8,128)(2,1)S(1)}, bf16[256,128]{1,0:T(8,128)(2,1)S(1)}, u32[]{:S(2)}, u32[]{:S(2)}) collective-permute-start(bf16[256,128]{1,0:T(8,128)(2,1)S(1)} %get-tuple-element.135), channel_id=1, source_target_pairs={{0,6},{1,7},{2,4},{3,5},{4,2},{5,3},{6,0},{7,1},{8,14},{9,15},{10,... | collective-permute-start | bytes 196616 | tf_op jit(solution)/shard_map/ppermute | solution.py:615
  73.0 1.6 %collective-permute-done.20.refs_2_ = bf16[256,128]{1,0:T(8,128)(2,1)S(1)} collective-permute-done((bf16[256,128]{1,0:T(8,128)(2,1)S(1)}, bf16[256,128]{1,0:T(8,128)(2,1)S(1)}, u32[]{:S(2)}, u32[]{:S(2)}) %collective-permute-start.20) | collective-permute-done | bytes 65568 | tf_op jit(solution)/shard_map/ppermute | solution.py:615
  76.1 1.8 %collective-permute-start.25 = (bf16[192,128]{1,0:T(8,128)(2,1)S(1)}, bf16[192,128]{1,0:T(8,128)(2,1)S(1)}, u32[]{:S(2)}, u32[]{:S(2)}) collective-permute-start(bf16[192,128]{1,0:T(8,128)(2,1)S(1)} %get-tuple-element.147.refs_0_), channel_id=1, source_target_pairs={{0,24},{8,16},{16,8},{24,0},{1,25},{9,17},{17,9},{25,1},{2,26},{10... | collective-permute-start | bytes 147464 | tf_op jit(solution)/shard_map/ppermute | solution.py:618
  79.6 1.5 %collective-permute-done.25.refs_3_ = bf16[192,128]{1,0:T(8,128)(2,1)S(1)} collective-permute-done((bf16[192,128]{1,0:T(8,128)(2,1)S(1)}, bf16[192,128]{1,0:T(8,128)(2,1)S(1)}, u32[]{:S(2)}, u32[]{:S(2)}) %collective-permute-start.25) | collective-permute-done | bytes 49184 | tf_op jit(solution)/shard_map/ppermute | solution.py:618
  82.5 1.8 %nodes.1 = bf16[49,32,128]{2,1,0:T(8,128)(2,1)} custom-call(bf16[32,128]{1,0:T(8,128)(2,1)S(1)} %get-tuple-element.144.dquery, bf16[49,32,128]{2,1,0:T(8,128)(2,1)S(1)} %get-tuple-element.145.dv_own, bf16[49,32,128]{2,1,0:T(8,128)(2,1)S(1)} %collective-permute-done.22.dv_sib, bf16[49,32,128]{2,1,0:T(8,128)(2,1)S(1)} %bitcast.30, ...), custom_call_target="tpu_custom_call" | custom-call | flops 2990000128 | bytes 1000 | tf_op jit(solution)/shard_map/nodes/pallas_call | solution.py:563
  (66 shorter events, 21.5 us)
Async XLA Ops:
  0.6 24.8 %collective-permute-start.8 = (bf16[49,32,128]{2,1,0:T(8,128)(2,1)}, bf16[49,32,128]{2,1,0:T(8,128)(2,1)S(1)}, u32[]{:S(2)}, u32[]{:S(2)}) collective-permute-start(bf16[49,32,128]{2,1,0:T(8,128)(2,1)} %bitcast.26), channel_id=1, source_target_pairs={{0,2},{1,3},{2,0},{3,1},{4,6},{5,7},{6,4},{7,5},{8,10},{9,11},{10,... | collective-permute-start | bytes 1204232 | tf_op jit(solution)/shard_map/ppermute | solution.py:615
  3.7 20.9 %collective-permute-start.6 = (bf16[49,32,128]{2,1,0:T(8,128)(2,1)}, bf16[49,32,128]{2,1,0:T(8,128)(2,1)S(1)}, u32[]{:S(2)}, u32[]{:S(2)}) collective-permute-start(bf16[49,32,128]{2,1,0:T(8,128)(2,1)} %bitcast.27), channel_id=1, source_target_pairs={{0,4},{1,5},{2,6},{3,7},{4,0},{5,1},{6,2},{7,3},{8,12},{9,13},{10,... | collective-permute-start | bytes 1204232 | tf_op jit(solution)/shard_map/ppermute | solution.py:615
  6.3 3.2 %collective-permute-start.2 = (bf16[49,32,128]{2,1,0:T(8,128)(2,1)}, bf16[49,32,128]{2,1,0:T(8,128)(2,1)S(1)}, u32[]{:S(2)}, u32[]{:S(2)}) collective-permute-start(bf16[49,32,128]{2,1,0:T(8,128)(2,1)} %bitcast.31), channel_id=1, source_target_pairs={{0,1},{1,0},{2,3},{3,2},{4,5},{5,4},{6,7},{7,6},{8,9},{9,8},{10,11... | collective-permute-start | bytes 1204232 | tf_op jit(solution)/shard_map/ppermute | solution.py:612
  16.9 7.8 %collective-permute-start.5 = (bf16[32,128]{1,0:T(8,128)(2,1)S(1)}, bf16[32,128]{1,0:T(8,128)(2,1)S(1)}, u32[]{:S(2)}, u32[]{:S(2)}) collective-permute-start(bf16[32,128]{1,0:T(8,128)(2,1)S(1)} %slice_bitcast_fusion.refs_1_.refs_8_), channel_id=1, source_target_pairs={{0,6},{1,7},{2,4},{3,5},{4,2},{5,3},{6,0},{7,1},{8,14},{9,15},{10,... | collective-permute-start | bytes 24584 | tf_op jit(solution)/shard_map/ppermute | solution.py:615
  16.9 8.0 %collective-permute-start.4 = (bf16[32,128]{1,0:T(8,128)(2,1)S(1)}, bf16[32,128]{1,0:T(8,128)(2,1)S(1)}, u32[]{:S(2)}, u32[]{:S(2)}) collective-permute-start(bf16[32,128]{1,0:T(8,128)(2,1)S(1)} %slice_bitcast_fusion.refs_1_.refs_8_), channel_id=1, source_target_pairs={{0,4},{1,5},{2,6},{3,7},{4,0},{5,1},{6,2},{7,3},{8,12},{9,13},{10,... | collective-permute-start | bytes 24584 | tf_op jit(solution)/shard_map/ppermute | solution.py:615
  18.8 6.1 %collective-permute-start.3 = (bf16[32,128]{1,0:T(8,128)(2,1)S(1)}, bf16[32,128]{1,0:T(8,128)(2,1)S(1)}, u32[]{:S(2)}, u32[]{:S(2)}) collective-permute-start(bf16[32,128]{1,0:T(8,128)(2,1)S(1)} %slice_bitcast_fusion.refs_1_.refs_8_), channel_id=1, source_target_pairs={{0,2},{1,3},{2,0},{3,1},{4,6},{5,7},{6,4},{7,5},{8,10},{9,11},{10,... | collective-permute-start | bytes 24584 | tf_op jit(solution)/shard_map/ppermute | solution.py:615
  24.9 11.2 %collective-permute-start.7 = (bf16[49,32,128]{2,1,0:T(8,128)(2,1)S(1)}, bf16[49,32,128]{2,1,0:T(8,128)(2,1)S(1)}, u32[]{:S(2)}, u32[]{:S(2)}) collective-permute-start(bf16[49,32,128]{2,1,0:T(8,128)(2,1)S(1)} %collective-permute-done.6.refs_0_.refs_6_), channel_id=1, source_target_pairs={{0,2},{1,3},{2,0},{3,1},{4,6},{5,7},{6,4},{7,5},{8,10},{9,11},{10,... | collective-permute-start | bytes 1204232 | tf_op jit(solution)/shard_map/ppermute | solution.py:615
  36.2 11.2 %collective-permute-start.12 = (bf16[49,32,128]{2,1,0:T(8,128)(2,1)S(1)}, bf16[49,32,128]{2,1,0:T(8,128)(2,1)S(1)}, u32[]{:S(2)}, u32[]{:S(2)}) collective-permute-start(bf16[49,32,128]{2,1,0:T(8,128)(2,1)S(1)} %get-tuple-element.102.refs_7_), channel_id=1, source_target_pairs={{0,2},{1,3},{2,0},{3,1},{4,6},{5,7},{6,4},{7,5},{8,10},{9,11},{10,... | collective-permute-start | bytes 1204232 | tf_op jit(solution)/shard_map/ppermute | solution.py:615
  39.0 6.6 %collective-permute-start.11 = (f32[24,128]{1,0:T(8,128)S(1)}, f32[24,128]{1,0:T(8,128)S(1)}, u32[]{:S(2)}, u32[]{:S(2)}) collective-permute-start(f32[24,128]{1,0:T(8,128)S(1)} %get-tuple-element.98.refs_0_), channel_id=1, source_target_pairs={{0,6},{1,7},{2,4},{3,5},{4,2},{5,3},{6,0},{7,1},{8,14},{9,15},{10,... | collective-permute-start | bytes 36872 | tf_op jit(solution)/shard_map/ppermute | solution.py:615
  40.4 5.2 %collective-permute-start.10 = (f32[24,128]{1,0:T(8,128)S(1)}, f32[24,128]{1,0:T(8,128)S(1)}, u32[]{:S(2)}, u32[]{:S(2)}) collective-permute-start(f32[24,128]{1,0:T(8,128)S(1)} %get-tuple-element.98.refs_0_), channel_id=1, source_target_pairs={{0,4},{1,5},{2,6},{3,7},{4,0},{5,1},{6,2},{7,3},{8,12},{9,13},{10,... | collective-permute-start | bytes 36872 | tf_op jit(solution)/shard_map/ppermute | solution.py:615
  42.1 5.3 %collective-permute-start.9 = (f32[24,128]{1,0:T(8,128)S(1)}, f32[24,128]{1,0:T(8,128)S(1)}, u32[]{:S(2)}, u32[]{:S(2)}) collective-permute-start(f32[24,128]{1,0:T(8,128)S(1)} %get-tuple-element.98.refs_0_), channel_id=1, source_target_pairs={{0,2},{1,3},{2,0},{3,1},{4,6},{5,7},{6,4},{7,5},{8,10},{9,11},{10,... | collective-permute-start | bytes 36872 | tf_op jit(solution)/shard_map/ppermute | solution.py:615
  48.0 19.2 %collective-permute-start.18 = (bf16[49,32,128]{2,1,0:T(8,128)(2,1)S(1)}, bf16[49,32,128]{2,1,0:T(8,128)(2,1)S(1)}, u32[]{:S(2)}, u32[]{:S(2)}) collective-permute-start(bf16[49,32,128]{2,1,0:T(8,128)(2,1)S(1)} %get-tuple-element.124), channel_id=1, source_target_pairs={{0,4},{1,5},{2,6},{3,7},{4,0},{5,1},{6,2},{7,3},{8,12},{9,13},{10,... | collective-permute-start | bytes 1204232 | tf_op jit(solution)/shard_map/ppermute | solution.py:615
  49.2 18.1 %collective-permute-start.17 = (bf16[49,32,128]{2,1,0:T(8,128)(2,1)S(1)}, bf16[49,32,128]{2,1,0:T(8,128)(2,1)S(1)}, u32[]{:S(2)}, u32[]{:S(2)}) collective-permute-start(bf16[49,32,128]{2,1,0:T(8,128)(2,1)S(1)} %get-tuple-element.105.refs_1_), channel_id=1, source_target_pairs={{0,2},{1,3},{2,0},{3,1},{4,6},{5,7},{6,4},{7,5},{8,10},{9,11},{10,... | collective-permute-start | bytes 1204232 | tf_op jit(solution)/shard_map/ppermute | solution.py:615
  59.2 4.2 %collective-permute-start.14 = (bf16[192,128]{1,0:T(8,128)(2,1)S(1)}, bf16[192,128]{1,0:T(8,128)(2,1)S(1)}, u32[]{:S(2)}, u32[]{:S(2)}) collective-permute-start(bf16[192,128]{1,0:T(8,128)(2,1)S(1)} %get-tuple-element.121), channel_id=1, source_target_pairs={{0,8},{8,0},{16,24},{24,16},{1,9},{9,1},{17,25},{25,17},{2,10},{10... | collective-permute-start | bytes 147464 | tf_op jit(solution)/shard_map/ppermute | solution.py:618
  60.7 4.1 %collective-permute-start.15 = (bf16[192,128]{1,0:T(8,128)(2,1)S(1)}, bf16[192,128]{1,0:T(8,128)(2,1)S(1)}, u32[]{:S(2)}, u32[]{:S(2)}) collective-permute-start(bf16[192,128]{1,0:T(8,128)(2,1)S(1)} %get-tuple-element.122), channel_id=1, source_target_pairs={{0,16},{8,24},{16,0},{24,8},{1,17},{9,25},{17,1},{25,9},{2,18},{10... | collective-permute-start | bytes 147464 | tf_op jit(solution)/shard_map/ppermute | solution.py:618
  62.3 5.0 %collective-permute-start.16 = (bf16[192,128]{1,0:T(8,128)(2,1)S(1)}, bf16[192,128]{1,0:T(8,128)(2,1)S(1)}, u32[]{:S(2)}, u32[]{:S(2)}) collective-permute-start(bf16[192,128]{1,0:T(8,128)(2,1)S(1)} %get-tuple-element.123), channel_id=1, source_target_pairs={{0,24},{8,16},{16,8},{24,0},{1,25},{9,17},{17,9},{25,1},{2,26},{10... | collective-permute-start | bytes 147464 | tf_op jit(solution)/shard_map/ppermute | solution.py:618
  63.3 19.2 %collective-permute-start.22 = (bf16[49,32,128]{2,1,0:T(8,128)(2,1)S(1)}, bf16[49,32,128]{2,1,0:T(8,128)(2,1)S(1)}, u32[]{:S(2)}, u32[]{:S(2)}) collective-permute-start(bf16[49,32,128]{2,1,0:T(8,128)(2,1)S(1)} %get-tuple-element.146), channel_id=1, source_target_pairs={{0,1},{1,0},{2,3},{3,2},{4,5},{5,4},{6,7},{7,6},{8,9},{9,8},{10,11... | collective-permute-start | bytes 1204232 | tf_op jit(solution)/shard_map/ppermute | solution.py:612
  67.3 5.8 %collective-permute-start.19 = (bf16[256,128]{1,0:T(8,128)(2,1)S(1)}, bf16[256,128]{1,0:T(8,128)(2,1)S(1)}, u32[]{:S(2)}, u32[]{:S(2)}) collective-permute-start(bf16[256,128]{1,0:T(8,128)(2,1)S(1)} %get-tuple-element.133), channel_id=1, source_target_pairs={{0,2},{1,3},{2,0},{3,1},{4,6},{5,7},{6,4},{7,5},{8,10},{9,11},{10,... | collective-permute-start | bytes 196616 | tf_op jit(solution)/shard_map/ppermute | solution.py:615
  68.0 6.6 %collective-permute-start.20 = (bf16[256,128]{1,0:T(8,128)(2,1)S(1)}, bf16[256,128]{1,0:T(8,128)(2,1)S(1)}, u32[]{:S(2)}, u32[]{:S(2)}) collective-permute-start(bf16[256,128]{1,0:T(8,128)(2,1)S(1)} %get-tuple-element.134), channel_id=1, source_target_pairs={{0,4},{1,5},{2,6},{3,7},{4,0},{5,1},{6,2},{7,3},{8,12},{9,13},{10,... | collective-permute-start | bytes 196616 | tf_op jit(solution)/shard_map/ppermute | solution.py:615
  69.9 6.2 %collective-permute-start.21 = (bf16[256,128]{1,0:T(8,128)(2,1)S(1)}, bf16[256,128]{1,0:T(8,128)(2,1)S(1)}, u32[]{:S(2)}, u32[]{:S(2)}) collective-permute-start(bf16[256,128]{1,0:T(8,128)(2,1)S(1)} %get-tuple-element.135), channel_id=1, source_target_pairs={{0,6},{1,7},{2,4},{3,5},{4,2},{5,3},{6,0},{7,1},{8,14},{9,15},{10,... | collective-permute-start | bytes 196616 | tf_op jit(solution)/shard_map/ppermute | solution.py:615
  76.1 5.1 %collective-permute-start.25 = (bf16[192,128]{1,0:T(8,128)(2,1)S(1)}, bf16[192,128]{1,0:T(8,128)(2,1)S(1)}, u32[]{:S(2)}, u32[]{:S(2)}) collective-permute-start(bf16[192,128]{1,0:T(8,128)(2,1)S(1)} %get-tuple-element.147.refs_0_), channel_id=1, source_target_pairs={{0,24},{8,16},{16,8},{24,0},{1,25},{9,17},{17,9},{25,1},{2,26},{10... | collective-permute-start | bytes 147464 | tf_op jit(solution)/shard_map/ppermute | solution.py:618
  77.9 4.1 %collective-permute-start.24 = (bf16[192,128]{1,0:T(8,128)(2,1)S(1)}, bf16[192,128]{1,0:T(8,128)(2,1)S(1)}, u32[]{:S(2)}, u32[]{:S(2)}) collective-permute-start(bf16[192,128]{1,0:T(8,128)(2,1)S(1)} %get-tuple-element.147.refs_0_), channel_id=1, source_target_pairs={{0,16},{8,24},{16,0},{24,8},{1,17},{9,25},{17,1},{25,9},{2,18},{10... | collective-permute-start | bytes 147464 | tf_op jit(solution)/shard_map/ppermute | solution.py:618
  78.4 4.1 %collective-permute-start.23 = (bf16[192,128]{1,0:T(8,128)(2,1)S(1)}, bf16[192,128]{1,0:T(8,128)(2,1)S(1)}, u32[]{:S(2)}, u32[]{:S(2)}) collective-permute-start(bf16[192,128]{1,0:T(8,128)(2,1)S(1)} %get-tuple-element.147.refs_0_), channel_id=1, source_target_pairs={{0,8},{8,0},{16,24},{24,16},{1,9},{9,1},{17,25},{25,17},{2,10},{10... | collective-permute-start | bytes 147464 | tf_op jit(solution)/shard_map/ppermute | solution.py:618
  79.6 4.6 %collective-permute-start.26 = (bf16[192,128]{1,0:T(8,128)(2,1)S(1)}, bf16[192,128]{1,0:T(8,128)(2,1)S(1)}, u32[]{:S(2)}, u32[]{:S(2)}) collective-permute-start(bf16[192,128]{1,0:T(8,128)(2,1)S(1)} %get-tuple-element.147.refs_0_), channel_id=1, source_target_pairs={{0,1},{1,0},{2,3},{3,2},{4,5},{5,4},{6,7},{7,6},{8,9},{9,8},{10,11... | collective-permute-start | bytes 147464 | tf_op jit(solution)/shard_map/ppermute | solution.py:612
  (12 other events, 85.8 us)

commit v4 on v3

--- a/solution.py
+++ b/solution.py
@@ -156,7 +156,7 @@
     )
 
 
-def forward_kernel(chips, where, *refs):
+def forward_kernel(chips, *refs):
     far, refs = refs[:6], refs[6:]
     pack_own, pack_sib, radial_sib, feats_sib, *refs = refs
     table, scaled, mixed, gating, pack, radial, incoming, *refs = refs
@@ -165,13 +165,14 @@
     for c in copies:
         c.start()
     radial_own, w_radial, rot, feats_own, w_value, w_mix = near
-    core, chip = where[0], where[1]
+    rank = lax.axis_index("graph")
+    core, chip = rank % 2, rank // 2
     slots = pack_own.shape[1]
     cap = slots // (2 * chips)
     nodes = feats_sib.shape[1]
     bins = rot.shape[2]
 
-    edge = lax.broadcasted_iota(jnp.int32, (2 * slots, slots), 1)
+    edge = lax.broadcasted_iota(jnp.int32, (1, slots), 1)
     place = lax.broadcasted_iota(jnp.int32, (2 * slots, slots), 0)
     side = (edge // cap) % 2
     origin = side * slots + (2 * ((edge // (2 * cap)) ^ chip) + core) * cap + edge % cap
@@ -371,7 +372,7 @@
         stats[2 * H :] = dot(every, hits(pack[1:2], stats.shape[1], F32), 1, 1, exact=True)
 
 
-def back_kernel(chips, where, *refs):
+def back_kernel(chips, *refs):
     parts, cots, firsts = refs[:chips], refs[chips : 2 * chips], refs[2 * chips : 3 * chips]
     refs = refs[3 * chips :]
     feats_own, feats_sib, pulled_a, pulled_b, pulled0_a, pulled0_b = refs[:6]
@@ -460,16 +461,18 @@
         grads[0, 2 * wide : 3 * wide] += total
 
     by_sevens(weigh)
-    keep[...] = grads[where[0]]
-    send[...] = grads[1 - where[0]].astype(BF)
-
-
-def split_kernel(planes, where, keep, got, own, *outs):
+    core = lax.axis_index("graph") % 2
+    keep[...] = grads[core]
+    send[...] = grads[1 - core].astype(BF)
+
+
+def split_kernel(planes, keep, got, own, *outs):
     *sends, total = outs
     total[...] = (keep[...] + got[...].astype(F32)).reshape(total.shape)
-    own[...] = total[where[1]]
+    plane = lax.axis_index("dp")
+    own[...] = total[plane]
     for step in range(1, planes):
-        sends[step - 1][...] = total[where[1] ^ step].astype(BF)
+        sends[step - 1][...] = total[plane ^ step].astype(BF)
 
 
 def address_kernel(planes, own, *refs):
@@ -496,12 +499,13 @@
     )
 
 
-def join_kernel(planes, where, *refs):
+def join_kernel(planes, *refs):
     mine, theirs = refs[:planes], refs[planes : 2 * planes]
     g_value, g_query, g_out, g_radial, g_mix, total = refs[2 * planes :]
+    core, plane = lax.axis_index("graph") % 2, lax.axis_index("dp")
     for step in range(planes):
-        total[where[0] * planes + (where[1] ^ step)] = mine[step][...].astype(F32)
-        total[(1 - where[0]) * planes + (where[1] ^ step)] = theirs[step][...].astype(F32)
+        total[core * planes + (plane ^ step)] = mine[step][...].astype(F32)
+        total[(1 - core) * planes + (plane ^ step)] = theirs[step][...].astype(F32)
     wide = H * VH
     flat = total[...].reshape(total.shape[0] * total.shape[1], wide)
     pieces = [flat[i * wide : (i + 1) * wide] for i in range(flat.shape[0] // wide)]
@@ -548,17 +552,15 @@
     each_k(one)
 
 
-def call(name, us, kernel, args, outs, scratch=(), smem=0, far=0, limit=24):
+def call(name, us, kernel, args, outs, scratch=(), far=0, limit=24):
     whole = pl.BlockSpec(memory_space=pltpu.VMEM)
-    specs = [pl.BlockSpec(memory_space=pltpu.SMEM)] * smem
-    specs += [pl.BlockSpec(memory_space=pltpu.HBM)] * far
-    specs += [whole] * (len(args) - smem - far)
+    specs = [pl.BlockSpec(memory_space=pltpu.HBM)] * far + [whole] * (len(args) - far)
     buffers = [pltpu.VMEM(s, d) for s, d in scratch]
     if far:
-        buffers += [pltpu.VMEM(a.shape, a.dtype) for a in args[smem : smem + far]]
+        buffers += [pltpu.VMEM(a.shape, a.dtype) for a in args[:far]]
         buffers += [pltpu.SemaphoreType.DMA((far,))]
     args = list(args)
-    for i in range(smem, smem + far):
+    for i in range(far):
         args[i] = pltpu.with_memory_space_constraint(args[i], pltpu.HBM)
     return pl.pallas_call(
         kernel,
@@ -605,8 +607,6 @@
     plane = lax.axis_index("dp")
     core, chip = rank % 2, rank // 2
     spot = chips * nodes
-    where = jnp.stack([core, chip, plane]).astype(jnp.int32)
-    where_sum = jnp.stack([core, plane]).astype(jnp.int32)
 
     def other_core(a):
         return lax.ppermute(a, "graph", [(i, i ^ 1) for i in range(ranks)])
@@ -625,13 +625,13 @@
     pack_own = jnp.where(
         line < 4, ids.astype(F32), jnp.pad(bias.astype(F32), ((8, 0), (0, 0)))
     )
+    neighbour = along(cot, 1)
     have = {0: cot}
     step = some
     while step > 1:
         for p in list(have):
             have[p ^ step] = along(have[p], step)
         step //= 2
-    neighbour = along(cot, 1)
     pack_sib = other_core(pack_own)
     radial_sib = other_core(radial[0])
     feats_sib = other_core(feats)
@@ -644,7 +644,6 @@
         9,
         functools.partial(forward_kernel, chips),
         [
-            where,
             radial[0],
             w_radial,
             rot,
@@ -665,7 +664,6 @@
             ((slots, radial.shape[2]), BF),
         ],
         [((K, wide, slots), BF)],
-        smem=1,
         far=6,
         limit=32,
     )
@@ -703,7 +701,6 @@
         )
 
     pulled_a, pulled0_a, dalpha_a = pull(False, [], [])
-    raw, cots[-1] = lax.optimization_barrier((raw, cots[-1]))
     near = [along(raw[p], 1) for p in range(3, chips, 2)]
     pulled_b, pulled0_b, dalpha_b, stats = pull(
         True, [dalpha_a, weight, stats], [((3 * H, spot), F32)]
@@ -734,7 +731,6 @@
         9,
         functools.partial(back_kernel, chips),
         [
-            where_sum,
             *parts,
             *cots,
             *firsts,
@@ -763,7 +759,6 @@
             *([((2 * nodes, wide), BF)] * chips),
         ],
         [((R, wide, slots), BF), ((K, wide, slots), BF), ((2, total_rows // 2, wide), F32)],
-        smem=1,
         limit=32,
     )
     dv_got = other_core(dv_sib)
@@ -773,10 +768,9 @@
         "split",
         0.6,
         functools.partial(split_kernel, planes),
-        [where_sum, keep, got],
+        [keep, got],
         [((cut, wide), F32), *([((cut, wide), BF)] * (planes - 1))],
         [((planes, cut, wide), F32)],
-        smem=1,
     )
     got = [beside(sends[step - 1], step) for step in range(1, planes)]
     got, pending = lax.optimization_barrier((got, pending))
@@ -799,7 +793,7 @@
         "join",
         1.5,
         functools.partial(join_kernel, planes),
-        [where_sum, *mine, *theirs],
+        [*mine, *theirs],
         [
             ((wide, wide), F32),
             ((wide, wide), F32),
@@ -808,7 +802,6 @@
             (w_mix.shape, F32),
         ],
         [((2 * planes, cut, wide), F32)],
-        smem=1,
     )
 
     (grad_nodes,) = call(

time: 86.1 us -> 84.9 us (0.986)
  Pallas kernels: 29.7 us -> 27.6 us
  starting transfers between devices: 30.2 us -> 31.8 us
    pallas_call x12, Pallas kernels: 29.7 us -> 27.6 us  [call(): pl.pallas_call(kernel, out_shape=[jax.ShapeDtypeStruct(s, d) for s, d in...]
    ppermute x15, starting transfers between devices: 22.3 us -> 24.1 us  [along(): return lax.ppermute(a, 'graph', [(i, i ^ 2 * step) for i in range(ranks)])]
    ppermute x15, waiting for transfers between devices: 13.7 us -> 12.9 us  [along(): return lax.ppermute(a, 'graph', [(i, i ^ 2 * step) for i in range(ranks)])]
  transfers between devices with their start and end apart: 30 -> 30, of which waited for: 15 -> 16; matrix products, arithmetic and copies ran while one was open for 2% -> 2% of each run, Pallas kernels for 32% -> 31%
where the time goes in v4:
time: 84.9 us; the launch traced here: 84.5 us
  starting transfers between devices  31.8 us (37%)
  Pallas kernels  27.6 us (33%)
  waiting for transfers between devices  22.8 us (27%)
    pallas_call x12, Pallas kernels, call(): pl.pallas_call(kernel, out_shape=[jax.ShapeDtypeStruct(s, d) for s, d in...  27.6 us
    ppermute x15, starting transfers between devices, along(): return lax.ppermute(a, 'graph', [(i, i ^ 2 * step) for i in range(ranks)])  24.1 us
    ppermute x15, waiting for transfers between devices, along(): return lax.ppermute(a, 'graph', [(i, i ^ 2 * step) for i in range(ranks)])  12.9 us
    ppermute x6, waiting for transfers between devices, beside(): return lax.ppermute(a, 'dp', [(i, i ^ step) for i in range(planes)])  8.03 us
    ppermute x6, starting transfers between devices, beside(): return lax.ppermute(a, 'dp', [(i, i ^ step) for i in range(planes)])  7.11 us
    ppermute x9, waiting for transfers between devices, other_core(): return lax.ppermute(a, 'graph', [(i, i ^ 1) for i in range(ranks)])  1.92 us
  transfers between devices with their start and end apart: 30, of which 16 were waited for; matrix products, arithmetic and copies ran while one was open for 2% of the time, Pallas kernels for 31%

profile of v4, /device:TPU:0, one launch (start us, length us, event | category | flops | bytes accessed | tf_op | source)
XLA Modules:
  0.0 84.5 jit_solution(3859220077155657314)
XLA Ops:
  0.6 3.1 %collective-permute-start.8 = (bf16[49,32,128]{2,1,0:T(8,128)(2,1)}, bf16[49,32,128]{2,1,0:T(8,128)(2,1)S(1)}, u32[]{:S(2)}, u32[]{:S(2)}) collective-permute-start(bf16[49,32,128]{2,1,0:T(8,128)(2,1)} %bitcast.23), channel_id=1, source_target_pairs={{0,2},{1,3},{2,0},{3,1},{4,6},{5,7},{6,4},{7,5},{8,10},{9,11},{10,... | collective-permute-start | bytes 1204232 | tf_op jit(solution)/shard_map/ppermute | solution.py:615
  3.7 2.6 %collective-permute-start.6 = (bf16[49,32,128]{2,1,0:T(8,128)(2,1)}, bf16[49,32,128]{2,1,0:T(8,128)(2,1)S(1)}, u32[]{:S(2)}, u32[]{:S(2)}) collective-permute-start(bf16[49,32,128]{2,1,0:T(8,128)(2,1)} %bitcast.24), channel_id=1, source_target_pairs={{0,4},{1,5},{2,6},{3,7},{4,0},{5,1},{6,2},{7,3},{8,12},{9,13},{10,... | collective-permute-start | bytes 1204232 | tf_op jit(solution)/shard_map/ppermute | solution.py:615
  8.9 6.8 %forward.1 = (f32[29,56,256]{2,1,0:T(8,128)S(1)}, bf16[29,128,256]{2,1,0:T(8,128)(2,1)S(1)}, bf16[29,128,256]{2,1,0:T(8,128)(2,1)S(1)}, f32[128,256]{1,0:T(8,128...) custom-call(bf16[256,512]{1,0:T(8,128)(2,1)} %bitcast.40, bf16[512,128]{1,0:T(8,128)(2,1)} %refs_1_.1, ...), custom_call_target="tpu_custom_call" | custom-call | flops 10350000128 | bytes 1000 | tf_op jit(solution)/shard_map/forward/pallas_call | solution.py:565
  15.8 1.9 %collective-permute-start.4 = (bf16[32,128]{1,0:T(8,128)(2,1)S(1)}, bf16[32,128]{1,0:T(8,128)(2,1)S(1)}, u32[]{:S(2)}, u32[]{:S(2)}) collective-permute-start(bf16[32,128]{1,0:T(8,128)(2,1)S(1)} %slice_bitcast_fusion.refs_1_.refs_8_), channel_id=1, source_target_pairs={{0,4},{1,5},{2,6},{3,7},{4,0},{5,1},{6,2},{7,3},{8,12},{9,13},{10,... | collective-permute-start | bytes 24584 | tf_op jit(solution)/shard_map/ppermute | solution.py:615
  17.7 2.5 %collective-permute-start.3 = (bf16[32,128]{1,0:T(8,128)(2,1)S(1)}, bf16[32,128]{1,0:T(8,128)(2,1)S(1)}, u32[]{:S(2)}, u32[]{:S(2)}) collective-permute-start(bf16[32,128]{1,0:T(8,128)(2,1)S(1)} %slice_bitcast_fusion.refs_1_.refs_8_), channel_id=1, source_target_pairs={{0,2},{1,3},{2,0},{3,1},{4,6},{5,7},{6,4},{7,5},{8,10},{9,11},{10,... | collective-permute-start | bytes 24584 | tf_op jit(solution)/shard_map/ppermute | solution.py:615
  20.2 4.5 %collective-permute-done.6.refs_0_.refs_6_ = bf16[49,32,128]{2,1,0:T(8,128)(2,1)S(1)} collective-permute-done((bf16[49,32,128]{2,1,0:T(8,128)(2,1)}, bf16[49,32,128]{2,1,0:T(8,128)(2,1)S(1)}, u32[]{:S(2)}, u32[]{:S(2)}) %collective-permute-start.6) | collective-permute-done | bytes 401440 | tf_op jit(solution)/shard_map/ppermute | solution.py:615
  25.4 2.0 %pull.2 = (bf16[29,128,128]{2,1,0:T(8,128)(2,1)S(1)}, f32[128,128]{1,0:T(8,128)S(1)}, f32[8,128]{1,0:T(8,128)S(1)}) custom-call(bf16[49,32,128]{2,1,0:T(8,128)(2,1)S(1)} %bitcast.25, bf16[49,32,128]{2,1,0:T(8,128)(2,1)S(1)} %collective-permute-done.8.refs_1_.refs_5_, bf16[128,128]{1,0:T(8,128)(2,1)S(1)} %copy-done.1, ...), custom_call_target="tpu_custom_call" | custom-call | flops 1150000000 | bytes 1000 | tf_op jit(solution)/shard_map/pull/pallas_call | solution.py:565
  27.4 5.6 %attend.1 = (f32[8,256]{1,0:T(8,128)S(1)}, f32[16,128]{1,0:T(8,128)S(1)}, f32[128,256]{1,0:T(8,128)S(1)}, bf16[49,32,128]{2,1,0:T(8,128)(2,1)S(1)}, bf16[49,32,1...) custom-call(bf16[128,128]{1,0:T(8,128)(2,1)} %w_query.1, ...), custom_call_target="tpu_custom_call" | custom-call | flops 1150000000 | bytes 1000 | tf_op jit(solution)/shard_map/attend/pallas_call | solution.py:565
  33.0 1.6 %collective-permute-start.12 = (bf16[49,32,128]{2,1,0:T(8,128)(2,1)S(1)}, bf16[49,32,128]{2,1,0:T(8,128)(2,1)S(1)}, u32[]{:S(2)}, u32[]{:S(2)}) collective-permute-start(bf16[49,32,128]{2,1,0:T(8,128)(2,1)S(1)} %get-tuple-element.92.refs_7_), channel_id=1, source_target_pairs={{0,2},{1,3},{2,0},{3,1},{4,6},{5,7},{6,4},{7,5},{8,10},{9,11},{10,... | collective-permute-start | bytes 1204232 | tf_op jit(solution)/shard_map/ppermute | solution.py:615
  34.6 2.3 %collective-permute-done.7.refs_1_.refs_7_ = bf16[49,32,128]{2,1,0:T(8,128)(2,1)S(1)} collective-permute-done((bf16[49,32,128]{2,1,0:T(8,128)(2,1)S(1)}, bf16[49,32,128]{2,1,0:T(8,128)(2,1)S(1)}, u32[]{:S(2)}, u32[]{:S(2)}) %collective-permute-start.7) | collective-permute-done | bytes 401440 | tf_op jit(solution)/shard_map/ppermute | solution.py:615
  36.9 2.4 %pull.3 = (bf16[29,128,128]{2,1,0:T(8,128)(2,1)S(1)}, f32[128,128]{1,0:T(8,128)S(1)}, f32[8,128]{1,0:T(8,128)S(1)}, f32[24,128]{1,0:T(8,128)S(1)}) custom-call(bf16[49,32,128]{2,1,0:T(8,128)(2,1)S(1)} %collective-permute-done.6.refs_0_.refs_6_, bf16[49,32,128]{2,1,0:T(8,128)(2,1)S(1)} %collective-permute-done.7.refs_1_.refs_7_, ...), custom_call_target="tpu_custom_call" | custom-call | flops 4600000000 | bytes 1000 | tf_op jit(solution)/shard_map/pull/pallas_call | solution.py:565
  40.7 3.0 %collective-permute-start.9 = (f32[24,128]{1,0:T(8,128)S(1)}, f32[24,128]{1,0:T(8,128)S(1)}, u32[]{:S(2)}, u32[]{:S(2)}) collective-permute-start(f32[24,128]{1,0:T(8,128)S(1)} %get-tuple-element.88.refs_0_), channel_id=1, source_target_pairs={{0,2},{1,3},{2,0},{3,1},{4,6},{5,7},{6,4},{7,5},{8,10},{9,11},{10,... | collective-permute-start | bytes 36872 | tf_op jit(solution)/shard_map/ppermute | solution.py:615
  46.2 1.8 %collective-permute-start.18 = (bf16[49,32,128]{2,1,0:T(8,128)(2,1)S(1)}, bf16[49,32,128]{2,1,0:T(8,128)(2,1)S(1)}, u32[]{:S(2)}, u32[]{:S(2)}) collective-permute-start(bf16[49,32,128]{2,1,0:T(8,128)(2,1)S(1)} %get-tuple-element.114), channel_id=1, source_target_pairs={{0,4},{1,5},{2,6},{3,7},{4,0},{5,1},{6,2},{7,3},{8,12},{9,13},{10,... | collective-permute-start | bytes 1204232 | tf_op jit(solution)/shard_map/ppermute | solution.py:615
  49.2 6.1 %back.1 = (f32[768,128]{1,0:T(8,128)S(1)}, bf16[768,128]{1,0:T(8,128)(2,1)S(1)}, bf16[49,32,128]{2,1,0:T(8,128)(2,1)S(1)}, bf16[49,32,128]{2,1,0:T(8,128)(2,1)S(...) custom-call(bf16[49,32,128]{2,1,0:T(8,128)(2,1)S(1)} %get-tuple-elem, ...), custom_call_target="tpu_custom_call" | custom-call | flops 10350000128 | bytes 1000 | tf_op jit(solution)/shard_map/back/pallas_call | solution.py:565
  56.8 1.6 %collective-permute-start.14 = (bf16[192,128]{1,0:T(8,128)(2,1)S(1)}, bf16[192,128]{1,0:T(8,128)(2,1)S(1)}, u32[]{:S(2)}, u32[]{:S(2)}) collective-permute-start(bf16[192,128]{1,0:T(8,128)(2,1)S(1)} %get-tuple-element.111), channel_id=1, source_target_pairs={{0,8},{8,0},{16,24},{24,16},{1,9},{9,1},{17,25},{25,17},{2,10},{10... | collective-permute-start | bytes 147464 | tf_op jit(solution)/shard_map/ppermute | solution.py:618
  58.4 1.5 %collective-permute-start.15 = (bf16[192,128]{1,0:T(8,128)(2,1)S(1)}, bf16[192,128]{1,0:T(8,128)(2,1)S(1)}, u32[]{:S(2)}, u32[]{:S(2)}) collective-permute-start(bf16[192,128]{1,0:T(8,128)(2,1)S(1)} %get-tuple-element.112), channel_id=1, source_target_pairs={{0,16},{8,24},{16,0},{24,8},{1,17},{9,25},{17,1},{25,9},{2,18},{10... | collective-permute-start | bytes 147464 | tf_op jit(solution)/shard_map/ppermute | solution.py:618
  61.0 1.5 %collective-permute-done.15.refs_1_ = bf16[192,128]{1,0:T(8,128)(2,1)S(1)} collective-permute-done((bf16[192,128]{1,0:T(8,128)(2,1)S(1)}, bf16[192,128]{1,0:T(8,128)(2,1)S(1)}, u32[]{:S(2)}, u32[]{:S(2)}) %collective-permute-start.15) | collective-permute-done | bytes 49184 | tf_op jit(solution)/shard_map/ppermute | solution.py:618
  62.5 2.4 %collective-permute-done.16.refs_2_ = bf16[192,128]{1,0:T(8,128)(2,1)S(1)} collective-permute-done((bf16[192,128]{1,0:T(8,128)(2,1)S(1)}, bf16[192,128]{1,0:T(8,128)(2,1)S(1)}, u32[]{:S(2)}, u32[]{:S(2)}) %collective-permute-start.16) | collective-permute-done | bytes 49184 | tf_op jit(solution)/shard_map/ppermute | solution.py:618
  66.2 2.1 %collective-permute-start.20 = (bf16[256,128]{1,0:T(8,128)(2,1)S(1)}, bf16[256,128]{1,0:T(8,128)(2,1)S(1)}, u32[]{:S(2)}, u32[]{:S(2)}) collective-permute-start(bf16[256,128]{1,0:T(8,128)(2,1)S(1)} %get-tuple-element.124), channel_id=1, source_target_pairs={{0,4},{1,5},{2,6},{3,7},{4,0},{5,1},{6,2},{7,3},{8,12},{9,13},{10,... | collective-permute-start | bytes 196616 | tf_op jit(solution)/shard_map/ppermute | solution.py:615
  68.3 2.3 %collective-permute-start.21 = (bf16[256,128]{1,0:T(8,128)(2,1)S(1)}, bf16[256,128]{1,0:T(8,128)(2,1)S(1)}, u32[]{:S(2)}, u32[]{:S(2)}) collective-permute-start(bf16[256,128]{1,0:T(8,128)(2,1)S(1)} %get-tuple-element.125), channel_id=1, source_target_pairs={{0,6},{1,7},{2,4},{3,5},{4,2},{5,3},{6,0},{7,1},{8,14},{9,15},{10,... | collective-permute-start | bytes 196616 | tf_op jit(solution)/shard_map/ppermute | solution.py:615
  71.9 2.8 %collective-permute-done.20.refs_2_ = bf16[256,128]{1,0:T(8,128)(2,1)S(1)} collective-permute-done((bf16[256,128]{1,0:T(8,128)(2,1)S(1)}, bf16[256,128]{1,0:T(8,128)(2,1)S(1)}, u32[]{:S(2)}, u32[]{:S(2)}) %collective-permute-start.20) | collective-permute-done | bytes 65568 | tf_op jit(solution)/shard_map/ppermute | solution.py:615
  74.7 2.5 %collective-permute-start.25 = (bf16[192,128]{1,0:T(8,128)(2,1)S(1)}, bf16[192,128]{1,0:T(8,128)(2,1)S(1)}, u32[]{:S(2)}, u32[]{:S(2)}) collective-permute-start(bf16[192,128]{1,0:T(8,128)(2,1)S(1)} %get-tuple-element.137.refs_0_), channel_id=1, source_target_pairs={{0,24},{8,16},{16,8},{24,0},{1,25},{9,17},{17,9},{25,1},{2,26},{10... | collective-permute-start | bytes 147464 | tf_op jit(solution)/shard_map/ppermute | solution.py:618
  78.3 1.7 %collective-permute-done.25.refs_3_ = bf16[192,128]{1,0:T(8,128)(2,1)S(1)} collective-permute-done((bf16[192,128]{1,0:T(8,128)(2,1)S(1)}, bf16[192,128]{1,0:T(8,128)(2,1)S(1)}, u32[]{:S(2)}, u32[]{:S(2)}) %collective-permute-start.25) | collective-permute-done | bytes 49184 | tf_op jit(solution)/shard_map/ppermute | solution.py:618
  81.8 1.8 %nodes.1 = bf16[49,32,128]{2,1,0:T(8,128)(2,1)} custom-call(bf16[32,128]{1,0:T(8,128)(2,1)S(1)} %get-tuple-element.134.dquery, bf16[49,32,128]{2,1,0:T(8,128)(2,1)S(1)} %get-tuple-element.135.dv_own, bf16[49,32,128]{2,1,0:T(8,128)(2,1)S(1)} %collective-permute-done.22.dv_sib, bf16[49,32,128]{2,1,0:T(8,128)(2,1)S(1)} %bitcast.27, ...), custom_call_target="tpu_custom_call" | custom-call | flops 2990000128 | bytes 1000 | tf_op jit(solution)/shard_map/nodes/pallas_call | solution.py:565
  (64 shorter events, 17.6 us)
Async XLA Ops:
  0.6 24.8 %collective-permute-start.8 = (bf16[49,32,128]{2,1,0:T(8,128)(2,1)}, bf16[49,32,128]{2,1,0:T(8,128)(2,1)S(1)}, u32[]{:S(2)}, u32[]{:S(2)}) collective-permute-start(bf16[49,32,128]{2,1,0:T(8,128)(2,1)} %bitcast.23), channel_id=1, source_target_pairs={{0,2},{1,3},{2,0},{3,1},{4,6},{5,7},{6,4},{7,5},{8,10},{9,11},{10,... | collective-permute-start | bytes 1204232 | tf_op jit(solution)/shard_map/ppermute | solution.py:615
  3.7 20.9 %collective-permute-start.6 = (bf16[49,32,128]{2,1,0:T(8,128)(2,1)}, bf16[49,32,128]{2,1,0:T(8,128)(2,1)S(1)}, u32[]{:S(2)}, u32[]{:S(2)}) collective-permute-start(bf16[49,32,128]{2,1,0:T(8,128)(2,1)} %bitcast.24), channel_id=1, source_target_pairs={{0,4},{1,5},{2,6},{3,7},{4,0},{5,1},{6,2},{7,3},{8,12},{9,13},{10,... | collective-permute-start | bytes 1204232 | tf_op jit(solution)/shard_map/ppermute | solution.py:615
  15.7 8.9 %collective-permute-start.5 = (bf16[32,128]{1,0:T(8,128)(2,1)S(1)}, bf16[32,128]{1,0:T(8,128)(2,1)S(1)}, u32[]{:S(2)}, u32[]{:S(2)}) collective-permute-start(bf16[32,128]{1,0:T(8,128)(2,1)S(1)} %slice_bitcast_fusion.refs_1_.refs_8_), channel_id=1, source_target_pairs={{0,6},{1,7},{2,4},{3,5},{4,2},{5,3},{6,0},{7,1},{8,14},{9,15},{10,... | collective-permute-start | bytes 24584 | tf_op jit(solution)/shard_map/ppermute | solution.py:615
  15.8 9.1 %collective-permute-start.4 = (bf16[32,128]{1,0:T(8,128)(2,1)S(1)}, bf16[32,128]{1,0:T(8,128)(2,1)S(1)}, u32[]{:S(2)}, u32[]{:S(2)}) collective-permute-start(bf16[32,128]{1,0:T(8,128)(2,1)S(1)} %slice_bitcast_fusion.refs_1_.refs_8_), channel_id=1, source_target_pairs={{0,4},{1,5},{2,6},{3,7},{4,0},{5,1},{6,2},{7,3},{8,12},{9,13},{10,... | collective-permute-start | bytes 24584 | tf_op jit(solution)/shard_map/ppermute | solution.py:615
  17.7 7.2 %collective-permute-start.3 = (bf16[32,128]{1,0:T(8,128)(2,1)S(1)}, bf16[32,128]{1,0:T(8,128)(2,1)S(1)}, u32[]{:S(2)}, u32[]{:S(2)}) collective-permute-start(bf16[32,128]{1,0:T(8,128)(2,1)S(1)} %slice_bitcast_fusion.refs_1_.refs_8_), channel_id=1, source_target_pairs={{0,2},{1,3},{2,0},{3,1},{4,6},{5,7},{6,4},{7,5},{8,10},{9,11},{10,... | collective-permute-start | bytes 24584 | tf_op jit(solution)/shard_map/ppermute | solution.py:615
  24.9 12.0 %collective-permute-start.7 = (bf16[49,32,128]{2,1,0:T(8,128)(2,1)S(1)}, bf16[49,32,128]{2,1,0:T(8,128)(2,1)S(1)}, u32[]{:S(2)}, u32[]{:S(2)}) collective-permute-start(bf16[49,32,128]{2,1,0:T(8,128)(2,1)S(1)} %collective-permute-done.6.refs_0_.refs_6_), channel_id=1, source_target_pairs={{0,2},{1,3},{2,0},{3,1},{4,6},{5,7},{6,4},{7,5},{8,10},{9,11},{10,... | collective-permute-start | bytes 1204232 | tf_op jit(solution)/shard_map/ppermute | solution.py:615
  33.0 12.2 %collective-permute-start.12 = (bf16[49,32,128]{2,1,0:T(8,128)(2,1)S(1)}, bf16[49,32,128]{2,1,0:T(8,128)(2,1)S(1)}, u32[]{:S(2)}, u32[]{:S(2)}) collective-permute-start(bf16[49,32,128]{2,1,0:T(8,128)(2,1)S(1)} %get-tuple-element.92.refs_7_), channel_id=1, source_target_pairs={{0,2},{1,3},{2,0},{3,1},{4,6},{5,7},{6,4},{7,5},{8,10},{9,11},{10,... | collective-permute-start | bytes 1204232 | tf_op jit(solution)/shard_map/ppermute | solution.py:615
  39.3 6.1 %collective-permute-start.11 = (f32[24,128]{1,0:T(8,128)S(1)}, f32[24,128]{1,0:T(8,128)S(1)}, u32[]{:S(2)}, u32[]{:S(2)}) collective-permute-start(f32[24,128]{1,0:T(8,128)S(1)} %get-tuple-element.88.refs_0_), channel_id=1, source_target_pairs={{0,6},{1,7},{2,4},{3,5},{4,2},{5,3},{6,0},{7,1},{8,14},{9,15},{10,... | collective-permute-start | bytes 36872 | tf_op jit(solution)/shard_map/ppermute | solution.py:615
  40.7 4.7 %collective-permute-start.10 = (f32[24,128]{1,0:T(8,128)S(1)}, f32[24,128]{1,0:T(8,128)S(1)}, u32[]{:S(2)}, u32[]{:S(2)}) collective-permute-start(f32[24,128]{1,0:T(8,128)S(1)} %get-tuple-element.88.refs_0_), channel_id=1, source_target_pairs={{0,4},{1,5},{2,6},{3,7},{4,0},{5,1},{6,2},{7,3},{8,12},{9,13},{10,... | collective-permute-start | bytes 36872 | tf_op jit(solution)/shard_map/ppermute | solution.py:615
  40.7 4.9 %collective-permute-start.9 = (f32[24,128]{1,0:T(8,128)S(1)}, f32[24,128]{1,0:T(8,128)S(1)}, u32[]{:S(2)}, u32[]{:S(2)}) collective-permute-start(f32[24,128]{1,0:T(8,128)S(1)} %get-tuple-element.88.refs_0_), channel_id=1, source_target_pairs={{0,2},{1,3},{2,0},{3,1},{4,6},{5,7},{6,4},{7,5},{8,10},{9,11},{10,... | collective-permute-start | bytes 36872 | tf_op jit(solution)/shard_map/ppermute | solution.py:615
  46.2 19.9 %collective-permute-start.18 = (bf16[49,32,128]{2,1,0:T(8,128)(2,1)S(1)}, bf16[49,32,128]{2,1,0:T(8,128)(2,1)S(1)}, u32[]{:S(2)}, u32[]{:S(2)}) collective-permute-start(bf16[49,32,128]{2,1,0:T(8,128)(2,1)S(1)} %get-tuple-element.114), channel_id=1, source_target_pairs={{0,4},{1,5},{2,6},{3,7},{4,0},{5,1},{6,2},{7,3},{8,12},{9,13},{10,... | collective-permute-start | bytes 1204232 | tf_op jit(solution)/shard_map/ppermute | solution.py:615
  48.0 18.0 %collective-permute-start.17 = (bf16[49,32,128]{2,1,0:T(8,128)(2,1)S(1)}, bf16[49,32,128]{2,1,0:T(8,128)(2,1)S(1)}, u32[]{:S(2)}, u32[]{:S(2)}) collective-permute-start(bf16[49,32,128]{2,1,0:T(8,128)(2,1)S(1)} %get-tuple-element.95.refs_1_), channel_id=1, source_target_pairs={{0,2},{1,3},{2,0},{3,1},{4,6},{5,7},{6,4},{7,5},{8,10},{9,11},{10,... | collective-permute-start | bytes 1204232 | tf_op jit(solution)/shard_map/ppermute | solution.py:615
  56.8 4.2 %collective-permute-start.14 = (bf16[192,128]{1,0:T(8,128)(2,1)S(1)}, bf16[192,128]{1,0:T(8,128)(2,1)S(1)}, u32[]{:S(2)}, u32[]{:S(2)}) collective-permute-start(bf16[192,128]{1,0:T(8,128)(2,1)S(1)} %get-tuple-element.111), channel_id=1, source_target_pairs={{0,8},{8,0},{16,24},{24,16},{1,9},{9,1},{17,25},{25,17},{2,10},{10... | collective-permute-start | bytes 147464 | tf_op jit(solution)/shard_map/ppermute | solution.py:618
  58.4 4.1 %collective-permute-start.15 = (bf16[192,128]{1,0:T(8,128)(2,1)S(1)}, bf16[192,128]{1,0:T(8,128)(2,1)S(1)}, u32[]{:S(2)}, u32[]{:S(2)}) collective-permute-start(bf16[192,128]{1,0:T(8,128)(2,1)S(1)} %get-tuple-element.112), channel_id=1, source_target_pairs={{0,16},{8,24},{16,0},{24,8},{1,17},{9,25},{17,1},{25,9},{2,18},{10... | collective-permute-start | bytes 147464 | tf_op jit(solution)/shard_map/ppermute | solution.py:618
  59.9 5.0 %collective-permute-start.16 = (bf16[192,128]{1,0:T(8,128)(2,1)S(1)}, bf16[192,128]{1,0:T(8,128)(2,1)S(1)}, u32[]{:S(2)}, u32[]{:S(2)}) collective-permute-start(bf16[192,128]{1,0:T(8,128)(2,1)S(1)} %get-tuple-element.113), channel_id=1, source_target_pairs={{0,24},{8,16},{16,8},{24,0},{1,25},{9,17},{17,9},{25,1},{2,26},{10... | collective-permute-start | bytes 147464 | tf_op jit(solution)/shard_map/ppermute | solution.py:618
  61.0 20.8 %collective-permute-start.22 = (bf16[49,32,128]{2,1,0:T(8,128)(2,1)S(1)}, bf16[49,32,128]{2,1,0:T(8,128)(2,1)S(1)}, u32[]{:S(2)}, u32[]{:S(2)}) collective-permute-start(bf16[49,32,128]{2,1,0:T(8,128)(2,1)S(1)} %get-tuple-element.136), channel_id=1, source_target_pairs={{0,1},{1,0},{2,3},{3,2},{4,5},{5,4},{6,7},{7,6},{8,9},{9,8},{10,11... | collective-permute-start | bytes 1204232 | tf_op jit(solution)/shard_map/ppermute | solution.py:612
  66.1 5.8 %collective-permute-start.19 = (bf16[256,128]{1,0:T(8,128)(2,1)S(1)}, bf16[256,128]{1,0:T(8,128)(2,1)S(1)}, u32[]{:S(2)}, u32[]{:S(2)}) collective-permute-start(bf16[256,128]{1,0:T(8,128)(2,1)S(1)} %get-tuple-element.123), channel_id=1, source_target_pairs={{0,2},{1,3},{2,0},{3,1},{4,6},{5,7},{6,4},{7,5},{8,10},{9,11},{10,... | collective-permute-start | bytes 196616 | tf_op jit(solution)/shard_map/ppermute | solution.py:615
  66.2 8.4 %collective-permute-start.20 = (bf16[256,128]{1,0:T(8,128)(2,1)S(1)}, bf16[256,128]{1,0:T(8,128)(2,1)S(1)}, u32[]{:S(2)}, u32[]{:S(2)}) collective-permute-start(bf16[256,128]{1,0:T(8,128)(2,1)S(1)} %get-tuple-element.124), channel_id=1, source_target_pairs={{0,4},{1,5},{2,6},{3,7},{4,0},{5,1},{6,2},{7,3},{8,12},{9,13},{10,... | collective-permute-start | bytes 196616 | tf_op jit(solution)/shard_map/ppermute | solution.py:615
  68.3 6.4 %collective-permute-start.21 = (bf16[256,128]{1,0:T(8,128)(2,1)S(1)}, bf16[256,128]{1,0:T(8,128)(2,1)S(1)}, u32[]{:S(2)}, u32[]{:S(2)}) collective-permute-start(bf16[256,128]{1,0:T(8,128)(2,1)S(1)} %get-tuple-element.125), channel_id=1, source_target_pairs={{0,6},{1,7},{2,4},{3,5},{4,2},{5,3},{6,0},{7,1},{8,14},{9,15},{10,... | collective-permute-start | bytes 196616 | tf_op jit(solution)/shard_map/ppermute | solution.py:615
  74.7 5.2 %collective-permute-start.25 = (bf16[192,128]{1,0:T(8,128)(2,1)S(1)}, bf16[192,128]{1,0:T(8,128)(2,1)S(1)}, u32[]{:S(2)}, u32[]{:S(2)}) collective-permute-start(bf16[192,128]{1,0:T(8,128)(2,1)S(1)} %get-tuple-element.137.refs_0_), channel_id=1, source_target_pairs={{0,24},{8,16},{16,8},{24,0},{1,25},{9,17},{17,9},{25,1},{2,26},{10... | collective-permute-start | bytes 147464 | tf_op jit(solution)/shard_map/ppermute | solution.py:618
  77.2 4.1 %collective-permute-start.24 = (bf16[192,128]{1,0:T(8,128)(2,1)S(1)}, bf16[192,128]{1,0:T(8,128)(2,1)S(1)}, u32[]{:S(2)}, u32[]{:S(2)}) collective-permute-start(bf16[192,128]{1,0:T(8,128)(2,1)S(1)} %get-tuple-element.137.refs_0_), channel_id=1, source_target_pairs={{0,16},{8,24},{16,0},{24,8},{1,17},{9,25},{17,1},{25,9},{2,18},{10... | collective-permute-start | bytes 147464 | tf_op jit(solution)/shard_map/ppermute | solution.py:618
  77.7 4.1 %collective-permute-start.23 = (bf16[192,128]{1,0:T(8,128)(2,1)S(1)}, bf16[192,128]{1,0:T(8,128)(2,1)S(1)}, u32[]{:S(2)}, u32[]{:S(2)}) collective-permute-start(bf16[192,128]{1,0:T(8,128)(2,1)S(1)} %get-tuple-element.137.refs_0_), channel_id=1, source_target_pairs={{0,8},{8,0},{16,24},{24,16},{1,9},{9,1},{17,25},{25,17},{2,10},{10... | collective-permute-start | bytes 147464 | tf_op jit(solution)/shard_map/ppermute | solution.py:618
  78.3 5.3 %collective-permute-start.26 = (bf16[192,128]{1,0:T(8,128)(2,1)S(1)}, bf16[192,128]{1,0:T(8,128)(2,1)S(1)}, u32[]{:S(2)}, u32[]{:S(2)}) collective-permute-start(bf16[192,128]{1,0:T(8,128)(2,1)S(1)} %get-tuple-element.137.refs_0_), channel_id=1, source_target_pairs={{0,1},{1,0},{2,3},{3,2},{4,5},{5,4},{6,7},{7,6},{8,9},{9,8},{10,11... | collective-permute-start | bytes 147464 | tf_op jit(solution)/shard_map/ppermute | solution.py:612
  79.9 3.6 %collective-permute-start.29 = (bf16[192,128]{1,0:T(8,128)(2,1)S(1)}, bf16[192,128]{1,0:T(8,128)(2,1)S(1)}, u32[]{:S(2)}, u32[]{:S(2)}) collective-permute-start(bf16[192,128]{1,0:T(8,128)(2,1)S(1)} %collective-permute-done.25.refs_3_), channel_id=1, source_target_pairs={{0,1},{1,0},{2,3},{3,2},{4,5},{5,4},{6,7},{7,6},{8,9},{9,8},{10,11... | collective-permute-start | bytes 147464 | tf_op jit(solution)/shard_map/ppermute | solution.py:612
  (12 other events, 84.7 us)

commit v5 on v4

--- a/solution.py
+++ b/solution.py
@@ -772,8 +772,7 @@
         [((cut, wide), F32), *([((cut, wide), BF)] * (planes - 1))],
         [((planes, cut, wide), F32)],
     )
-    got = [beside(sends[step - 1], step) for step in range(1, planes)]
-    got, pending = lax.optimization_barrier((got, pending))
+    got = [beside(sends[step - 1], step) for step in reversed(range(1, planes))]
     letters = call(
         "address",
         0.6,

time: 84.9 us -> 82.5 us (0.972)
  waiting for transfers between devices: 22.8 us -> 20.5 us
    ppermute x15, waiting for transfers between devices: 12.9 us -> 11.5 us  [along(): return lax.ppermute(a, 'graph', [(i, i ^ 2 * step) for i in range(ranks)])]
    ppermute x6, waiting for transfers between devices: 8.03 us -> 7.1 us  [beside(): return lax.ppermute(a, 'dp', [(i, i ^ step) for i in range(planes)])]
  transfers between devices with their start and end apart: 30 -> 30, of which waited for: 16 -> 17; matrix products, arithmetic and copies ran while one was open for 2% -> 2% of each run, Pallas kernels for 31% -> 32%
where the time goes in v5:
time: 82.5 us; the launch traced here: 82.2 us
  starting transfers between devices  31.8 us (39%)
  Pallas kernels  27.6 us (33%)
  waiting for transfers between devices  20.5 us (25%)
  other arithmetic  0.83 us (1%)
    pallas_call x12, Pallas kernels, call(): pl.pallas_call(kernel, out_shape=[jax.ShapeDtypeStruct(s, d) for s, d in...  27.6 us
    ppermute x15, starting transfers between devices, along(): return lax.ppermute(a, 'graph', [(i, i ^ 2 * step) for i in range(ranks)])  24 us
    ppermute x15, waiting for transfers between devices, along(): return lax.ppermute(a, 'graph', [(i, i ^ 2 * step) for i in range(ranks)])  11.5 us
    ppermute x6, starting transfers between devices, beside(): return lax.ppermute(a, 'dp', [(i, i ^ step) for i in range(planes)])  7.11 us
    ppermute x6, waiting for transfers between devices, beside(): return lax.ppermute(a, 'dp', [(i, i ^ step) for i in range(planes)])  7.1 us
    ppermute x9, waiting for transfers between devices, other_core(): return lax.ppermute(a, 'graph', [(i, i ^ 1) for i in range(ranks)])  1.92 us
  transfers between devices with their start and end apart: 30, of which 17 were waited for; matrix products, arithmetic and copies ran while one was open for 2% of the time, Pallas kernels for 32%

profile of v5, /device:TPU:0, one launch (start us, length us, event | category | flops | bytes accessed | tf_op | source)
XLA Modules:
  0.0 82.2 jit_solution(14767026681342242300)
XLA Ops:
  0.6 3.1 %collective-permute-start.8 = (bf16[49,32,128]{2,1,0:T(8,128)(2,1)}, bf16[49,32,128]{2,1,0:T(8,128)(2,1)S(1)}, u32[]{:S(2)}, u32[]{:S(2)}) collective-permute-start(bf16[49,32,128]{2,1,0:T(8,128)(2,1)} %bitcast.23), channel_id=1, source_target_pairs={{0,2},{1,3},{2,0},{3,1},{4,6},{5,7},{6,4},{7,5},{8,10},{9,11},{10,... | collective-permute-start | bytes 1204232 | tf_op jit(solution)/shard_map/ppermute | solution.py:615
  3.7 2.6 %collective-permute-start.6 = (bf16[49,32,128]{2,1,0:T(8,128)(2,1)}, bf16[49,32,128]{2,1,0:T(8,128)(2,1)S(1)}, u32[]{:S(2)}, u32[]{:S(2)}) collective-permute-start(bf16[49,32,128]{2,1,0:T(8,128)(2,1)} %bitcast.24), channel_id=1, source_target_pairs={{0,4},{1,5},{2,6},{3,7},{4,0},{5,1},{6,2},{7,3},{8,12},{9,13},{10,... | collective-permute-start | bytes 1204232 | tf_op jit(solution)/shard_map/ppermute | solution.py:615
  8.9 6.8 %forward.1 = (f32[29,56,256]{2,1,0:T(8,128)S(1)}, bf16[29,128,256]{2,1,0:T(8,128)(2,1)S(1)}, bf16[29,128,256]{2,1,0:T(8,128)(2,1)S(1)}, f32[128,256]{1,0:T(8,128...) custom-call(bf16[256,512]{1,0:T(8,128)(2,1)} %bitcast.40, bf16[512,128]{1,0:T(8,128)(2,1)} %refs_1_.1, ...), custom_call_target="tpu_custom_call" | custom-call | flops 10350000128 | bytes 1000 | tf_op jit(solution)/shard_map/forward/pallas_call | solution.py:565
  15.8 1.9 %collective-permute-start.4 = (bf16[32,128]{1,0:T(8,128)(2,1)S(1)}, bf16[32,128]{1,0:T(8,128)(2,1)S(1)}, u32[]{:S(2)}, u32[]{:S(2)}) collective-permute-start(bf16[32,128]{1,0:T(8,128)(2,1)S(1)} %slice_bitcast_fusion.refs_1_.refs_8_), channel_id=1, source_target_pairs={{0,4},{1,5},{2,6},{3,7},{4,0},{5,1},{6,2},{7,3},{8,12},{9,13},{10,... | collective-permute-start | bytes 24584 | tf_op jit(solution)/shard_map/ppermute | solution.py:615
  17.7 2.5 %collective-permute-start.3 = (bf16[32,128]{1,0:T(8,128)(2,1)S(1)}, bf16[32,128]{1,0:T(8,128)(2,1)S(1)}, u32[]{:S(2)}, u32[]{:S(2)}) collective-permute-start(bf16[32,128]{1,0:T(8,128)(2,1)S(1)} %slice_bitcast_fusion.refs_1_.refs_8_), channel_id=1, source_target_pairs={{0,2},{1,3},{2,0},{3,1},{4,6},{5,7},{6,4},{7,5},{8,10},{9,11},{10,... | collective-permute-start | bytes 24584 | tf_op jit(solution)/shard_map/ppermute | solution.py:615
  20.2 4.5 %collective-permute-done.6.refs_0_.refs_6_ = bf16[49,32,128]{2,1,0:T(8,128)(2,1)S(1)} collective-permute-done((bf16[49,32,128]{2,1,0:T(8,128)(2,1)}, bf16[49,32,128]{2,1,0:T(8,128)(2,1)S(1)}, u32[]{:S(2)}, u32[]{:S(2)}) %collective-permute-start.6) | collective-permute-done | bytes 401440 | tf_op jit(solution)/shard_map/ppermute | solution.py:615
  25.4 2.0 %pull.2 = (bf16[29,128,128]{2,1,0:T(8,128)(2,1)S(1)}, f32[128,128]{1,0:T(8,128)S(1)}, f32[8,128]{1,0:T(8,128)S(1)}) custom-call(bf16[49,32,128]{2,1,0:T(8,128)(2,1)S(1)} %bitcast.25, bf16[49,32,128]{2,1,0:T(8,128)(2,1)S(1)} %collective-permute-done.8.refs_1_.refs_5_, bf16[128,128]{1,0:T(8,128)(2,1)S(1)} %copy-done.1, ...), custom_call_target="tpu_custom_call" | custom-call | flops 1150000000 | bytes 1000 | tf_op jit(solution)/shard_map/pull/pallas_call | solution.py:565
  27.4 5.6 %attend.1 = (f32[8,256]{1,0:T(8,128)S(1)}, f32[16,128]{1,0:T(8,128)S(1)}, f32[128,256]{1,0:T(8,128)S(1)}, bf16[49,32,128]{2,1,0:T(8,128)(2,1)S(1)}, bf16[49,32,1...) custom-call(bf16[128,128]{1,0:T(8,128)(2,1)} %w_query.1, ...), custom_call_target="tpu_custom_call" | custom-call | flops 1150000000 | bytes 1000 | tf_op jit(solution)/shard_map/attend/pallas_call | solution.py:565
  33.0 1.6 %collective-permute-start.12 = (bf16[49,32,128]{2,1,0:T(8,128)(2,1)S(1)}, bf16[49,32,128]{2,1,0:T(8,128)(2,1)S(1)}, u32[]{:S(2)}, u32[]{:S(2)}) collective-permute-start(bf16[49,32,128]{2,1,0:T(8,128)(2,1)S(1)} %get-tuple-element.86.refs_7_), channel_id=1, source_target_pairs={{0,2},{1,3},{2,0},{3,1},{4,6},{5,7},{6,4},{7,5},{8,10},{9,11},{10,... | collective-permute-start | bytes 1204232 | tf_op jit(solution)/shard_map/ppermute | solution.py:615
  34.6 2.3 %collective-permute-done.7.refs_1_.refs_7_ = bf16[49,32,128]{2,1,0:T(8,128)(2,1)S(1)} collective-permute-done((bf16[49,32,128]{2,1,0:T(8,128)(2,1)S(1)}, bf16[49,32,128]{2,1,0:T(8,128)(2,1)S(1)}, u32[]{:S(2)}, u32[]{:S(2)}) %collective-permute-start.7) | collective-permute-done | bytes 401440 | tf_op jit(solution)/shard_map/ppermute | solution.py:615
  36.9 2.4 %pull.3 = (bf16[29,128,128]{2,1,0:T(8,128)(2,1)S(1)}, f32[128,128]{1,0:T(8,128)S(1)}, f32[8,128]{1,0:T(8,128)S(1)}, f32[24,128]{1,0:T(8,128)S(1)}) custom-call(bf16[49,32,128]{2,1,0:T(8,128)(2,1)S(1)} %collective-permute-done.6.refs_0_.refs_6_, bf16[49,32,128]{2,1,0:T(8,128)(2,1)S(1)} %collective-permute-done.7.refs_1_.refs_7_, ...), custom_call_target="tpu_custom_call" | custom-call | flops 4600000000 | bytes 1000 | tf_op jit(solution)/shard_map/pull/pallas_call | solution.py:565
  40.7 3.0 %collective-permute-start.9 = (f32[24,128]{1,0:T(8,128)S(1)}, f32[24,128]{1,0:T(8,128)S(1)}, u32[]{:S(2)}, u32[]{:S(2)}) collective-permute-start(f32[24,128]{1,0:T(8,128)S(1)} %get-tuple-element.82.refs_0_), channel_id=1, source_target_pairs={{0,2},{1,3},{2,0},{3,1},{4,6},{5,7},{6,4},{7,5},{8,10},{9,11},{10,... | collective-permute-start | bytes 36872 | tf_op jit(solution)/shard_map/ppermute | solution.py:615
  43.8 1.4 %collective-permute-done.12.refs_8_ = bf16[49,32,128]{2,1,0:T(8,128)(2,1)S(1)} collective-permute-done((bf16[49,32,128]{2,1,0:T(8,128)(2,1)S(1)}, bf16[49,32,128]{2,1,0:T(8,128)(2,1)S(1)}, u32[]{:S(2)}, u32[]{:S(2)}) %collective-permute-start.12) | collective-permute-done | bytes 401440 | tf_op jit(solution)/shard_map/ppermute | solution.py:615
  46.2 1.8 %collective-permute-start.21 = (bf16[49,32,128]{2,1,0:T(8,128)(2,1)S(1)}, bf16[49,32,128]{2,1,0:T(8,128)(2,1)S(1)}, u32[]{:S(2)}, u32[]{:S(2)}) collective-permute-start(bf16[49,32,128]{2,1,0:T(8,128)(2,1)S(1)} %get-tuple-element.116), channel_id=1, source_target_pairs={{0,4},{1,5},{2,6},{3,7},{4,0},{5,1},{6,2},{7,3},{8,12},{9,13},{10,... | collective-permute-start | bytes 1204232 | tf_op jit(solution)/shard_map/ppermute | solution.py:615
  49.2 6.0 %back.1 = (f32[768,128]{1,0:T(8,128)S(1)}, bf16[768,128]{1,0:T(8,128)(2,1)S(1)}, bf16[49,32,128]{2,1,0:T(8,128)(2,1)S(1)}, bf16[49,32,128]{2,1,0:T(8,128)(2,1)S(...) custom-call(bf16[49,32,128]{2,1,0:T(8,128)(2,1)S(1)} %get-tuple-elem, ...), custom_call_target="tpu_custom_call" | custom-call | flops 10350000128 | bytes 1000 | tf_op jit(solution)/shard_map/back/pallas_call | solution.py:565
  55.3 1.4 %collective-permute-done.13.got = bf16[768,128]{1,0:T(8,128)(2,1)S(1)} collective-permute-done((bf16[768,128]{1,0:T(8,128)(2,1)S(1)}, bf16[768,128]{1,0:T(8,128)(2,1)S(1)}, u32[]{:S(2)}, u32[]{:S(2)}) %collective-permute-start.13) | collective-permute-done | bytes 196640 | tf_op jit(solution)/shard_map/ppermute | solution.py:612
  56.8 2.5 %collective-permute-start.14 = (bf16[192,128]{1,0:T(8,128)(2,1)S(1)}, bf16[192,128]{1,0:T(8,128)(2,1)S(1)}, u32[]{:S(2)}, u32[]{:S(2)}) collective-permute-start(bf16[192,128]{1,0:T(8,128)(2,1)S(1)} %get-tuple-element.105), channel_id=1, source_target_pairs={{0,24},{8,16},{16,8},{24,0},{1,25},{9,17},{17,9},{25,1},{2,26},{10... | collective-permute-start | bytes 147464 | tf_op jit(solution)/shard_map/ppermute | solution.py:618
  60.4 1.5 %collective-permute-done.14.refs_0_ = bf16[192,128]{1,0:T(8,128)(2,1)S(1)} collective-permute-done((bf16[192,128]{1,0:T(8,128)(2,1)S(1)}, bf16[192,128]{1,0:T(8,128)(2,1)S(1)}, u32[]{:S(2)}, u32[]{:S(2)}) %collective-permute-start.14) | collective-permute-done | bytes 49184 | tf_op jit(solution)/shard_map/ppermute | solution.py:618
  61.9 1.5 %collective-permute-done.15.refs_1_ = bf16[192,128]{1,0:T(8,128)(2,1)S(1)} collective-permute-done((bf16[192,128]{1,0:T(8,128)(2,1)S(1)}, bf16[192,128]{1,0:T(8,128)(2,1)S(1)}, u32[]{:S(2)}, u32[]{:S(2)}) %collective-permute-start.15) | collective-permute-done | bytes 49184 | tf_op jit(solution)/shard_map/ppermute | solution.py:618
  66.2 2.3 %collective-permute-start.19 = (bf16[256,128]{1,0:T(8,128)(2,1)S(1)}, bf16[256,128]{1,0:T(8,128)(2,1)S(1)}, u32[]{:S(2)}, u32[]{:S(2)}) collective-permute-start(bf16[256,128]{1,0:T(8,128)(2,1)S(1)} %get-tuple-element.115), channel_id=1, source_target_pairs={{0,6},{1,7},{2,4},{3,5},{4,2},{5,3},{6,0},{7,1},{8,14},{9,15},{10,... | collective-permute-start | bytes 196616 | tf_op jit(solution)/shard_map/ppermute | solution.py:615
  70.1 2.2 %collective-permute-done.19.refs_3_ = bf16[256,128]{1,0:T(8,128)(2,1)S(1)} collective-permute-done((bf16[256,128]{1,0:T(8,128)(2,1)S(1)}, bf16[256,128]{1,0:T(8,128)(2,1)S(1)}, u32[]{:S(2)}, u32[]{:S(2)}) %collective-permute-start.19) | collective-permute-done | bytes 65568 | tf_op jit(solution)/shard_map/ppermute | solution.py:615
  72.3 2.5 %collective-permute-start.25 = (bf16[192,128]{1,0:T(8,128)(2,1)S(1)}, bf16[192,128]{1,0:T(8,128)(2,1)S(1)}, u32[]{:S(2)}, u32[]{:S(2)}) collective-permute-start(bf16[192,128]{1,0:T(8,128)(2,1)S(1)} %get-tuple-element.125.refs_0_), channel_id=1, source_target_pairs={{0,24},{8,16},{16,8},{24,0},{1,25},{9,17},{17,9},{25,1},{2,26},{10... | collective-permute-start | bytes 147464 | tf_op jit(solution)/shard_map/ppermute | solution.py:618
  75.9 1.7 %collective-permute-done.25.refs_3_ = bf16[192,128]{1,0:T(8,128)(2,1)S(1)} collective-permute-done((bf16[192,128]{1,0:T(8,128)(2,1)S(1)}, bf16[192,128]{1,0:T(8,128)(2,1)S(1)}, u32[]{:S(2)}, u32[]{:S(2)}) %collective-permute-start.25) | collective-permute-done | bytes 49184 | tf_op jit(solution)/shard_map/ppermute | solution.py:618
  79.4 1.8 %nodes.1 = bf16[49,32,128]{2,1,0:T(8,128)(2,1)} custom-call(bf16[32,128]{1,0:T(8,128)(2,1)S(1)} %get-tuple-element.122.dquery, bf16[49,32,128]{2,1,0:T(8,128)(2,1)S(1)} %get-tuple-element.123.dv_own, bf16[49,32,128]{2,1,0:T(8,128)(2,1)S(1)} %collective-permute-done.22.dv_sib, bf16[49,32,128]{2,1,0:T(8,128)(2,1)S(1)} %bitcast.27, ...), custom_call_target="tpu_custom_call" | custom-call | flops 2990000128 | bytes 1000 | tf_op jit(solution)/shard_map/nodes/pallas_call | solution.py:565
  (64 shorter events, 16.4 us)
Async XLA Ops:
  0.6 24.8 %collective-permute-start.8 = (bf16[49,32,128]{2,1,0:T(8,128)(2,1)}, bf16[49,32,128]{2,1,0:T(8,128)(2,1)S(1)}, u32[]{:S(2)}, u32[]{:S(2)}) collective-permute-start(bf16[49,32,128]{2,1,0:T(8,128)(2,1)} %bitcast.23), channel_id=1, source_target_pairs={{0,2},{1,3},{2,0},{3,1},{4,6},{5,7},{6,4},{7,5},{8,10},{9,11},{10,... | collective-permute-start | bytes 1204232 | tf_op jit(solution)/shard_map/ppermute | solution.py:615
  3.7 20.9 %collective-permute-start.6 = (bf16[49,32,128]{2,1,0:T(8,128)(2,1)}, bf16[49,32,128]{2,1,0:T(8,128)(2,1)S(1)}, u32[]{:S(2)}, u32[]{:S(2)}) collective-permute-start(bf16[49,32,128]{2,1,0:T(8,128)(2,1)} %bitcast.24), channel_id=1, source_target_pairs={{0,4},{1,5},{2,6},{3,7},{4,0},{5,1},{6,2},{7,3},{8,12},{9,13},{10,... | collective-permute-start | bytes 1204232 | tf_op jit(solution)/shard_map/ppermute | solution.py:615
  15.7 8.9 %collective-permute-start.5 = (bf16[32,128]{1,0:T(8,128)(2,1)S(1)}, bf16[32,128]{1,0:T(8,128)(2,1)S(1)}, u32[]{:S(2)}, u32[]{:S(2)}) collective-permute-start(bf16[32,128]{1,0:T(8,128)(2,1)S(1)} %slice_bitcast_fusion.refs_1_.refs_8_), channel_id=1, source_target_pairs={{0,6},{1,7},{2,4},{3,5},{4,2},{5,3},{6,0},{7,1},{8,14},{9,15},{10,... | collective-permute-start | bytes 24584 | tf_op jit(solution)/shard_map/ppermute | solution.py:615
  15.8 9.1 %collective-permute-start.4 = (bf16[32,128]{1,0:T(8,128)(2,1)S(1)}, bf16[32,128]{1,0:T(8,128)(2,1)S(1)}, u32[]{:S(2)}, u32[]{:S(2)}) collective-permute-start(bf16[32,128]{1,0:T(8,128)(2,1)S(1)} %slice_bitcast_fusion.refs_1_.refs_8_), channel_id=1, source_target_pairs={{0,4},{1,5},{2,6},{3,7},{4,0},{5,1},{6,2},{7,3},{8,12},{9,13},{10,... | collective-permute-start | bytes 24584 | tf_op jit(solution)/shard_map/ppermute | solution.py:615
  17.7 7.2 %collective-permute-start.3 = (bf16[32,128]{1,0:T(8,128)(2,1)S(1)}, bf16[32,128]{1,0:T(8,128)(2,1)S(1)}, u32[]{:S(2)}, u32[]{:S(2)}) collective-permute-start(bf16[32,128]{1,0:T(8,128)(2,1)S(1)} %slice_bitcast_fusion.refs_1_.refs_8_), channel_id=1, source_target_pairs={{0,2},{1,3},{2,0},{3,1},{4,6},{5,7},{6,4},{7,5},{8,10},{9,11},{10,... | collective-permute-start | bytes 24584 | tf_op jit(solution)/shard_map/ppermute | solution.py:615
  24.9 12.0 %collective-permute-start.7 = (bf16[49,32,128]{2,1,0:T(8,128)(2,1)S(1)}, bf16[49,32,128]{2,1,0:T(8,128)(2,1)S(1)}, u32[]{:S(2)}, u32[]{:S(2)}) collective-permute-start(bf16[49,32,128]{2,1,0:T(8,128)(2,1)S(1)} %collective-permute-done.6.refs_0_.refs_6_), channel_id=1, source_target_pairs={{0,2},{1,3},{2,0},{3,1},{4,6},{5,7},{6,4},{7,5},{8,10},{9,11},{10,... | collective-permute-start | bytes 1204232 | tf_op jit(solution)/shard_map/ppermute | solution.py:615
  33.0 12.2 %collective-permute-start.12 = (bf16[49,32,128]{2,1,0:T(8,128)(2,1)S(1)}, bf16[49,32,128]{2,1,0:T(8,128)(2,1)S(1)}, u32[]{:S(2)}, u32[]{:S(2)}) collective-permute-start(bf16[49,32,128]{2,1,0:T(8,128)(2,1)S(1)} %get-tuple-element.86.refs_7_), channel_id=1, source_target_pairs={{0,2},{1,3},{2,0},{3,1},{4,6},{5,7},{6,4},{7,5},{8,10},{9,11},{10,... | collective-permute-start | bytes 1204232 | tf_op jit(solution)/shard_map/ppermute | solution.py:615
  39.4 6.1 %collective-permute-start.11 = (f32[24,128]{1,0:T(8,128)S(1)}, f32[24,128]{1,0:T(8,128)S(1)}, u32[]{:S(2)}, u32[]{:S(2)}) collective-permute-start(f32[24,128]{1,0:T(8,128)S(1)} %get-tuple-element.82.refs_0_), channel_id=1, source_target_pairs={{0,6},{1,7},{2,4},{3,5},{4,2},{5,3},{6,0},{7,1},{8,14},{9,15},{10,... | collective-permute-start | bytes 36872 | tf_op jit(solution)/shard_map/ppermute | solution.py:615
  40.7 4.7 %collective-permute-start.10 = (f32[24,128]{1,0:T(8,128)S(1)}, f32[24,128]{1,0:T(8,128)S(1)}, u32[]{:S(2)}, u32[]{:S(2)}) collective-permute-start(f32[24,128]{1,0:T(8,128)S(1)} %get-tuple-element.82.refs_0_), channel_id=1, source_target_pairs={{0,4},{1,5},{2,6},{3,7},{4,0},{5,1},{6,2},{7,3},{8,12},{9,13},{10,... | collective-permute-start | bytes 36872 | tf_op jit(solution)/shard_map/ppermute | solution.py:615
  40.7 4.9 %collective-permute-start.9 = (f32[24,128]{1,0:T(8,128)S(1)}, f32[24,128]{1,0:T(8,128)S(1)}, u32[]{:S(2)}, u32[]{:S(2)}) collective-permute-start(f32[24,128]{1,0:T(8,128)S(1)} %get-tuple-element.82.refs_0_), channel_id=1, source_target_pairs={{0,2},{1,3},{2,0},{3,1},{4,6},{5,7},{6,4},{7,5},{8,10},{9,11},{10,... | collective-permute-start | bytes 36872 | tf_op jit(solution)/shard_map/ppermute | solution.py:615
  46.2 19.9 %collective-permute-start.21 = (bf16[49,32,128]{2,1,0:T(8,128)(2,1)S(1)}, bf16[49,32,128]{2,1,0:T(8,128)(2,1)S(1)}, u32[]{:S(2)}, u32[]{:S(2)}) collective-permute-start(bf16[49,32,128]{2,1,0:T(8,128)(2,1)S(1)} %get-tuple-element.116), channel_id=1, source_target_pairs={{0,4},{1,5},{2,6},{3,7},{4,0},{5,1},{6,2},{7,3},{8,12},{9,13},{10,... | collective-permute-start | bytes 1204232 | tf_op jit(solution)/shard_map/ppermute | solution.py:615
  48.1 20.4 %collective-permute-start.20 = (bf16[49,32,128]{2,1,0:T(8,128)(2,1)S(1)}, bf16[49,32,128]{2,1,0:T(8,128)(2,1)S(1)}, u32[]{:S(2)}, u32[]{:S(2)}) collective-permute-start(bf16[49,32,128]{2,1,0:T(8,128)(2,1)S(1)} %get-tuple-element.89.refs_1_), channel_id=1, source_target_pairs={{0,2},{1,3},{2,0},{3,1},{4,6},{5,7},{6,4},{7,5},{8,10},{9,11},{10,... | collective-permute-start | bytes 1204232 | tf_op jit(solution)/shard_map/ppermute | solution.py:615
  56.8 5.1 %collective-permute-start.14 = (bf16[192,128]{1,0:T(8,128)(2,1)S(1)}, bf16[192,128]{1,0:T(8,128)(2,1)S(1)}, u32[]{:S(2)}, u32[]{:S(2)}) collective-permute-start(bf16[192,128]{1,0:T(8,128)(2,1)S(1)} %get-tuple-element.105), channel_id=1, source_target_pairs={{0,24},{8,16},{16,8},{24,0},{1,25},{9,17},{17,9},{25,1},{2,26},{10... | collective-permute-start | bytes 147464 | tf_op jit(solution)/shard_map/ppermute | solution.py:618
  59.4 4.1 %collective-permute-start.15 = (bf16[192,128]{1,0:T(8,128)(2,1)S(1)}, bf16[192,128]{1,0:T(8,128)(2,1)S(1)}, u32[]{:S(2)}, u32[]{:S(2)}) collective-permute-start(bf16[192,128]{1,0:T(8,128)(2,1)S(1)} %get-tuple-element.106), channel_id=1, source_target_pairs={{0,16},{8,24},{16,0},{24,8},{1,17},{9,25},{17,1},{25,9},{2,18},{10... | collective-permute-start | bytes 147464 | tf_op jit(solution)/shard_map/ppermute | solution.py:618
  59.9 4.1 %collective-permute-start.16 = (bf16[192,128]{1,0:T(8,128)(2,1)S(1)}, bf16[192,128]{1,0:T(8,128)(2,1)S(1)}, u32[]{:S(2)}, u32[]{:S(2)}) collective-permute-start(bf16[192,128]{1,0:T(8,128)(2,1)S(1)} %get-tuple-element.107), channel_id=1, source_target_pairs={{0,8},{8,0},{16,24},{24,16},{1,9},{9,1},{17,25},{25,17},{2,10},{10... | collective-permute-start | bytes 147464 | tf_op jit(solution)/shard_map/ppermute | solution.py:618
  61.9 17.5 %collective-permute-start.22 = (bf16[49,32,128]{2,1,0:T(8,128)(2,1)S(1)}, bf16[49,32,128]{2,1,0:T(8,128)(2,1)S(1)}, u32[]{:S(2)}, u32[]{:S(2)}) collective-permute-start(bf16[49,32,128]{2,1,0:T(8,128)(2,1)S(1)} %get-tuple-element.124), channel_id=1, source_target_pairs={{0,1},{1,0},{2,3},{3,2},{4,5},{5,4},{6,7},{7,6},{8,9},{9,8},{10,11... | collective-permute-start | bytes 1204232 | tf_op jit(solution)/shard_map/ppermute | solution.py:612
  64.0 5.8 %collective-permute-start.17 = (bf16[256,128]{1,0:T(8,128)(2,1)S(1)}, bf16[256,128]{1,0:T(8,128)(2,1)S(1)}, u32[]{:S(2)}, u32[]{:S(2)}) collective-permute-start(bf16[256,128]{1,0:T(8,128)(2,1)S(1)} %get-tuple-element.113), channel_id=1, source_target_pairs={{0,2},{1,3},{2,0},{3,1},{4,6},{5,7},{6,4},{7,5},{8,10},{9,11},{10,... | collective-permute-start | bytes 196616 | tf_op jit(solution)/shard_map/ppermute | solution.py:615
  64.9 5.2 %collective-permute-start.18 = (bf16[256,128]{1,0:T(8,128)(2,1)S(1)}, bf16[256,128]{1,0:T(8,128)(2,1)S(1)}, u32[]{:S(2)}, u32[]{:S(2)}) collective-permute-start(bf16[256,128]{1,0:T(8,128)(2,1)S(1)} %get-tuple-element.114), channel_id=1, source_target_pairs={{0,4},{1,5},{2,6},{3,7},{4,0},{5,1},{6,2},{7,3},{8,12},{9,13},{10,... | collective-permute-start | bytes 196616 | tf_op jit(solution)/shard_map/ppermute | solution.py:615
  66.2 6.1 %collective-permute-start.19 = (bf16[256,128]{1,0:T(8,128)(2,1)S(1)}, bf16[256,128]{1,0:T(8,128)(2,1)S(1)}, u32[]{:S(2)}, u32[]{:S(2)}) collective-permute-start(bf16[256,128]{1,0:T(8,128)(2,1)S(1)} %get-tuple-element.115), channel_id=1, source_target_pairs={{0,6},{1,7},{2,4},{3,5},{4,2},{5,3},{6,0},{7,1},{8,14},{9,15},{10,... | collective-permute-start | bytes 196616 | tf_op jit(solution)/shard_map/ppermute | solution.py:615
  72.3 5.3 %collective-permute-start.25 = (bf16[192,128]{1,0:T(8,128)(2,1)S(1)}, bf16[192,128]{1,0:T(8,128)(2,1)S(1)}, u32[]{:S(2)}, u32[]{:S(2)}) collective-permute-start(bf16[192,128]{1,0:T(8,128)(2,1)S(1)} %get-tuple-element.125.refs_0_), channel_id=1, source_target_pairs={{0,24},{8,16},{16,8},{24,0},{1,25},{9,17},{17,9},{25,1},{2,26},{10... | collective-permute-start | bytes 147464 | tf_op jit(solution)/shard_map/ppermute | solution.py:618
  74.8 4.1 %collective-permute-start.24 = (bf16[192,128]{1,0:T(8,128)(2,1)S(1)}, bf16[192,128]{1,0:T(8,128)(2,1)S(1)}, u32[]{:S(2)}, u32[]{:S(2)}) collective-permute-start(bf16[192,128]{1,0:T(8,128)(2,1)S(1)} %get-tuple-element.125.refs_0_), channel_id=1, source_target_pairs={{0,16},{8,24},{16,0},{24,8},{1,17},{9,25},{17,1},{25,9},{2,18},{10... | collective-permute-start | bytes 147464 | tf_op jit(solution)/shard_map/ppermute | solution.py:618
  75.3 4.1 %collective-permute-start.23 = (bf16[192,128]{1,0:T(8,128)(2,1)S(1)}, bf16[192,128]{1,0:T(8,128)(2,1)S(1)}, u32[]{:S(2)}, u32[]{:S(2)}) collective-permute-start(bf16[192,128]{1,0:T(8,128)(2,1)S(1)} %get-tuple-element.125.refs_0_), channel_id=1, source_target_pairs={{0,8},{8,0},{16,24},{24,16},{1,9},{9,1},{17,25},{25,17},{2,10},{10... | collective-permute-start | bytes 147464 | tf_op jit(solution)/shard_map/ppermute | solution.py:618
  75.9 5.3 %collective-permute-start.26 = (bf16[192,128]{1,0:T(8,128)(2,1)S(1)}, bf16[192,128]{1,0:T(8,128)(2,1)S(1)}, u32[]{:S(2)}, u32[]{:S(2)}) collective-permute-start(bf16[192,128]{1,0:T(8,128)(2,1)S(1)} %get-tuple-element.125.refs_0_), channel_id=1, source_target_pairs={{0,1},{1,0},{2,3},{3,2},{4,5},{5,4},{6,7},{7,6},{8,9},{9,8},{10,11... | collective-permute-start | bytes 147464 | tf_op jit(solution)/shard_map/ppermute | solution.py:612
  77.6 3.6 %collective-permute-start.29 = (bf16[192,128]{1,0:T(8,128)(2,1)S(1)}, bf16[192,128]{1,0:T(8,128)(2,1)S(1)}, u32[]{:S(2)}, u32[]{:S(2)}) collective-permute-start(bf16[192,128]{1,0:T(8,128)(2,1)S(1)} %collective-permute-done.25.refs_3_), channel_id=1, source_target_pairs={{0,1},{1,0},{2,3},{3,2},{4,5},{5,4},{6,7},{7,6},{8,9},{9,8},{10,11... | collective-permute-start | bytes 147464 | tf_op jit(solution)/shard_map/ppermute | solution.py:612
  (12 other events, 84.1 us)
